TPU v7x, 32 devices: a whole 2x2x4 slice. The times are simulated.
32 devices in a mesh: dp: 4 (over z), expert: 2 (over x), tensor: 4 (over y, core).
Axes of the slice: x: 2, y: 2, z: 4, core: 2. Of those that a mesh axis runs over, the one named last changes fastest.
Arguments:
- tokens: bfloat16 [8, 512, 1536], P('dp', 'expert'), may hold values from -6 to 6
- cotangent: bfloat16 [8, 512, 1536], P('dp', 'expert'), may hold values from -6 to 6
- seg_start: int32 [8, 9], P('dp'), may hold values from 0 to 511, as said below
- seg_parent: int32 [8, 9], P('dp'), may hold values from 0 to 4, as said below
- routes: int32 [8, 512, 4], P('dp', 'expert'), may hold values from 0 to 7, all different within a row; in each aligned block of 256 rows (0 to 255, 256 to 511, ..., all dimensions but the last counted through in order) at most 256 rows name the same one
- attn_gain: bfloat16 [1536], P('dp'), may hold values from 0.5 to 1.5
- w_query: bfloat16 [1536, 1536], P('dp', 'tensor'), may hold values from -0.15625 to 0.15625
- key_projection_weight: bfloat16 [1536, 256], P('dp'), may hold values from -0.15625 to 0.15625
- value_projection_weight: bfloat16 [1536, 256], P('dp'), may hold values from -0.15625 to 0.15625
- w_output: bfloat16 [1536, 1536], P('tensor', 'dp'), may hold values from -0.625 to 0.625
- moe_gain: bfloat16 [1536], P('dp'), may hold values from 0.5 to 1.5
- w_router: bfloat16 [1536, 8], P('dp'), may hold values from -0.078125 to 0.078125
- w_gate: bfloat16 [8, 1536, 768], P('expert', 'dp', 'tensor'), may hold values from -0.15625 to 0.15625
- w_up: bfloat16 [8, 1536, 768], P('expert', 'dp', 'tensor'), may hold values from -0.15625 to 0.15625
- w_down: bfloat16 [8, 768, 1536], P('expert', 'tensor', 'dp'), may hold values from -0.625 to 0.625
Outputs:
- mixed_out: bfloat16 [8, 512, 1536], P('dp', 'expert')
- d_tokens: float32 [8, 512, 1536], P('dp', 'expert')
- d_attn_gain: float32 [1536], P(('dp', 'expert'))
- d_query: float32 [1536, 1536], P(('dp', 'expert'), 'tensor')
- d_key: float32 [1536, 256], P(('dp', 'expert', 'tensor'))
- d_value: float32 [1536, 256], P(('dp', 'expert', 'tensor'))
- d_output: float32 [1536, 1536], P('tensor', ('dp', 'expert'))
- d_moe_gain: float32 [1536], P(('dp', 'expert'))
- d_router: float32 [1536, 8], P(('dp', 'expert'))
- d_gate: float32 [8, 1536, 768], P('expert', 'dp', 'tensor')
- d_up: float32 [8, 1536, 768], P('expert', 'dp', 'tensor')
- d_down: float32 [8, 768, 1536], P('expert', 'tensor', 'dp')
Inputs may be any that keep to these rules, and one draw needn't show every extreme that they name: `seg_start`: for each tree: entry 0 is 0, entry 1 is 512/2 (the trunk ends there); entries 2 to 8 are the starts of the other segments, rising strictly, each segment one token or more. `seg_parent`: entries 0 to 4 are 0 (trunk and branches hang from the trunk); entry 5 + i is the branch (1 to 4) of leaf i, each branch exactly once. `routes`: each token names 4 different experts; among the 256 tokens of one device of one tree (aligned blocks), no expert is named more than 256 times.
All inputs are finite; a program needn't handle non-finite values.
Results may differ from a plain program's by a relative error of at most 0.029.
Values may be sent and summed in bfloat16 or wider, within the bound.
A program may use at most 256 MiB of HBM per device.

v0:
```python
import jax
import jax.numpy as jnp
from jax import lax
from jax.sharding import PartitionSpec as P

QUERY_HEADS = 12
KEY_VALUE_HEADS = 2
HEAD_SIZE = 128


EPS = 1e-05
ROPE_BASE = 10000.0
NEG = -1e30


def normed(value_matrix, gain):
    factor = lax.rsqrt(jnp.mean(value_matrix * value_matrix, -1, keepdims=True) + EPS)
    return (value_matrix * factor * gain, factor)


def norm_back(value_matrix, factor, gain, upstream):
    scaled = upstream * gain
    gain_grad = jnp.sum(upstream * value_matrix * factor, 0)
    inner = jnp.mean(scaled * value_matrix, -1, keepdims=True)
    return (factor * scaled - value_matrix * factor * factor * factor * inner, gain_grad)


def layout(starts, parents, places, sequence_length):
    labels = jnp.arange(starts.shape[0], dtype=jnp.int32)
    segment = (
        jnp.sum((starts[None, :] <= places[:, None]).astype(jnp.int32), 1, dtype=jnp.int32) - 1
    )
    hot_own = segment[:, None] == labels[None, :]
    parent_one = jnp.sum(jnp.where(hot_own, parents[None, :], 0), 1, dtype=jnp.int32)
    hot_above = parent_one[:, None] == labels[None, :]
    parent_two = jnp.sum(jnp.where(hot_above, parents[None, :], 0), 1, dtype=jnp.int32)
    hot_further = parent_two[:, None] == labels[None, :]
    seg_ends = jnp.concatenate([starts[1:], jnp.full((1,), sequence_length, jnp.int32)])
    seg_lengths = seg_ends - starts
    own_start = jnp.sum(jnp.where(hot_own, starts[None, :], 0), 1, dtype=jnp.int32)
    above_len = jnp.sum(jnp.where(hot_above, seg_lengths[None, :], 0), 1, dtype=jnp.int32)
    further_len = jnp.sum(jnp.where(hot_further, seg_lengths[None, :], 0), 1, dtype=jnp.int32)
    depths = (
        places
        - own_start
        + jnp.where(segment != 0, above_len, 0)
        + jnp.where(parent_one != 0, further_len, 0)
    )
    return (segment, parent_one, parent_two, depths)


def angles(depths, feature):
    half_width = feature // 2
    frequency = ROPE_BASE ** (-2.0 * jnp.arange(half_width, dtype=jnp.float32) / feature)
    turning = depths.astype(jnp.float32)[:, None] * frequency[None, :]
    return (jnp.cos(turning), jnp.sin(turning))


def rotated_input(value_matrix, cosine_table, sine_lookup, sign):
    half_width = value_matrix.shape[-1] // 2
    front = value_matrix[..., :half_width]
    back_half = value_matrix[..., half_width:]
    cos_rows = cosine_table[:, None, :]
    sin_rows = sign * sine_lookup[:, None, :]
    return jnp.concatenate(
        [front * cos_rows - back_half * sin_rows, back_half * cos_rows + front * sin_rows], -1
    )


def visible_mask(key_segment, key_places, segment, parent_one, parent_two, places):
    linked = (
        (key_segment[None, :] == segment[:, None])
        | (key_segment[None, :] == parent_one[:, None])
        | (key_segment[None, :] == parent_two[:, None])
    )
    return linked & (key_places[None, :] <= places[:, None])


def gated(pre_gate, pre_up):
    return jax.nn.gelu(pre_gate) * pre_up


def send_rows(rows, expert_count, per_device, capacity):
    feature = rows.shape[-1]
    landed = lax.all_to_all(
        rows.reshape(expert_count, per_device * capacity, feature),
        "expert",
        split_axis=0,
        concat_axis=0,
        tiled=True,
    )
    return landed.reshape(expert_count, per_device, capacity, feature)


def return_rows(partial_value, expert_count, per_device, capacity):
    feature = partial_value.shape[-1]
    slot_count = expert_count * per_device * capacity
    back = lax.all_to_all(
        partial_value.reshape(expert_count, per_device * capacity, feature),
        "expert",
        split_axis=0,
        concat_axis=0,
        tiled=True,
    )
    return back.reshape(slot_count, feature).astype(jnp.float32)


def head_total(partial_value):
    return lax.psum(partial_value.astype(jnp.bfloat16), "tensor").astype(jnp.float32)


def reduce_grads(grad_set):
    (
        gain_one,
        query_grad,
        key_grad,
        value_grad,
        output_grad,
        gain_two,
        router_grad,
        gate_grad,
        up_grad,
        down_grad,
    ) = grad_set
    dense_set = (
        lax.psum_scatter(
            gain_one.astype(jnp.bfloat16), ("dp", "expert"), scatter_dimension=0, tiled=True
        ).astype(jnp.float32),
        lax.psum_scatter(
            query_grad.astype(jnp.bfloat16), ("dp", "expert"), scatter_dimension=0, tiled=True
        ).astype(jnp.float32),
        lax.psum_scatter(
            output_grad.astype(jnp.bfloat16), ("dp", "expert"), scatter_dimension=1, tiled=True
        ).astype(jnp.float32),
        lax.psum_scatter(
            gain_two.astype(jnp.bfloat16), ("dp", "expert"), scatter_dimension=0, tiled=True
        ).astype(jnp.float32),
        lax.psum_scatter(
            router_grad.astype(jnp.bfloat16), ("dp", "expert"), scatter_dimension=0, tiled=True
        ).astype(jnp.float32),
    )
    kv_set = (
        lax.psum_scatter(key_grad, ("dp", "expert", "tensor"), scatter_dimension=0, tiled=True),
        lax.psum_scatter(value_grad, ("dp", "expert", "tensor"), scatter_dimension=0, tiled=True),
    )
    expert_set = (
        lax.psum_scatter(
            gate_grad.astype(jnp.bfloat16), "dp", scatter_dimension=1, tiled=True
        ).astype(jnp.float32),
        lax.psum_scatter(
            up_grad.astype(jnp.bfloat16), "dp", scatter_dimension=1, tiled=True
        ).astype(jnp.float32),
        lax.psum_scatter(
            down_grad.astype(jnp.bfloat16), "dp", scatter_dimension=2, tiled=True
        ).astype(jnp.float32),
    )
    return (
        dense_set[0],
        dense_set[1],
        kv_set[0],
        kv_set[1],
        dense_set[2],
        dense_set[3],
        dense_set[4],
        expert_set[0],
        expert_set[1],
        expert_set[2],
    )


def micro_step(tokens_tree, upstream, starts, parents, routed, dense_set, expert_set):
    (
        attn_gain,
        w_query,
        key_projection_weight,
        value_projection_weight,
        w_output,
        moe_gain,
        w_router,
    ) = dense_set
    w_gate, w_up, w_down = expert_set
    attn_gain = attn_gain.astype(jnp.float32)
    moe_gain = moe_gain.astype(jnp.float32)
    token_count, feature = tokens_tree.shape
    local_heads = w_query.shape[1] // HEAD_SIZE
    group_width = QUERY_HEADS // KEY_VALUE_HEADS
    tensor_count = lax.axis_size("tensor")
    expert_count = lax.axis_size("expert")
    tensor_at = lax.axis_index("tensor")
    expert_at = lax.axis_index("expert")
    sequence_length = token_count * expert_count
    key_value_head = tensor_at * local_heads // group_width
    inv_root = HEAD_SIZE ** (-0.5)
    places = expert_at * token_count + jnp.arange(token_count, dtype=jnp.int32)
    segment, parent_one, parent_two, depths = layout(starts, parents, places, sequence_length)
    cosine_table, sine_lookup = angles(depths, HEAD_SIZE)
    key_places = jnp.arange(sequence_length, dtype=jnp.int32)
    key_segment = layout(starts, parents, key_places, sequence_length)[0]
    residual = tokens_tree.astype(jnp.float32)
    normal_one, factor_one = normed(residual, attn_gain)
    hidden_first = normal_one.astype(jnp.bfloat16)
    key_proj = lax.dynamic_slice_in_dim(
        key_projection_weight, key_value_head * HEAD_SIZE, HEAD_SIZE, 1
    )
    value_proj = lax.dynamic_slice_in_dim(
        value_projection_weight, key_value_head * HEAD_SIZE, HEAD_SIZE, 1
    )
    query_pre = jnp.dot(hidden_first, w_query, preferred_element_type=jnp.float32).reshape(
        token_count, local_heads, HEAD_SIZE
    )
    key_pre = jnp.dot(hidden_first, key_proj, preferred_element_type=jnp.float32)
    values_local = jnp.dot(hidden_first, value_proj, preferred_element_type=jnp.float32).astype(
        jnp.bfloat16
    )
    query_matrix = rotated_input(query_pre, cosine_table, sine_lookup, 1.0).astype(jnp.bfloat16)
    keys_local = rotated_input(key_pre[:, None, :], cosine_table, sine_lookup, 1.0)[:, 0, :].astype(
        jnp.bfloat16
    )
    key_matrix, value_matrix = (
        lax.all_gather(keys_local, "expert", axis=0, tiled=True),
        lax.all_gather(values_local, "expert", axis=0, tiled=True),
    )
    visible = visible_mask(key_segment, key_places, segment, parent_one, parent_two, places)
    scores = (
        jnp.einsum("qhd,kd->hqk", query_matrix, key_matrix, preferred_element_type=jnp.float32)
        * inv_root
    )
    scores = jnp.where(visible[None], scores, NEG)
    row_max = jnp.max(scores, -1, keepdims=True)
    exponent = jnp.exp(scores - row_max)
    row_mass = jnp.sum(exponent, -1, keepdims=True)
    attend_probs = (exponent / row_mass).astype(jnp.bfloat16)
    log_mass = row_max + jnp.log(row_mass)
    context = jnp.einsum(
        "hqk,kd->qhd", attend_probs, value_matrix, preferred_element_type=jnp.float32
    )
    context_low = context.reshape(token_count, local_heads * HEAD_SIZE).astype(jnp.bfloat16)
    attn_out = head_total(jnp.dot(context_low, w_output, preferred_element_type=jnp.float32))
    after_attn = residual + attn_out
    normal_two, factor_two = normed(after_attn, moe_gain)
    hidden_two = normal_two.astype(jnp.bfloat16)
    logits = jnp.dot(hidden_two, w_router, preferred_element_type=jnp.float32)
    expert_total = w_router.shape[1]
    top_count = routed.shape[1]
    labels = jnp.arange(expert_total, dtype=jnp.int32)
    chosen = routed[:, :, None] == labels[None, None, :]
    picked = jnp.sum(jnp.where(chosen, logits[:, None, :], 0.0), -1)
    gate_mix = jax.nn.softmax(picked, -1)
    per_device = w_gate.shape[0]
    capacity = 2 * token_count * top_count // expert_total
    pair_ids = routed.reshape(-1)
    pair_hot = (pair_ids[:, None] == labels[None, :]).astype(jnp.int32)
    pair_rank = jnp.sum((jnp.cumsum(pair_hot, 0) - 1) * pair_hot, 1)
    target = pair_ids * capacity + pair_rank
    slot_count = expert_total * capacity
    slot_pair = (
        jnp.zeros((slot_count,), jnp.int32)
        .at[target]
        .set(jnp.arange(pair_ids.shape[0], dtype=jnp.int32))
    )
    filled = jnp.zeros((slot_count,), jnp.bool_).at[target].set(True)
    outgoing = jnp.where(
        filled[:, None], hidden_two[slot_pair // top_count], jnp.zeros((), jnp.bfloat16)
    )
    arrived = send_rows(outgoing, expert_count, per_device, capacity)
    pre_gate = jnp.einsum("secd,edf->secf", arrived, w_gate, preferred_element_type=jnp.float32)
    pre_up = jnp.einsum("secd,edf->secf", arrived, w_up, preferred_element_type=jnp.float32)
    activated, gated_back = jax.vjp(gated, pre_gate, pre_up)
    hidden_expert = activated.astype(jnp.bfloat16)
    produced = jnp.einsum(
        "secf,efd->secd", hidden_expert, w_down, preferred_element_type=jnp.float32
    ).astype(jnp.bfloat16)
    returned = return_rows(produced, expert_count, per_device, capacity)
    outputs = returned[target].reshape(token_count, top_count, feature)
    mixed_part = jnp.sum(gate_mix[:, :, None] * outputs, 1)
    moe_out = head_total(mixed_part)
    mixed_out = (after_attn + moe_out).astype(jnp.bfloat16)
    upstream = upstream.astype(jnp.float32)
    gate_grad_part = jnp.sum(upstream[:, None, :] * outputs, -1)
    send_back = (
        (gate_mix[:, :, None] * upstream[:, None, :])
        .astype(jnp.bfloat16)
        .reshape(token_count * top_count, feature)
    )
    outgoing_grad = jnp.where(filled[:, None], send_back[slot_pair], jnp.zeros((), jnp.bfloat16))
    arrived_grad = send_rows(outgoing_grad, expert_count, per_device, capacity)
    hidden_grad = jnp.einsum(
        "secd,efd->secf", arrived_grad, w_down, preferred_element_type=jnp.float32
    )
    gate_pre_grad, up_pre_grad = gated_back(hidden_grad)
    gate_pre_low = gate_pre_grad.astype(jnp.bfloat16)
    up_pre_low = up_pre_grad.astype(jnp.bfloat16)
    down_grad = jnp.einsum(
        "secf,secd->efd", hidden_expert, arrived_grad, preferred_element_type=jnp.float32
    )
    gate_grad = jnp.einsum(
        "secd,secf->edf", arrived, gate_pre_low, preferred_element_type=jnp.float32
    )
    up_grad = jnp.einsum("secd,secf->edf", arrived, up_pre_low, preferred_element_type=jnp.float32)
    rows_grad = jnp.einsum(
        "secf,edf->secd", gate_pre_low, w_gate, preferred_element_type=jnp.float32
    )
    rows_grad = (
        rows_grad
        + jnp.einsum("secf,edf->secd", up_pre_low, w_up, preferred_element_type=jnp.float32)
    ).astype(jnp.bfloat16)
    back_rows = return_rows(rows_grad, expert_count, per_device, capacity)
    token_grad = jnp.sum(back_rows[target].reshape(token_count, top_count, feature), 1)
    two_grad, gate_grad_all = (
        lax.psum(token_grad.astype(jnp.bfloat16), "tensor").astype(jnp.float32),
        lax.psum(gate_grad_part.astype(jnp.bfloat16), "tensor").astype(jnp.float32),
    )
    mean_term = jnp.sum(gate_mix * gate_grad_all, -1, keepdims=True)
    picked_grad = gate_mix * (gate_grad_all - mean_term)
    logit_grad = jnp.sum(jnp.where(chosen, picked_grad[:, :, None], 0.0), 1).astype(jnp.bfloat16)
    two_grad = two_grad + jnp.dot(logit_grad, w_router.T, preferred_element_type=jnp.float32)
    router_grad = jnp.dot(hidden_two.T, logit_grad, preferred_element_type=jnp.float32)
    norm_two_grad, gain_two_grad = norm_back(after_attn, factor_two, moe_gain, two_grad)
    attn_grad = upstream + norm_two_grad
    attn_low = attn_grad.astype(jnp.bfloat16)
    output_grad = jnp.dot(context_low.T, attn_low, preferred_element_type=jnp.float32)
    context_grad = (
        jnp.dot(attn_low, w_output.T, preferred_element_type=jnp.float32)
        .astype(jnp.bfloat16)
        .reshape(token_count, local_heads, HEAD_SIZE)
    )
    row_delta = jnp.sum(context_grad.astype(jnp.float32) * context, -1).T
    block_rows = min(1024, sequence_length)

    def key_block(query_acc, number):
        first_row = number * block_rows
        key_rows = lax.dynamic_slice_in_dim(key_matrix, first_row, block_rows, 0)
        value_rows = lax.dynamic_slice_in_dim(value_matrix, first_row, block_rows, 0)
        segment_rows = lax.dynamic_slice_in_dim(key_segment, first_row, block_rows, 0)
        place_rows = lax.dynamic_slice_in_dim(key_places, first_row, block_rows, 0)
        seen = visible_mask(segment_rows, place_rows, segment, parent_one, parent_two, places)
        again = (
            jnp.einsum("qhd,kd->hqk", query_matrix, key_rows, preferred_element_type=jnp.float32)
            * inv_root
        )
        again = jnp.where(seen[None], again, NEG)
        prob_full = jnp.exp(again - log_mass)
        value_part = jnp.einsum(
            "hqk,qhd->kd",
            prob_full.astype(jnp.bfloat16),
            context_grad,
            preferred_element_type=jnp.float32,
        )
        prob_grad = jnp.einsum(
            "qhd,kd->hqk", context_grad, value_rows, preferred_element_type=jnp.float32
        )
        score_grad = (prob_full * (prob_grad - row_delta[:, :, None])).astype(jnp.bfloat16)
        query_acc = query_acc + jnp.einsum(
            "hqk,kd->qhd", score_grad, key_rows, preferred_element_type=jnp.float32
        )
        key_part = (
            jnp.einsum("hqk,qhd->kd", score_grad, query_matrix, preferred_element_type=jnp.float32)
            * inv_root
        )
        return (query_acc, (key_part, value_part))

    query_zero = jnp.zeros((token_count, local_heads, HEAD_SIZE), jnp.float32)
    query_grad, (key_parts, value_parts) = lax.scan(
        key_block, query_zero, jnp.arange(sequence_length // block_rows, dtype=jnp.int32)
    )
    query_grad = query_grad * inv_root
    key_everything = key_parts.reshape(sequence_length, HEAD_SIZE)
    value_everything = value_parts.reshape(sequence_length, HEAD_SIZE)
    head_selection = (jnp.arange(KEY_VALUE_HEADS, dtype=jnp.int32) == key_value_head).astype(
        jnp.float32
    )
    key_term = jnp.concatenate(
        [
            (key_everything[:, None, :] * head_selection[None, :, None]).reshape(
                sequence_length, KEY_VALUE_HEADS * HEAD_SIZE
            ),
            (value_everything[:, None, :] * head_selection[None, :, None]).reshape(
                sequence_length, KEY_VALUE_HEADS * HEAD_SIZE
            ),
        ],
        1,
    )
    partial_row_set = token_count // tensor_count
    key_value_portion = lax.psum_scatter(
        key_term.astype(jnp.bfloat16), ("expert", "tensor"), scatter_dimension=0, tiled=True
    ).astype(jnp.float32)
    sub_begin = tensor_at * partial_row_set
    partial_cosine = lax.dynamic_slice_in_dim(cosine_table, sub_begin, partial_row_set, 0)
    partial_sine = lax.dynamic_slice_in_dim(sine_lookup, sub_begin, partial_row_set, 0)
    key_share = (
        rotated_input(
            key_value_portion[:, : KEY_VALUE_HEADS * HEAD_SIZE].reshape(
                partial_row_set, KEY_VALUE_HEADS, HEAD_SIZE
            ),
            partial_cosine,
            partial_sine,
            -1.0,
        )
        .reshape(partial_row_set, KEY_VALUE_HEADS * HEAD_SIZE)
        .astype(jnp.bfloat16)
    )
    value_portion = key_value_portion[:, KEY_VALUE_HEADS * HEAD_SIZE :].astype(jnp.bfloat16)
    hidden_sub = lax.dynamic_slice_in_dim(hidden_first, sub_begin, partial_row_set, 0)
    key_weight_grad = jnp.dot(hidden_sub.T, key_share, preferred_element_type=jnp.float32)
    value_weight_grad = jnp.dot(hidden_sub.T, value_portion, preferred_element_type=jnp.float32)
    kv_input = jnp.dot(
        key_share, key_projection_weight.T, preferred_element_type=jnp.float32
    ) + jnp.dot(value_portion, value_projection_weight.T, preferred_element_type=jnp.float32)
    query_low = (
        rotated_input(query_grad, cosine_table, sine_lookup, -1.0)
        .reshape(token_count, local_heads * HEAD_SIZE)
        .astype(jnp.bfloat16)
    )
    query_weight_grad = jnp.dot(hidden_first.T, query_low, preferred_element_type=jnp.float32)
    input_part = jnp.dot(query_low, w_query.T, preferred_element_type=jnp.float32)
    current = lax.dynamic_slice_in_dim(input_part, sub_begin, partial_row_set, 0)
    input_part = lax.dynamic_update_slice_in_dim(input_part, current + kv_input, sub_begin, 0)
    one_grad = head_total(input_part)
    norm_one_grad, gain_one_grad = norm_back(residual, factor_one, attn_gain, one_grad)
    tokens_grad = attn_grad + norm_one_grad
    grad_set = (
        gain_one_grad,
        query_weight_grad,
        key_weight_grad,
        value_weight_grad,
        output_grad,
        gain_two_grad,
        router_grad,
        gate_grad,
        up_grad,
        down_grad,
    )
    return (mixed_out, tokens_grad, grad_set)


def shards(
    tokens,
    cotangent,
    seg_start,
    seg_parent,
    routes,
    attn_gain,
    w_query,
    key_projection_weight,
    value_projection_weight,
    w_output,
    moe_gain,
    w_router,
    w_gate,
    w_up,
    w_down,
):
    micro_count = tokens.shape[0]
    mixed_list = []
    grad_list = []
    totals = None
    summed = None
    for number in range(micro_count):
        dense_set = (
            lax.all_gather(attn_gain, "dp", axis=0, tiled=True),
            lax.all_gather(w_query, "dp", axis=0, tiled=True),
            lax.all_gather(key_projection_weight, "dp", axis=0, tiled=True),
            lax.all_gather(value_projection_weight, "dp", axis=0, tiled=True),
            lax.all_gather(w_output, "dp", axis=1, tiled=True),
            lax.all_gather(moe_gain, "dp", axis=0, tiled=True),
            lax.all_gather(w_router, "dp", axis=0, tiled=True),
        )
        expert_set = (
            lax.all_gather(w_gate, "dp", axis=1, tiled=True),
            lax.all_gather(w_up, "dp", axis=1, tiled=True),
            lax.all_gather(w_down, "dp", axis=2, tiled=True),
        )
        mixed_out, tokens_grad, grad_set = micro_step(
            tokens[number],
            cotangent[number],
            seg_start[number],
            seg_parent[number],
            routes[number],
            dense_set,
            expert_set,
        )
        mixed_list.append(mixed_out)
        grad_list.append(tokens_grad)
        summed = grad_set if summed is None else jax.tree.map(jnp.add, summed, grad_set)
    totals = reduce_grads(summed)
    return (
        jnp.stack(mixed_list),
        jnp.stack(grad_list),
        totals[0],
        totals[1],
        totals[2],
        totals[3],
        totals[4],
        totals[5],
        totals[6],
        totals[7],
        totals[8],
        totals[9],
    )


def solution(mesh):
    placed = (
        P("dp", "expert", None),
        P("dp", "expert", None),
        P("dp", None),
        P("dp", None),
        P("dp", "expert", None),
        P("dp"),
        P("dp", "tensor"),
        P("dp", None),
        P("dp", None),
        P("tensor", "dp"),
        P("dp"),
        P("dp", None),
        P("expert", "dp", "tensor"),
        P("expert", "dp", "tensor"),
        P("expert", "tensor", "dp"),
    )
    return jax.shard_map(
        shards,
        mesh=mesh,
        in_specs=placed,
        out_specs=(
            P("dp", "expert", None),
            P("dp", "expert", None),
            P(("dp", "expert")),
            P(("dp", "expert"), "tensor"),
            P(("dp", "expert", "tensor"), None),
            P(("dp", "expert", "tensor"), None),
            P("tensor", ("dp", "expert")),
            P(("dp", "expert")),
            P(("dp", "expert"), None),
            P("expert", "dp", "tensor"),
            P("expert", "dp", "tensor"),
            P("expert", "tensor", "dp"),
        ),
        check_vma=False,
    )
```

profile of v0, /device:TPU:0, one launch (start us, length us, event | category | flops | bytes accessed | tf_op | source)
XLA Modules:
  0.0 1581.4 jit_solution(14144099011058711769)
XLA Ops:
  11.0 13.6 all-gather.2
  24.8 29.2 %all_gather.55 = bf16[1536,256]{1,0:T(8,128)(2,1)S(1)} all-gather(bf16[384,256]{1,0:T(8,128)(2,1)S(1)} %copy-done.99), channel_id=1, replica_groups=mesh['dp'=4,'expert'=2,'tensor'=4] {'dp'}, dimensions={0}, use_global_device_ids=true | all-gather | bytes 983040 | tf_op jit(solution)/shard_map/all_gather | solution.py:462
  55.6 22.7 %all_gather.53 = bf16[1536,256]{1,0:T(8,128)(2,1)S(1)} all-gather(bf16[384,256]{1,0:T(8,128)(2,1)S(1)} %copy-done.100), channel_id=1, replica_groups=mesh['dp'=4,'expert'=2,'tensor'=4] {'dp'}, dimensions={0}, use_global_device_ids=true | all-gather | bytes 983040 | tf_op jit(solution)/shard_map/all_gather | solution.py:463
  116.5 11.9 all-gather.3
  128.5 13.6 all_gather.60
  148.5 7.8 mul.999
  175.6 10.2 gather_fusion
  190.7 15.6 gather_fusion.4
  206.3 8.3 broadcast_select_fusion.2
  214.6 65.7 %all_to_all.40 = bf16[2,1024,1536]{2,1,0:T(8,128)(2,1)} all-to-all(bf16[2,1024,1536]{2,1,0:T(8,128)(2,1)S(1)} %get-tuple-element.195), channel_id=1, replica_groups=mesh['dp'=4,'expert'=2,'tensor'=4] {'expert'}, dimensions={0} | all-to-all | bytes 12582912 | tf_op jit(solution)/shard_map/all_to_all | solution.py:85
  291.2 7.9 mul.1060
  309.7 10.2 gather_fusion.2
  323.1 10.1 gather_fusion.6
  333.2 10.3 broadcast_select_fusion
  355.6 61.4 %all-to-all-done.2 = bf16[2,1024,1536]{2,1,0:T(8,128)(2,1)} async-done(((bf16[2,1024,1536]{2,1,0:T(8,128)(2,1)}), bf16[2,1024,1536]{2,1,0:T(8,128)(2,1)}, u32[]{:S(2)}, u32[]{:S(2)}) %all-to-all-start.2) | async-done | bytes 6291488 | tf_op jit(solution)/shard_map/all_to_all | solution.py:85
  435.9 7.8 fusion.103
  449.8 35.0 %all-to-all-done.6 = bf16[2,1024,1536]{2,1,0:T(8,128)(2,1)} async-done(((bf16[2,1024,1536]{2,1,0:T(8,128)(2,1)}), bf16[2,1024,1536]{2,1,0:T(8,128)(2,1)}, u32[]{:S(2)}, u32[]{:S(2)}) %all-to-all-start.6) | async-done | bytes 6291488 | tf_op jit(solution)/shard_map/all_to_all | solution.py:85
  514.8 38.6 %all-to-all-done.1 = bf16[2,1024,1536]{2,1,0:T(8,128)(2,1)} async-done(((bf16[2,1024,1536]{2,1,0:T(8,128)(2,1)}), bf16[2,1024,1536]{2,1,0:T(8,128)(2,1)}, u32[]{:S(2)}, u32[]{:S(2)}) %all-to-all-start.1) | async-done | bytes 6291488 | tf_op jit(solution)/shard_map/all_to_all | solution.py:98
  570.8 50.6 %all-to-all-done.3 = bf16[2,1024,1536]{2,1,0:T(8,128)(2,1)} async-done(((bf16[2,1024,1536]{2,1,0:T(8,128)(2,1)}), bf16[2,1024,1536]{2,1,0:T(8,128)(2,1)}, u32[]{:S(2)}, u32[]{:S(2)}) %all-to-all-start.3) | async-done | bytes 6291488 | tf_op jit(solution)/shard_map/all_to_all | solution.py:98
  637.2 9.1 bitcast_convert_fusion.3
  646.3 12.3 gather_fusion.1
  658.7 7.7 reshape.1131
  666.4 9.5 multiply_reduce_fusion.1
  675.9 14.1 all-to-all-done.5
  696.7 9.1 bitcast_convert_fusion.2
  705.8 12.3 gather_fusion.3
  718.0 7.8 reshape.1135
  725.8 9.5 multiply_reduce_fusion
  735.4 9.1 bitcast_convert_fusion.1
  744.5 12.4 gather_fusion.5
  756.9 7.6 reshape.1138
  770.7 9.1 bitcast_convert_fusion
  779.8 12.3 gather_fusion.7
  792.1 7.6 reshape.1144
  799.7 7.5 reduce_sum.448
  807.2 7.5 reduce_sum.455
  815.5 42.8 %all-reduce.13.cloned.1.call-done = (bf16[256,1536]{1,0:T(8,128)(2,1)}, bf16[256,1536]{1,0:T(8,128)(2,1)}) async-done(((bf16[256,1536]{1,0:T(8,128)(2,1)}, bf16[256,1536]{1,0:T(8,128)(2,1)}), (bf16[256,1536]{1,0:T(8,128)(2,1)}, bf16[256,1536]{1,0:T(8,128)(2,1)})) %all-reduce.13.cloned.1.call-update) | async-done | bytes 1572880 | tf_op jit(solution)/shard_map/psum | solution.py:310
  888.4 7.1 fusion.16
  997.2 18.6 %reduce-scatter.31.cloned.1.call-done = bf16[192,8]{1,0:T(8,128)(2,1)} async-done(((bf16[1536,8]{1,0:T(8,128)(2,1)}), bf16[192,8]{1,0:T(8,128)(2,1)}) %reduce-scatter.31.cloned.1.call-update) | async-done | bytes 3088
  1017.3 47.9 %reduce-scatter.37.cloned.1.call-done = bf16[384,768]{1,0:T(8,128)(2,1)} async-done(((bf16[1536,768]{1,0:T(8,128)(2,1)}), bf16[384,768]{1,0:T(8,128)(2,1)}) %reduce-scatter.37.cloned.1.call-update) | async-done | bytes 589840
  1072.4 42.5 %reduce-scatter.35.cloned.1.call-done = bf16[384,768]{1,0:T(8,128)(2,1)} async-done(((bf16[1536,768]{1,0:T(8,128)(2,1)}), bf16[384,768]{1,0:T(8,128)(2,1)}) %reduce-scatter.35.cloned.1.call-update) | async-done | bytes 589840
  1122.1 42.6 %reduce-scatter.33.cloned.1.call-done = bf16[384,768]{1,0:T(8,128)(2,1)} async-done(((bf16[1536,768]{1,0:T(8,128)(2,1)}), bf16[384,768]{1,0:T(8,128)(2,1)}) %reduce-scatter.33.cloned.1.call-update) | async-done | bytes 589840
  1175.9 59.8 %all-reduce.11.cloned.1.call-done = (bf16[256,1536]{1,0:T(8,128)(2,1)}, bf16[256,1536]{1,0:T(8,128)(2,1)}, bf16[256,1536]{1,0:T(8,128)(2,1)}, bf16[256,1536]{1,0:T(8,128)(2,1)}) async-done(((bf16[256,1536]{1,0:T(8,128)(2,1)}, bf16[256,1536]{1,0:T(8,128)(2,1)}, bf16[256,1536]{1,0:T(8,128)(2,1)}, bf16[256,1536]{1,0:T(8,128)(2,1)}), (bf16[256,1536]{1,0:T(8,128)(2,1)}, bf16[256,1536]{1,0:T(8,128)(2,1)}, ...) | async-done | bytes 3145744 | tf_op jit(solution)/shard_map/psum | solution.py:109
  1238.1 21.8 %all-reduce.2 = (bf16[1536]{0:T(1024)(128)(2,1)S(1)}, bf16[1536]{0:T(1024)(128)(2,1)S(1)}) all-reduce(bf16[1536]{0:T(1024)(128)(2,1)S(1)} %add_convert_fusion.9, bf16[1536]{0:T(1024)(128)(2,1)S(1)} %add_convert_fusion.8), channel_id=6, replica_groups=mesh['dp'=4,'expert'=2,'tensor'=4] {'dp','expert'}, use_global_device_ids=true, to_apply=%region_68.69.clone | all-reduce | flops 3072 | bytes 12288
  1260.5 43.3 %reduce-scatter.29.cloned.1.call-done = bf16[384,192]{0,1:T(8,128)(2,1)} async-done(((bf16[384,1536]{0,1:T(8,128)(2,1)}), bf16[384,192]{0,1:T(8,128)(2,1)}) %reduce-scatter.29.cloned.1.call-update) | async-done | bytes 147472 | tf_op jit(solution)/shard_map/reduce_scatter | solution.py:132
  1305.5 65.2 %reduce-scatter.23.cloned.1.call-done = bf16[192,384]{1,0:T(8,128)(2,1)} async-done(((bf16[1536,384]{1,0:T(8,128)(2,1)}), bf16[192,384]{1,0:T(8,128)(2,1)}) %reduce-scatter.23.cloned.1.call-update) | async-done | bytes 147472 | tf_op jit(solution)/shard_map/reduce_scatter | solution.py:129
  1379.8 92.6 %reduce-scatter.27.cloned.1.call-done = f32[48,256]{1,0:T(8,128)} async-done(((f32[1536,256]{1,0:T(8,128)}), f32[48,256]{1,0:T(8,128)}) %reduce-scatter.27.cloned.1.call-update) | async-done | bytes 49168 | tf_op jit(solution)/shard_map/reduce_scatter | solution.py:144
  1472.4 101.7 %reduce-scatter.25.cloned.1.call-done = f32[48,256]{1,0:T(8,128)} async-done(((f32[1536,256]{1,0:T(8,128)}), f32[48,256]{1,0:T(8,128)}) %reduce-scatter.25.cloned.1.call-update) | async-done | bytes 49168 | tf_op jit(solution)/shard_map/reduce_scatter | solution.py:143
  (610 shorter events, 382.8 us)
Async XLA Ops:
  7.2 96.0 %all-gather.10.cloned.1.call-start = ((), (), s32[]{:S(2)}) async-start(), calls=%async_computation.18 | async-start | bytes 1474560 | tf_op jit(solution)/shard_map/all_gather | solution.py:461
  7.2 46.7 %copy-start.4 = (bf16[2,256,1536]{2,1,0:T(8,128)(2,1)S(1)}, bf16[2,256,1536]{2,1,0:T(8,128)(2,1)}, u32[]{:S(2)}) copy-start(bf16[2,256,1536]{2,1,0:T(8,128)(2,1)} %param.15) | copy-start | bytes 4718596
  7.9 102.8 %all-gather.12.cloned.1.call-start = ((), (), s32[]{:S(2)}) async-start(), calls=%async_computation.19 | async-start | bytes 1474560 | tf_op jit(solution)/shard_map/all_gather | solution.py:464
  8.7 162.7 %all-reduce.15.cloned.1.call-start = ((), (), s32[]{:S(2)}) async-start(), calls=%async_computation.35 | async-start | bytes 3145728 | tf_op jit(solution)/shard_map/psum | solution.py:109
  24.7 81.6 %copy-start.91 = (f32[1536]{0:T(1024)}, f32[1536]{0:T(1024)S(1)}, u32[]{:S(2)}) copy-start(f32[1536]{0:T(1024)S(1)} %reshape.1266) | copy-start | bytes 18436
  53.9 50.8 %copy-start.123 = (f32[256]{0:T(256)}, f32[256]{0:T(256)S(1)}, u32[]{:S(2)}) copy-start(f32[256]{0:T(256)S(1)} %get-tuple-element.233) | copy-start | bytes 3076
  54.0 52.4 %copy-start.121 = (f32[256]{0:T(256)}, f32[256]{0:T(256)S(1)}, u32[]{:S(2)}) copy-start(f32[256]{0:T(256)S(1)} %get-tuple-element.232) | copy-start | bytes 3076
  54.4 24.3 %copy-start.32 = (bf16[256,1536]{1,0:T(8,128)(2,1)}, bf16[256,1536]{1,0:T(8,128)(2,1)S(1)}, u32[]{:S(2)}) copy-start(bf16[256,1536]{1,0:T(8,128)(2,1)S(1)} %get-tuple-element.163) | copy-start | bytes 2359300
  55.6 24.4 %copy-start.155 = (s32[2,9]{1,0:T(2,128)S(1)}, s32[2,9]{1,0:T(2,128)}, u32[]{:S(2)}) copy-start(s32[2,9]{1,0:T(2,128)} %param.18) | copy-start | bytes 220
  55.6 24.9 %copy-start.152 = (f32[64]{0:T(128)S(1)}, f32[64]{0:T(128)}, u32[]{:S(2)}) copy-start(f32[64]{0:T(128)} %multiply_power_fusion) | copy-start | bytes 772
  81.7 25.3 %copy-start.61 = (f32[256,64]{0,1:T(8,128)}, f32[256,64]{0,1:T(8,128)S(1)}, u32[]{:S(2)}) copy-start(f32[256,64]{0,1:T(8,128)S(1)} %get-tuple-element.219) | copy-start | bytes 196612
  81.7 25.3 %copy-start.76 = (f32[256,64]{0,1:T(8,128)}, f32[256,64]{0,1:T(8,128)S(1)}, u32[]{:S(2)}) copy-start(f32[256,64]{0,1:T(8,128)S(1)} %get-tuple-element.218) | copy-start | bytes 196612
  115.0 27.0 %copy-start.44 = (bf16[2,256,1536]{2,1,0:T(8,128)(2,1)S(1)}, bf16[2,256,1536]{2,1,0:T(8,128)(2,1)}, u32[]{:S(2)}) copy-start(bf16[2,256,1536]{2,1,0:T(8,128)(2,1)} %param.16) | copy-start | bytes 4718596
  115.1 308.3 %all-gather.16.cloned.1.call-start = ((), (), s32[]{:S(2)}) async-start(), calls=%async_computation.21 | async-start | bytes 2949120 | tf_op jit(solution)/shard_map/all_gather | solution.py:470
  115.7 58.8 %copy-start.119 = (s32[256,4]{0,1:T(4,128)}, s32[256,4]{0,1:T(4,128)S(1)}, u32[]{:S(2)}) copy-start(s32[256,4]{0,1:T(4,128)S(1)} %get-tuple-element.188) | copy-start | bytes 12292
  115.7 192.5 %copy-start.117 = (s32[256,4]{0,1:T(4,128)}, s32[256,4]{0,1:T(4,128)S(1)}, u32[]{:S(2)}) copy-start(s32[256,4]{0,1:T(4,128)S(1)} %get-tuple-element.190) | copy-start | bytes 12292
  128.4 45.1 %copy-start.113 = (f32[1536]{0:T(1024)}, f32[1536]{0:T(1024)S(1)}, u32[]{:S(2)}) copy-start(f32[1536]{0:T(1024)S(1)} %reshape.1267) | copy-start | bytes 18436
  142.0 165.9 %copy-start.80 = (bf16[1536,8]{0,1:T(8,128)(2,1)}, bf16[1536,8]{0,1:T(8,128)(2,1)S(1)}, u32[]{:S(2)}) copy-start(bf16[1536,8]{0,1:T(8,128)(2,1)S(1)} %all_gather.60) | copy-start | bytes 73732
  174.2 135.0 %copy-start = (bf16[256,1536]{1,0:T(8,128)(2,1)}, bf16[256,1536]{1,0:T(8,128)(2,1)S(1)}, u32[]{:S(2)}) copy-start(bf16[256,1536]{1,0:T(8,128)(2,1)S(1)} %get-tuple-element.161) | copy-start | bytes 2359300
  280.3 68.5 %all-to-all-start.4 = ((bf16[2,1024,1536]{2,1,0:T(8,128)(2,1)}), bf16[2,1024,1536]{2,1,0:T(8,128)(2,1)}, u32[]{:S(2)}, u32[]{:S(2)}) async-start(bf16[2,1024,1536]{2,1,0:T(8,128)(2,1)} %get-tuple-element.194), calls=%async_computation.4 | async-start | bytes 12582912 | tf_op jit(solution)/shard_map/all_to_all | solution.py:85
  286.8 142.3 %all-gather.14.cloned.1.call-start = ((), (), s32[]{:S(2)}) async-start(), calls=%async_computation.20 | async-start | bytes 2949120 | tf_op jit(solution)/shard_map/all_gather | solution.py:469
  348.8 68.3 %all-to-all-start.2 = ((bf16[2,1024,1536]{2,1,0:T(8,128)(2,1)}), bf16[2,1024,1536]{2,1,0:T(8,128)(2,1)}, u32[]{:S(2)}, u32[]{:S(2)}) async-start(bf16[2,1024,1536]{2,1,0:T(8,128)(2,1)} %get-tuple-element.197), calls=%async_computation.2 | async-start | bytes 12582912 | tf_op jit(solution)/shard_map/all_to_all | solution.py:85
  355.1 80.8 %all-gather.18.cloned.1.call-start = ((), (), s32[]{:S(2)}) async-start(), calls=%async_computation.22 | async-start | bytes 2949120 | tf_op jit(solution)/shard_map/all_gather | solution.py:471
  417.1 67.7 %all-to-all-start.6 = ((bf16[2,1024,1536]{2,1,0:T(8,128)(2,1)}), bf16[2,1024,1536]{2,1,0:T(8,128)(2,1)}, u32[]{:S(2)}, u32[]{:S(2)}) async-start(bf16[2,1024,1536]{2,1,0:T(8,128)(2,1)} %get-tuple-element.196), calls=%async_computation.7 | async-start | bytes 12582912 | tf_op jit(solution)/shard_map/all_to_all | solution.py:85
  443.7 118.0 %copy-start.51 = (bf16[2,4,256,192]{2,3,0,1:T(8,128)(2,1)}, bf16[2,4,256,192]{2,3,0,1:T(8,128)(2,1)S(1)}, u32[]{:S(2)}) copy-start(bf16[2,4,256,192]{2,3,0,1:T(8,128)(2,1)S(1)} %get-tuple-element.153) | copy-start | bytes 2359300
  484.8 68.6 %all-to-all-start.1 = ((bf16[2,1024,1536]{2,1,0:T(8,128)(2,1)}), bf16[2,1024,1536]{2,1,0:T(8,128)(2,1)}, u32[]{:S(2)}, u32[]{:S(2)}) async-start(bf16[2,1024,1536]{2,1,0:T(8,128)(2,1)} %bitcast.528), calls=%async_computation.1 | async-start | bytes 12582912 | tf_op jit(solution)/shard_map/all_to_all | solution.py:98
  553.4 67.9 %all-to-all-start.3 = ((bf16[2,1024,1536]{2,1,0:T(8,128)(2,1)}), bf16[2,1024,1536]{2,1,0:T(8,128)(2,1)}, u32[]{:S(2)}, u32[]{:S(2)}) async-start(bf16[2,1024,1536]{2,1,0:T(8,128)(2,1)} %bitcast.527), calls=%async_computation.3 | async-start | bytes 12582912 | tf_op jit(solution)/shard_map/all_to_all | solution.py:98
  621.4 68.7 %all-to-all-start.5 = ((bf16[2,1024,1536]{2,1,0:T(8,128)(2,1)}), bf16[2,1024,1536]{2,1,0:T(8,128)(2,1)}, u32[]{:S(2)}, u32[]{:S(2)}) async-start(bf16[2,1024,1536]{2,1,0:T(8,128)(2,1)} %bitcast.526), calls=%async_computation.5 | async-start | bytes 12582912 | tf_op jit(solution)/shard_map/all_to_all | solution.py:98
  690.1 80.6 %all-to-all-start.7 = ((bf16[2,1024,1536]{2,1,0:T(8,128)(2,1)}), bf16[2,1024,1536]{2,1,0:T(8,128)(2,1)}, u32[]{:S(2)}, u32[]{:S(2)}) async-start(bf16[2,1024,1536]{2,1,0:T(8,128)(2,1)} %bitcast.525), calls=%async_computation.8 | async-start | bytes 12582912 | tf_op jit(solution)/shard_map/all_to_all | solution.py:98
  696.4 161.9 %all-reduce.13.cloned.1.call-start = ((), (), s32[]{:S(2)}) async-start(), calls=%async_computation.34 | async-start | bytes 3145728 | tf_op jit(solution)/shard_map/psum | solution.py:310
  814.7 43.5 %copy-start.81 = (bf16[1536,8]{0,1:T(8,128)(2,1)S(1)}, bf16[1536,8]{0,1:T(8,128)(2,1)}, u32[]{:S(2)}) copy-start(bf16[1536,8]{0,1:T(8,128)(2,1)} %copy-done.80) | copy-start | bytes 73732
  814.7 45.1 %copy-start.25 = (bf16[256,1536]{1,0:T(8,128)(2,1)S(1)}, bf16[256,1536]{1,0:T(8,128)(2,1)}, u32[]{:S(2)}) copy-start(bf16[256,1536]{1,0:T(8,128)(2,1)} %get-tuple-element.149) | copy-start | bytes 2359300
  814.8 45.1 %copy-start.5 = (bf16[2,256,1536]{2,1,0:T(8,128)(2,1)S(1)}, bf16[2,256,1536]{2,1,0:T(8,128)(2,1)}, u32[]{:S(2)}) copy-start(bf16[2,256,1536]{2,1,0:T(8,128)(2,1)} %param.15) | copy-start | bytes 4718596
  814.8 45.1 %copy-start.22 = (bf16[256,1536]{1,0:T(8,128)(2,1)S(1)}, bf16[256,1536]{1,0:T(8,128)(2,1)}, u32[]{:S(2)}) copy-start(bf16[256,1536]{1,0:T(8,128)(2,1)} %get-tuple-element.148) | copy-start | bytes 2359300
  814.8 45.1 %copy-start.114 = (f32[1536]{0:T(1024)S(1)}, f32[1536]{0:T(1024)}, u32[]{:S(2)}) copy-start(f32[1536]{0:T(1024)} %copy-done.113) | copy-start | bytes 18436
  814.8 45.1 %copy-start.144 = (f32[256]{0:T(256)S(1)}, f32[256]{0:T(256)}, u32[]{:S(2)}) copy-start(f32[256]{0:T(256)} %copy-done.143) | copy-start | bytes 3076
  814.8 45.1 %copy-start.146 = (f32[256]{0:T(256)S(1)}, f32[256]{0:T(256)}, u32[]{:S(2)}) copy-start(f32[256]{0:T(256)} %copy-done.145) | copy-start | bytes 3076
  814.8 154.0 %reduce-scatter.19.cloned.1.call-start = ((), (), s32[]{:S(2)}) async-start(), calls=%async_computation.23 | async-start | bytes 589824 | tf_op jit(solution)/shard_map/reduce_scatter | solution.py:384
  879.3 92.5 %reduce-scatter.21.cloned.1.call-start = ((), (), s32[]{:S(2)}) async-start(), calls=%async_computation.24 | async-start | bytes 589824 | tf_op jit(solution)/shard_map/reduce_scatter | solution.py:384
  880.2 135.5 %reduce-scatter.31.cloned.1.call-start = ((), (), s32[]{:S(2)}) async-start(), calls=%async_computation.29 | async-start | bytes 442368
  888.4 176.8 %reduce-scatter.37.cloned.1.call-start = ((), (), s32[]{:S(2)}) async-start(), calls=%async_computation.32 | async-start | bytes 2949120
  907.6 207.2 %reduce-scatter.35.cloned.1.call-start = ((), (), s32[]{:S(2)}) async-start(), calls=%async_computation.31 | async-start | bytes 2949120
  930.9 233.9 %reduce-scatter.33.cloned.1.call-start = ((), (), s32[]{:S(2)}) async-start(), calls=%async_computation.30 | async-start | bytes 2949120
  954.1 281.5 %all-reduce.11.cloned.1.call-start = ((), (), s32[]{:S(2)}) async-start(), calls=%async_computation.33 | async-start | bytes 6291456 | tf_op jit(solution)/shard_map/psum | solution.py:109
  983.8 320.0 %reduce-scatter.29.cloned.1.call-start = ((), (), s32[]{:S(2)}) async-start(), calls=%async_computation.28 | async-start | bytes 1327104 | tf_op jit(solution)/shard_map/reduce_scatter | solution.py:132
  988.6 382.1 %reduce-scatter.23.cloned.1.call-start = ((), (), s32[]{:S(2)}) async-start(), calls=%async_computation.25 | async-start | bytes 1327104 | tf_op jit(solution)/shard_map/reduce_scatter | solution.py:129
  991.4 481.0 %reduce-scatter.27.cloned.1.call-start = ((), (), s32[]{:S(2)}) async-start(), calls=%async_computation.27 | async-start | bytes 1622016 | tf_op jit(solution)/shard_map/reduce_scatter | solution.py:144
  995.3 578.8 %reduce-scatter.25.cloned.1.call-start = ((), (), s32[]{:S(2)}) async-start(), calls=%async_computation.26 | async-start | bytes 1622016 | tf_op jit(solution)/shard_map/reduce_scatter | solution.py:143
  (135 other events, 679.8 us)
Sparse Core Ops, SparseCore 0:
  9.6 45.8 all-gather.9
  57.1 33.2 all-gather.11
  115.2 43.9 all-reduce.14
  160.6 50.3 all-gather.15
  288.9 50.2 all-gather.13
  357.2 50.2 all-gather.17
  814.9 43.3 all-reduce.12
  879.4 34.1 reduce-scatter.18
  917.0 34.1 reduce-scatter.20
  954.3 61.4 reduce-scatter.30
  1018.1 47.0 reduce-scatter.36
  1067.3 47.5 reduce-scatter.34
  1117.2 47.4 reduce-scatter.32
  1167.1 68.4 all-reduce.10
  1239.5 64.2 reduce-scatter.28
  1307.7 63.0 reduce-scatter.22
  1376.4 95.9 reduce-scatter.26
  1478.1 96.0 reduce-scatter.24
where the time goes:
time: 1590 us; the launch traced here: 1580 us
  waiting for transfers between devices  765 us (48%)
  local copies, waits for them, and re-layouts  266 us (17%)
  blocking collectives  204 us (13%)
  other arithmetic  149 us (9%)
  matrix products  132 us (8%)
  starting transfers between devices  46.9 us (3%)
  between operations  17.6 us (1%)
    unnamed x22, waiting for transfers between devices  155 us
    all_to_all x4, waiting for transfers between devices, return_rows(): lax.all_to_all(partial_value.reshape(expert_count, per_device * capacity,...  103 us
    reduce_scatter x1, waiting for transfers between devices, reduce_grads(): lax.psum_scatter(key_grad, ('dp', 'expert', 'tensor'), scatter_dimension=...  102 us
    all_to_all x3, waiting for transfers between devices, send_rows(): lax.all_to_all(rows.reshape(expert_count, per_device * capacity, feature)...  102 us
    reduce_scatter x1, waiting for transfers between devices, reduce_grads(): lax.psum_scatter(value_grad, ('dp', 'expert', 'tensor'), scatter_dimensio...  92.6 us
    unnamed x333, local copies, waits for them, and re-layouts  69.7 us
    all_to_all x1, blocking collectives, send_rows(): lax.all_to_all(rows.reshape(expert_count, per_device * capacity, feature)...  65.7 us
    reduce_scatter x1, waiting for transfers between devices, reduce_grads(): lax.psum_scatter(query_grad.astype(jnp.bfloat16), ('dp', 'expert'), scatt...  65.2 us
  transfers between devices with their start and end apart: 25, of which 16 were waited for; matrix products, arithmetic and copies ran while one was open for 29% of the time, Pallas kernels for 0%

commit v1 on v0

v1 whole, which is shorter than its diff:
```python
import jax
import jax.numpy as jnp
from jax import lax
from jax.sharding import PartitionSpec as P

QUERY_HEADS = 12
KEY_VALUE_HEADS = 2
HEAD_SIZE = 128
GROUP = QUERY_HEADS // KEY_VALUE_HEADS
EPS = 1e-05
ROPE_BASE = 10000.0
NEG = -1e30
F32 = jnp.float32
BF16 = jnp.bfloat16


def dot(left, right, dims):
    return lax.dot_general(left, right, (dims, ((), ())), preferred_element_type=F32)


def norm_factor(rows):
    return lax.rsqrt(jnp.mean(rows * rows, -1, keepdims=True) + EPS)


def norm_back(rows, factor, gain, upstream):
    scaled = upstream * gain
    gain_grad = jnp.sum(upstream * rows * factor, 0)
    inner = jnp.mean(scaled * rows, -1, keepdims=True)
    return factor * scaled - rows * (factor * factor * factor * inner), gain_grad


def layout(starts, parents, places, length):
    labels = jnp.arange(starts.shape[1], dtype=jnp.int32)

    def pick(table, at):
        hot = at[:, :, None] == labels[None, None, :]
        return jnp.sum(jnp.where(hot, table[:, None, :], 0), 2, dtype=jnp.int32)

    segment = jnp.sum((starts[:, None, :] <= places[None, :, None]).astype(jnp.int32), 2) - 1
    above = pick(parents, segment)
    further = pick(parents, above)
    ends = jnp.concatenate(
        [starts[:, 1:], jnp.full((starts.shape[0], 1), length, jnp.int32)], 1
    )
    lengths = ends - starts
    depths = (
        places[None, :]
        - pick(starts, segment)
        + jnp.where(segment != 0, pick(lengths, above), 0)
        + jnp.where(above != 0, pick(lengths, further), 0)
    )
    return segment, above, further, depths


def angles(depths):
    half = HEAD_SIZE // 2
    frequency = ROPE_BASE ** (-2.0 * jnp.arange(half, dtype=F32) / HEAD_SIZE)
    turning = depths.astype(F32)[..., None] * frequency
    return jnp.cos(turning), jnp.sin(turning)


def rotate(heads, cosine, sine):
    half = HEAD_SIZE // 2
    front, back = heads[..., :half], heads[..., half:]
    return jnp.concatenate([front * cosine - back * sine, back * cosine + front * sine], -1)


def shards(
    tokens,
    cotangent,
    seg_start,
    seg_parent,
    routes,
    attn_gain,
    w_query,
    w_key,
    w_value,
    w_output,
    moe_gain,
    w_router,
    w_gate,
    w_up,
    w_down,
):
    trees, rows, width = tokens.shape
    expert_count = lax.axis_size("expert")
    tensor_count = lax.axis_size("tensor")
    tensor_at = lax.axis_index("tensor")
    expert_at = lax.axis_index("expert")
    length = rows * expert_count
    heads = w_query.shape[1] // HEAD_SIZE
    kv_head = tensor_at * heads // GROUP
    inv_root = HEAD_SIZE ** (-0.5)
    own_experts = w_gate.shape[0]
    quarter = w_gate.shape[2]
    all_experts = w_router.shape[1]

    def over_dp(array, axis):
        return lax.all_gather(array, "dp", axis=axis, tiled=True)

    w_query = over_dp(w_query, 0)
    w_output = over_dp(w_output, 1)
    gate_t = over_dp(jnp.swapaxes(w_gate, 1, 2), 2)
    up_t = over_dp(jnp.swapaxes(w_up, 1, 2), 2)
    down = over_dp(w_down, 2)
    small = over_dp(
        jnp.concatenate(
            [
                lax.dynamic_slice_in_dim(w_key, kv_head * HEAD_SIZE, HEAD_SIZE, 1),
                lax.dynamic_slice_in_dim(w_value, kv_head * HEAD_SIZE, HEAD_SIZE, 1),
                w_router,
                attn_gain[:, None],
                moe_gain[:, None],
            ],
            1,
        ),
        0,
    )
    w_kv = small[:, : 2 * HEAD_SIZE]
    w_router = small[:, 2 * HEAD_SIZE : 2 * HEAD_SIZE + all_experts]
    attn_gain = small[:, -2].astype(F32)
    moe_gain = small[:, -1].astype(F32)

    all_places = jnp.arange(length, dtype=jnp.int32)
    places = expert_at * rows + jnp.arange(rows, dtype=jnp.int32)
    segment, above, further, depths = layout(seg_start, seg_parent, places, length)
    key_segment = layout(seg_start, seg_parent, all_places, length)[0]
    cosine, sine = angles(depths)
    of_key = key_segment[:, None, :]
    visible = (
        (of_key == segment[:, :, None])
        | (of_key == above[:, :, None])
        | (of_key == further[:, :, None])
    ) & (all_places[None, None, :] <= places[None, :, None])

    residual = tokens.astype(F32).reshape(trees * rows, width)
    factor_one = norm_factor(residual)
    hidden_one = (residual * factor_one * attn_gain).astype(BF16)
    query_pre = dot(hidden_one, w_query, ((1,), (0,))).reshape(trees, rows, heads, HEAD_SIZE)
    kv_pre = dot(hidden_one, w_kv, ((1,), (0,))).reshape(trees, rows, 2 * HEAD_SIZE)
    queries = rotate(query_pre, cosine[:, :, None, :], sine[:, :, None, :]).astype(BF16)
    own_keys = rotate(kv_pre[..., :HEAD_SIZE], cosine, sine).astype(BF16)
    own_kv = jnp.concatenate([own_keys, kv_pre[..., HEAD_SIZE:].astype(BF16)], -1)
    keys_values = lax.all_gather(own_kv, "expert", axis=1, tiled=True)
    keys, values = keys_values[..., :HEAD_SIZE], keys_values[..., HEAD_SIZE:]
    scores = jnp.einsum("bqhd,bkd->bhqk", queries, keys, preferred_element_type=F32) * inv_root
    scores = jnp.where(visible[:, None], scores, NEG)
    row_max = jnp.max(scores, -1, keepdims=True)
    exponent = jnp.exp(scores - row_max)
    probs = exponent / jnp.sum(exponent, -1, keepdims=True)
    probs_low = probs.astype(BF16)
    context = jnp.einsum("bhqk,bkd->bqhd", probs_low, values, preferred_element_type=F32)
    context_low = context.reshape(trees * rows, heads * HEAD_SIZE).astype(BF16)
    attn_out = dot(context_low, w_output, ((1,), (0,))).astype(BF16)
    after_attn = residual + lax.psum(attn_out, "tensor").astype(F32)

    factor_two = norm_factor(after_attn)
    hidden_two = (after_attn * factor_two * moe_gain).astype(BF16)
    logits = dot(hidden_two, w_router, ((1,), (0,)))
    chosen = jnp.any(
        routes.reshape(trees * rows, -1)[:, :, None]
        == jnp.arange(all_experts, dtype=jnp.int32)[None, None, :],
        1,
    )
    masked = jnp.where(chosen, logits, NEG)
    raised = jnp.where(chosen, jnp.exp(masked - jnp.max(masked, -1, keepdims=True)), 0.0)
    mixing = raised / jnp.sum(raised, -1, keepdims=True)

    def over_expert(array):
        full = lax.all_gather(
            array.reshape(trees, rows, array.shape[-1]), "expert", axis=1, tiled=True
        )
        return full.reshape(trees * length, array.shape[-1])

    every_hidden = over_expert(hidden_two)
    every_up = over_expert(cotangent)
    every_mix = lax.dynamic_slice_in_dim(
        over_expert(mixing), expert_at * own_experts, own_experts, 1
    )
    count = trees * length
    pre_gate = dot(every_hidden, gate_t.reshape(-1, width), ((1,), (1,)))
    pre_up = dot(every_hidden, up_t.reshape(-1, width), ((1,), (1,)))
    down_rows = down.reshape(-1, width)
    down_back = dot(every_up, down_rows, ((1,), (1,)))
    wide_mix = jnp.repeat(every_mix, quarter, axis=1)
    activated, pull = jax.vjp(jax.nn.gelu, pre_gate)
    hidden = activated * pre_up
    mixed_hidden = (hidden * wide_mix).astype(BF16)
    moe_part = dot(mixed_hidden, down_rows, ((1,), (0,))).astype(BF16)
    gate_part = jnp.sum((hidden * down_back).reshape(count, own_experts, quarter), -1)
    hidden_grad = wide_mix * down_back
    gate_pre = pull(hidden_grad * pre_up)[0].astype(BF16)
    up_pre = (hidden_grad * activated).astype(BF16)
    two_part = (
        dot(gate_pre, gate_t.reshape(-1, width), ((1,), (0,)))
        + dot(up_pre, up_t.reshape(-1, width), ((1,), (0,)))
    ).astype(BF16)
    d_down = dot(mixed_hidden, every_up, ((0,), (0,)))
    d_gate = dot(gate_pre, every_hidden, ((0,), (0,)))
    d_up = dot(up_pre, every_hidden, ((0,), (0,)))

    def to_owner(array):
        array = array.reshape(trees, length, array.shape[-1])
        part = lax.psum_scatter(array, "expert", scatter_dimension=1, tiled=True)
        return lax.psum(part, "tensor").reshape(trees * rows, -1)

    spread = jnp.arange(all_experts) // own_experts == expert_at
    gate_wide = jnp.where(
        spread[None, :], jnp.tile(gate_part, (1, all_experts // own_experts)), 0.0
    )
    two_grad = to_owner(two_part).astype(F32)
    mix_grad = to_owner(gate_wide)
    mixed_out = (after_attn + to_owner(moe_part).astype(F32)).astype(BF16)

    picked_grad = mixing * (mix_grad - jnp.sum(mixing * mix_grad, -1, keepdims=True))
    logit_grad = picked_grad.astype(BF16)
    two_grad = two_grad + dot(logit_grad, w_router, ((1,), (1,)))
    d_router = dot(hidden_two, logit_grad, ((0,), (0,)))
    norm_two, d_moe_gain = norm_back(after_attn, factor_two, moe_gain, two_grad)
    attn_grad = cotangent.astype(F32).reshape(trees * rows, width) + norm_two
    attn_low = attn_grad.astype(BF16)

    d_output = dot(context_low, attn_low, ((0,), (0,)))
    context_grad = (
        dot(attn_low, w_output, ((1,), (1,)))
        .astype(BF16)
        .reshape(trees, rows, heads, HEAD_SIZE)
    )
    prob_grad = jnp.einsum("bqhd,bkd->bhqk", context_grad, values, preferred_element_type=F32)
    score_grad = probs * (prob_grad - jnp.sum(probs * prob_grad, -1, keepdims=True))
    score_grad = score_grad.astype(BF16)
    query_grad = (
        jnp.einsum("bhqk,bkd->bqhd", score_grad, keys, preferred_element_type=F32) * inv_root
    )
    key_grad = (
        jnp.einsum("bhqk,bqhd->bkd", score_grad, queries, preferred_element_type=F32) * inv_root
    )
    value_grad = jnp.einsum("bhqk,bqhd->bkd", probs_low, context_grad, preferred_element_type=F32)
    kv_part = jnp.concatenate([key_grad, value_grad], -1).astype(BF16)
    kv_sum = lax.psum_scatter(kv_part, "expert", scatter_dimension=1, tiled=True)
    sharing = GROUP // heads
    own_rows = rows // sharing
    place = tensor_at % sharing
    kv_rows = kv_sum.reshape(trees, sharing, own_rows, 2 * HEAD_SIZE)
    mine = lax.dynamic_index_in_dim(kv_rows, place, 1, False).astype(F32)
    for step in range(1, sharing):
        order = [
            (at, at // sharing * sharing + (at + step) % sharing) for at in range(tensor_count)
        ]
        away = lax.dynamic_index_in_dim(kv_rows, (place + step) % sharing, 1, False)
        mine = mine + lax.ppermute(away, "tensor", order).astype(F32)

    def own(array):
        return lax.dynamic_slice_in_dim(array, place * own_rows, own_rows, 1)

    key_low = rotate(mine[..., :HEAD_SIZE], own(cosine), -own(sine)).astype(BF16)
    kv_low = jnp.concatenate([key_low, mine[..., HEAD_SIZE:].astype(BF16)], -1)
    kv_low = kv_low.reshape(trees * own_rows, 2 * HEAD_SIZE)
    hidden_own = own(hidden_one.reshape(trees, rows, width)).reshape(trees * own_rows, width)
    d_kv = dot(hidden_own, kv_low, ((0,), (0,)))
    kv_back = dot(kv_low, w_kv, ((1,), (1,))).reshape(trees, own_rows, width)
    query_low = rotate(query_grad, cosine[:, :, None, :], -sine[:, :, None, :])
    query_low = query_low.astype(BF16).reshape(trees * rows, heads * HEAD_SIZE)
    d_query = dot(hidden_one, query_low, ((0,), (0,)))
    one_part = dot(query_low, w_query, ((1,), (1,))).reshape(trees, rows, width)
    one_part = lax.dynamic_update_slice_in_dim(
        one_part, own(one_part) + kv_back, place * own_rows, 1
    ).reshape(trees * rows, width)
    one_grad = lax.psum(one_part.astype(BF16), "tensor").astype(F32)
    norm_one, d_attn_gain = norm_back(residual, factor_one, attn_gain, one_grad)
    d_tokens = (attn_grad + norm_one).reshape(trees, rows, width)

    def scatter_dp(array, axis):
        return lax.psum_scatter(array, "dp", scatter_dimension=axis, tiled=True)

    def scatter_expert(array, axis):
        return lax.psum_scatter(array, "expert", scatter_dimension=axis, tiled=True)

    def experts_home(array):
        return scatter_dp(array.astype(BF16), 1).astype(F32).reshape(own_experts, quarter, -1)

    d_gate, d_up, d_down = experts_home(d_gate), experts_home(d_up), experts_home(d_down)
    d_query = scatter_expert(scatter_dp(d_query.astype(BF16), 0), 0).astype(F32)
    d_output = scatter_expert(scatter_dp(d_output.astype(BF16), 1), 1).astype(F32)
    flat = jnp.concatenate([d_attn_gain[:, None], d_moe_gain[:, None], d_router], 1)
    flat = scatter_expert(scatter_dp(flat, 0), 0)
    of_head = (jnp.arange(KEY_VALUE_HEADS) == kv_head).astype(F32)[None, None, :, None]
    d_kv = scatter_expert(scatter_dp(d_kv, 0), 0).reshape(-1, 2, 1, HEAD_SIZE) * of_head
    d_kv = d_kv.reshape(-1, 2 * KEY_VALUE_HEADS * HEAD_SIZE)
    d_kv = lax.psum_scatter(d_kv, "tensor", scatter_dimension=0, tiled=True)
    return (
        mixed_out.reshape(trees, rows, width),
        d_tokens,
        flat[:, 0],
        d_query,
        d_kv[:, : KEY_VALUE_HEADS * HEAD_SIZE],
        d_kv[:, KEY_VALUE_HEADS * HEAD_SIZE :],
        d_output,
        flat[:, 1],
        flat[:, 2:],
        jnp.swapaxes(d_gate, 1, 2),
        jnp.swapaxes(d_up, 1, 2),
        d_down,
    )


def solution(mesh):
    placed = (
        P("dp", "expert", None),
        P("dp", "expert", None),
        P("dp", None),
        P("dp", None),
        P("dp", "expert", None),
        P("dp"),
        P("dp", "tensor"),
        P("dp", None),
        P("dp", None),
        P("tensor", "dp"),
        P("dp"),
        P("dp", None),
        P("expert", "dp", "tensor"),
        P("expert", "dp", "tensor"),
        P("expert", "tensor", "dp"),
    )
    return jax.shard_map(
        shards,
        mesh=mesh,
        in_specs=placed,
        out_specs=(
            P("dp", "expert", None),
            P("dp", "expert", None),
            P(("dp", "expert")),
            P(("dp", "expert"), "tensor"),
            P(("dp", "expert", "tensor"), None),
            P(("dp", "expert", "tensor"), None),
            P("tensor", ("dp", "expert")),
            P(("dp", "expert")),
            P(("dp", "expert"), None),
            P("expert", "dp", "tensor"),
            P("expert", "dp", "tensor"),
            P("expert", "tensor", "dp"),
        ),
        check_vma=False,
    )
```

time: 1590 us -> 1050 us (0.66)
  local copies, waits for them, and re-layouts: 266 us -> 80.6 us
  blocking collectives: 204 us -> 57.8 us
  other arithmetic: 149 us -> 55.9 us
  starting transfers between devices: 46.9 us -> 1.64 us
  waiting for transfers between devices: 765 us -> 729 us
  matrix products: 132 us -> 103 us
    all_gather x5 -> x7, waiting for transfers between devices: 0.05 us -> 231 us  [the longest x5 147 us: over_dp(): return lax.all_gather(array, 'dp', axis=axis, tiled=True)]
    all_to_all x7 -> x0, waiting for transfers between devices: 205 us -> none  [the longest x4 103 us: return_rows(): lax.all_to_all(partial_value.reshape(expert_count, per_device * capacity,...]
    reduce_scatter x6 -> x9, waiting for transfers between devices: 303 us -> 147 us  [the longest x2 68.7 us: to_owner(): part = lax.psum_scatter(array, 'expert', scatter_dimension=1, tiled=True)]
    gather x8 -> x0, local copies, waits for them, and re-layouts: 95.3 us -> none  [the longest x2 25.7 us: micro_step(): send_back[slot_pair]]
    all_to_all x1 -> x0, blocking collectives: 65.7 us -> none  [send_rows(): lax.all_to_all(rows.reshape(expert_count, per_device * capacity, feature)...]
    all_gather x9 -> x3, blocking collectives: 111 us -> 45.3 us  [the longest x1 32.7 us: over_dp(): return lax.all_gather(array, 'dp', axis=axis, tiled=True)]
    unnamed x22 -> x33, waiting for transfers between devices: 155 us -> 204 us
    all_to_all x7 -> x0, starting transfers between devices: 45.3 us -> none  [the longest x4 26.3 us: return_rows(): lax.all_to_all(partial_value.reshape(expert_count, per_device * capacity,...]
  transfers between devices with their start and end apart: 25 -> 27, of which waited for: 16 -> 24; matrix products, arithmetic and copies ran while one was open for 29% -> 16% of each run, Pallas kernels for 0% -> 0%
where the time goes in v1:
time: 1050 us; the launch traced here: 1040 us
  waiting for transfers between devices  729 us (69%)
  matrix products  103 us (10%)
  local copies, waits for them, and re-layouts  80.6 us (8%)
  blocking collectives  57.8 us (6%)
  other arithmetic  55.9 us (5%)
  between operations  15.1 us (1%)
    unnamed x33, waiting for transfers between devices  204 us
    all_gather x5, waiting for transfers between devices, over_dp(): return lax.all_gather(array, 'dp', axis=axis, tiled=True)  147 us
    psum x2, waiting for transfers between devices, to_owner(): return lax.psum(part, 'tensor').reshape(trees * rows, -1)  108 us
    dot_general x21, matrix products, dot(): lax.dot_general(left, right, (dims, ((), ())), preferred_element_type=F32)  90.6 us
    all_gather x2, waiting for transfers between devices, over_expert(): lax.all_gather(array.reshape(trees, rows, array.shape[-1]), 'expert', axi...  84 us
    reduce_scatter x2, waiting for transfers between devices, to_owner(): part = lax.psum_scatter(array, 'expert', scatter_dimension=1, tiled=True)  68.7 us
    unnamed x121, local copies, waits for them, and re-layouts  48.4 us
    psum x1, waiting for transfers between devices, shards(): after_attn = residual + lax.psum(attn_out, 'tensor').astype(F32)  39.8 us
  transfers between devices with their start and end apart: 27, of which 24 were waited for; matrix products, arithmetic and copies ran while one was open for 16% of the time, Pallas kernels for 0%

profile of v1, /device:TPU:0, one launch (start us, length us, event | category | flops | bytes accessed | tf_op | source)
XLA Modules:
  0.0 1043.4 jit_solution(15651364704823093715)
XLA Ops:
  14.4 32.7 %all_gather.30 = bf16[1536,266]{0,1:T(8,128)(2,1)S(1)} all-gather(bf16[384,266]{0,1:T(8,128)(2,1)S(1)} %concatenate.32), channel_id=1, replica_groups=mesh['dp'=4,'expert'=2,'tensor'=4] {'dp'}, dimensions={0}, use_global_device_ids=true | all-gather | bytes 1021440 | tf_op jit(solution)/shard_map/all_gather | solution.py:99
  55.3 7.8 all_gather.31
  69.5 4.1 fusion.82
  76.3 8.6 all-gather.10.cloned.1.call-done
  84.9 3.4 convolution_convert_fusion.4
  91.0 39.8 %all-reduce.6.cloned.1.call-done = bf16[512,1536]{1,0:T(8,128)(2,1)} async-done(((bf16[512,1536]{1,0:T(8,128)(2,1)}), bf16[512,1536]{1,0:T(8,128)(2,1)}) %all-reduce.6.cloned.1.call-update) | async-done | bytes 1572880 | tf_op jit(solution)/shard_map/psum | solution.py:155
  141.2 41.4 %all-gather.14.cloned.1.call-done = bf16[4,192,1536]{2,1,0:T(8,128)(2,1)} async-done(((bf16[4,192,384]{2,1,0:T(8,128)(2,1)}), bf16[4,192,1536]{2,1,0:T(8,128)(2,1)}) %all-gather.14.cloned.1.call-update) | async-done | bytes 2359312 | tf_op jit(solution)/shard_map/all_gather | solution.py:99
  182.6 45.6 %all-gather.12.cloned.1.call-done = bf16[2,512,1536]{2,1,0:T(8,128)(2,1)} async-done(((bf16[2,256,1536]{2,1,0:T(8,128)(2,1)}), bf16[2,512,1536]{2,1,0:T(8,128)(2,1)}) %all-gather.12.cloned.1.call-update) | async-done | bytes 3145744 | tf_op jit(solution)/shard_map/all_gather | solution.py:170
  228.3 6.9 fusion.84
  235.2 44.9 %all-gather.16.cloned.1.call-done = bf16[4,192,1536]{2,1,0:T(8,128)(2,1)} async-done(((bf16[4,192,384]{2,1,0:T(8,128)(2,1)}), bf16[4,192,1536]{2,1,0:T(8,128)(2,1)}) %all-gather.16.cloned.1.call-update) | async-done | bytes 2359312 | tf_op jit(solution)/shard_map/all_gather | solution.py:99
  280.1 6.9 fusion.85
  287.0 38.3 %all-gather.20.cloned.1.call-done = bf16[2,512,1536]{2,1,0:T(8,128)(2,1)} async-done(((bf16[2,256,1536]{2,1,0:T(8,128)(2,1)}), bf16[2,512,1536]{2,1,0:T(8,128)(2,1)}) %all-gather.20.cloned.1.call-update) | async-done | bytes 3145744 | tf_op jit(solution)/shard_map/all_gather | solution.py:170
  325.3 51.9 %all-gather.18.cloned.1.call-done = bf16[4,192,1536]{2,1,0:T(8,128)(2,1)} async-done(((bf16[4,192,384]{2,1,0:T(8,128)(2,1)}), bf16[4,192,1536]{2,1,0:T(8,128)(2,1)}) %all-gather.18.cloned.1.call-update) | async-done | bytes 2359312 | tf_op jit(solution)/shard_map/all_gather | solution.py:99
  377.3 10.1 fusion.78
  401.1 9.2 reduce-scatter.49.cloned.1.call-done
  416.0 12.4 %psum.38 = f32[512,8]{0,1:T(8,128)} all-reduce(f32[512,8]{0,1:T(8,128)} %bitcast.250), channel_id=1, replica_groups=mesh['dp'=4,'expert'=2,'tensor'=4] {'tensor'}, use_global_device_ids=true, to_apply=%region_21.22 | all-reduce | flops 4096 | bytes 32768 | tf_op jit(solution)/shard_map/psum | solution.py:205
  429.8 4.8 all_gather.37
  434.6 6.3 multiply_convert_fusion
  443.7 4.3 add_convert_fusion
  448.0 42.6 %reduce-scatter.33.cloned.1.call-done = bf16[2,256,1536]{2,1,0:T(8,128)(2,1)} async-done(((bf16[2,512,1536]{2,1,0:T(8,128)(2,1)}), bf16[2,256,1536]{2,1,0:T(8,128)(2,1)}) %reduce-scatter.33.cloned.1.call-update) | async-done | bytes 1572880 | tf_op jit(solution)/shard_map/reduce_scatter | solution.py:204
  492.0 43.9 %all-reduce.8.cloned.1.call-done = bf16[512,1536]{1,0:T(8,128)(2,1)} async-done(((bf16[512,1536]{1,0:T(8,128)(2,1)}), bf16[512,1536]{1,0:T(8,128)(2,1)}) %all-reduce.8.cloned.1.call-update) | async-done | bytes 1572880 | tf_op jit(solution)/shard_map/psum | solution.py:205
  535.9 3.3 multiply_reduce_fusion
  554.6 6.5 convolution_convert_fusion
  564.9 4.2 reduce-scatter.35.cloned.1.call-done
  574.3 4.2 fusion.32
  589.3 26.2 %reduce-scatter.31.cloned.1.call-done = bf16[2,256,1536]{2,1,0:T(8,128)(2,1)} async-done(((bf16[2,512,1536]{2,1,0:T(8,128)(2,1)}), bf16[2,256,1536]{2,1,0:T(8,128)(2,1)}) %reduce-scatter.31.cloned.1.call-update) | async-done | bytes 1572880 | tf_op jit(solution)/shard_map/reduce_scatter | solution.py:204
  622.6 63.8 %all-reduce.10.cloned.1.call-done = (bf16[512,1536]{1,0:T(8,128)(2,1)}, bf16[512,1536]{1,0:T(8,128)(2,1)}) async-done(((bf16[512,1536]{1,0:T(8,128)(2,1)}, bf16[512,1536]{1,0:T(8,128)(2,1)}), (bf16[512,1536]{1,0:T(8,128)(2,1)}, bf16[512,1536]{1,0:T(8,128)(2,1)})) %all-reduce.10.cloned.1.call-update) | async-done | bytes 3145744 | tf_op jit(solution)/shard_map/psum | solution.py:205
  686.3 3.9 fusion.7
  691.0 3.7 convolution_convert_fusion.5
  697.1 6.4 convolution_convert_fusion.2
  703.5 4.3 copy.172
  707.9 6.4 convolution_convert_fusion.3
  714.3 4.3 copy.170
  718.9 6.4 convolution_convert_fusion.1
  725.3 4.3 copy.174
  732.8 3.5 convolution_convert_fusion.6
  737.0 7.6 reduce-scatter.37.cloned.1.call-done
  746.3 28.7 %reduce-scatter.53.cloned.1.call-done = bf16[384,384]{1,0:T(8,128)(2,1)} async-done(((bf16[1536,384]{1,0:T(8,128)(2,1)}), bf16[384,384]{1,0:T(8,128)(2,1)}) %reduce-scatter.53.cloned.1.call-update) | async-done | bytes 294928
  775.0 49.0 %reduce-scatter.59.cloned.1.call-done = bf16[384,768]{1,0:T(8,128)(2,1)} async-done(((bf16[1536,768]{1,0:T(8,128)(2,1)}), bf16[384,768]{1,0:T(8,128)(2,1)}) %reduce-scatter.59.cloned.1.call-update) | async-done | bytes 589840
  826.1 47.8 %reduce-scatter.57.cloned.1.call-done = bf16[384,768]{1,0:T(8,128)(2,1)} async-done(((bf16[1536,768]{1,0:T(8,128)(2,1)}), bf16[384,768]{1,0:T(8,128)(2,1)}) %reduce-scatter.57.cloned.1.call-update) | async-done | bytes 589840
  876.1 47.7 %reduce-scatter.61.cloned.1.call-done = bf16[384,768]{1,0:T(8,128)(2,1)} async-done(((bf16[1536,768]{1,0:T(8,128)(2,1)}), bf16[384,768]{1,0:T(8,128)(2,1)}) %reduce-scatter.61.cloned.1.call-update) | async-done | bytes 589840
  931.4 24.1 %reduce-scatter.39.cloned.1.call-done = bf16[384,384]{1,0:T(8,128)(2,1)} async-done(((bf16[1536,384]{1,0:T(8,128)(2,1)}), bf16[384,384]{1,0:T(8,128)(2,1)}) %reduce-scatter.39.cloned.1.call-update) | async-done | bytes 294928 | tf_op jit(solution)/shard_map/reduce_scatter | solution.py:274
  955.6 5.6 fusion.4
  961.2 8.4 reduce-scatter.45.cloned.1.call-done
  976.8 6.7 reduce-scatter.51.cloned.1.call-done
  987.5 10.2 reduce-scatter.55.cloned.1.call-done
  999.5 12.4 %reduce-scatter.41.cloned.1.call-done = bf16[192,384]{1,0:T(8,128)(2,1)} async-done(((bf16[384,384]{1,0:T(8,128)(2,1)}), bf16[192,384]{1,0:T(8,128)(2,1)}) %reduce-scatter.41.cloned.1.call-update) | async-done | bytes 147472 | tf_op jit(solution)/shard_map/reduce_scatter | solution.py:277
  1013.6 21.6 %reduce-scatter.47.cloned.1.call-done = f32[48,512]{1,0:T(8,128)} async-done(((f32[192,512]{1,0:T(8,128)}), f32[48,512]{1,0:T(8,128)}) %reduce-scatter.47.cloned.1.call-update) | async-done | bytes 98320 | tf_op jit(solution)/shard_map/reduce_scatter | solution.py:290
  (265 shorter events, 141.3 us)
Async XLA Ops:
  7.2 40.9 %copy-start.11 = (bf16[2,256,1536]{2,1,0:T(8,128)(2,1)S(1)}, bf16[2,256,1536]{2,1,0:T(8,128)(2,1)}, u32[]{:S(2)}) copy-start(bf16[2,256,1536]{2,1,0:T(8,128)(2,1)} %param.15) | copy-start | bytes 4718596
  7.2 57.7 %all-gather.8.cloned.1.call-start = ((), (), s32[]{:S(2)}) async-start(), calls=%async_computation.16 | async-start | bytes 1474560 | tf_op jit(solution)/shard_map/all_gather | solution.py:99
  7.9 77.0 %all-gather.10.cloned.1.call-start = ((), (), s32[]{:S(2)}) async-start(), calls=%async_computation.17 | async-start | bytes 1474560 | tf_op jit(solution)/shard_map/all_gather | solution.py:99
  8.7 122.1 %all-reduce.6.cloned.1.call-start = ((), (), s32[]{:S(2)}) async-start(), calls=%async_computation.18 | async-start | bytes 3145728 | tf_op jit(solution)/shard_map/psum | solution.py:155
  48.1 85.6 %copy-start.29 = (f32[1536]{0:T(1024)}, f32[1536]{0:T(1024)S(1)}, u32[]{:S(2)}) copy-start(f32[1536]{0:T(1024)S(1)} %get-tuple-element.64) | copy-start | bytes 18436
  50.2 17.1 %copy-start.2 = (bf16[2,256,1536]{1,2,0:T(8,128)(2,1)}, bf16[2,256,1536]{1,2,0:T(8,128)(2,1)S(1)}, u32[]{:S(2)}) copy-start(bf16[2,256,1536]{1,2,0:T(8,128)(2,1)S(1)} %multiply_convert_fusion.2) | copy-start | bytes 4718596
  55.3 14.0 %copy-start.10 = (f32[2,256,64]{1,2,0:T(8,128)}, f32[2,256,64]{1,2,0:T(8,128)S(1)}, u32[]{:S(2)}) copy-start(f32[2,256,64]{1,2,0:T(8,128)S(1)} %get-tuple-element.97) | copy-start | bytes 393220
  55.3 14.0 %copy-start.15 = (f32[2,256,64]{1,2,0:T(8,128)}, f32[2,256,64]{1,2,0:T(8,128)S(1)}, u32[]{:S(2)}) copy-start(f32[2,256,64]{1,2,0:T(8,128)S(1)} %get-tuple-element.94) | copy-start | bytes 393220
  69.4 4.1 copy-start.16
  69.4 4.1 copy-start.18
  69.4 4.1 copy-start.14
  88.3 94.3 %all-gather.14.cloned.1.call-start = ((), (), s32[]{:S(2)}) async-start(), calls=%async_computation.20 | async-start | bytes 2949120 | tf_op jit(solution)/shard_map/all_gather | solution.py:99
  88.9 139.4 %all-gather.12.cloned.1.call-start = ((), (), s32[]{:S(2)}) async-start(), calls=%async_computation.19 | async-start | bytes 4718592 | tf_op jit(solution)/shard_map/all_gather | solution.py:170
  135.2 144.9 %all-gather.16.cloned.1.call-start = ((), (), s32[]{:S(2)}) async-start(), calls=%async_computation.21 | async-start | bytes 2949120 | tf_op jit(solution)/shard_map/all_gather | solution.py:99
  135.8 189.6 %all-gather.20.cloned.1.call-start = ((), (), s32[]{:S(2)}) async-start(), calls=%async_computation.24 | async-start | bytes 4718592 | tf_op jit(solution)/shard_map/all_gather | solution.py:170
  136.5 240.8 %all-gather.18.cloned.1.call-start = ((), (), s32[]{:S(2)}) async-start(), calls=%async_computation.22 | async-start | bytes 2949120 | tf_op jit(solution)/shard_map/all_gather | solution.py:99
  137.3 273.1 %reduce-scatter.49.cloned.1.call-start = ((), (), s32[]{:S(2)}) async-start(), calls=%async_computation.34 | async-start | bytes 393216
  399.8 90.8 %reduce-scatter.33.cloned.1.call-start = ((), (), s32[]{:S(2)}) async-start(), calls=%async_computation.25 | async-start | bytes 4718592 | tf_op jit(solution)/shard_map/reduce_scatter | solution.py:204
  429.8 4.8 copy-start.25
  434.6 6.3 copy-start.45
  447.9 42.7 %copy-start.26 = (f32[512,8]{0,1:T(8,128)S(1)}, f32[512,8]{0,1:T(8,128)}, u32[]{:S(2)}) copy-start(f32[512,8]{0,1:T(8,128)} %copy-done.25) | copy-start | bytes 49156
  448.0 87.9 %all-reduce.8.cloned.1.call-start = ((), (), s32[]{:S(2)}) async-start(), calls=%async_computation.26 | async-start | bytes 3145728 | tf_op jit(solution)/shard_map/psum | solution.py:205
  490.6 78.5 %reduce-scatter.35.cloned.1.call-start = ((), (), s32[]{:S(2)}) async-start(), calls=%async_computation.27 | async-start | bytes 786432 | tf_op jit(solution)/shard_map/reduce_scatter | solution.py:240
  492.0 47.2 %copy-start.37 = (f32[512]{0:T(512)S(1)}, f32[512]{0:T(512)}, u32[]{:S(2)}) copy-start(f32[512]{0:T(512)} %copy-done.36) | copy-start | bytes 6148
  492.0 47.2 %copy-start.30 = (f32[1536]{0:T(1024)S(1)}, f32[1536]{0:T(1024)}, u32[]{:S(2)}) copy-start(f32[1536]{0:T(1024)} %copy-done.29) | copy-start | bytes 18436
  492.0 47.2 %copy-start.34 = (f32[512]{0:T(512)S(1)}, f32[512]{0:T(512)}, u32[]{:S(2)}) copy-start(f32[512]{0:T(512)} %copy-done.33) | copy-start | bytes 6148
  541.7 5.8 copy-start.43
  554.4 61.0 %reduce-scatter.31.cloned.1.call-start = ((), (), s32[]{:S(2)}) async-start(), calls=%async_computation.23 | async-start | bytes 4718592 | tf_op jit(solution)/shard_map/reduce_scatter | solution.py:204
  561.1 125.3 %all-reduce.10.cloned.1.call-start = ((), (), s32[]{:S(2)}) async-start(), calls=%async_computation.41 | async-start | bytes 6291456 | tf_op jit(solution)/shard_map/psum | solution.py:205
  574.3 6.0 collective-permute-start
  615.4 4.1 copy-start.31
  615.4 70.9 %copy-start.28 = (f32[1536]{0:T(1024)S(1)}, f32[1536]{0:T(1024)}, u32[]{:S(2)}) copy-start(f32[1536]{0:T(1024)} %copy-done.27) | copy-start | bytes 18436
  615.5 120.9 %reduce-scatter.43.cloned.1.call-start = ((), (), s32[]{:S(2)}) async-start(), calls=%async_computation.31 | async-start | bytes 1966080 | tf_op jit(solution)/shard_map/reduce_scatter | solution.py:274
  618.3 126.4 %reduce-scatter.37.cloned.1.call-start = ((), (), s32[]{:S(2)}) async-start(), calls=%async_computation.28 | async-start | bytes 122880 | tf_op jit(solution)/shard_map/reduce_scatter | solution.py:274
  686.3 3.9 copy-start.24
  690.9 84.0 %reduce-scatter.53.cloned.1.call-start = ((), (), s32[]{:S(2)}) async-start(), calls=%async_computation.36 | async-start | bytes 1474560
  697.1 126.9 %reduce-scatter.59.cloned.1.call-start = ((), (), s32[]{:S(2)}) async-start(), calls=%async_computation.39 | async-start | bytes 2949120
  707.8 166.2 %reduce-scatter.57.cloned.1.call-start = ((), (), s32[]{:S(2)}) async-start(), calls=%async_computation.38 | async-start | bytes 2949120
  718.6 205.1 %reduce-scatter.61.cloned.1.call-start = ((), (), s32[]{:S(2)}) async-start(), calls=%async_computation.40 | async-start | bytes 2949120
  729.6 225.8 %reduce-scatter.39.cloned.1.call-start = ((), (), s32[]{:S(2)}) async-start(), calls=%async_computation.29 | async-start | bytes 1474560 | tf_op jit(solution)/shard_map/reduce_scatter | solution.py:274
  736.2 233.4 %reduce-scatter.45.cloned.1.call-start = ((), (), s32[]{:S(2)}) async-start(), calls=%async_computation.32 | async-start | bytes 589824 | tf_op jit(solution)/shard_map/reduce_scatter | solution.py:277
  737.0 246.5 %reduce-scatter.51.cloned.1.call-start = ((), (), s32[]{:S(2)}) async-start(), calls=%async_computation.35 | async-start | bytes 294912
  746.2 251.4 %reduce-scatter.55.cloned.1.call-start = ((), (), s32[]{:S(2)}) async-start(), calls=%async_computation.37 | async-start | bytes 442368
  775.0 237.0 %reduce-scatter.41.cloned.1.call-start = ((), (), s32[]{:S(2)}) async-start(), calls=%async_computation.30 | async-start | bytes 442368 | tf_op jit(solution)/shard_map/reduce_scatter | solution.py:277
  923.8 31.8 %copy-start.35 = (f32[1,2,2,128]{3,1,2,0:T(2,128)S(1)}, f32[1,2,2,128]{3,1,2,0:T(2,128)}, u32[]{:S(2)}) copy-start(f32[1,2,2,128]{3,1,2,0:T(2,128)} %copy.186) | copy-start | bytes 6148
  923.8 31.8 %copy-start.40 = (f32[512]{0:T(512)S(1)}, f32[512]{0:T(512)}, u32[]{:S(2)}) copy-start(f32[512]{0:T(512)} %get-tuple-element.63) | copy-start | bytes 6148
  925.9 4.4 copy-start.9
  955.5 79.6 %reduce-scatter.47.cloned.1.call-start = ((), (), s32[]{:S(2)}) async-start(), calls=%async_computation.33 | async-start | bytes 491520 | tf_op jit(solution)/shard_map/reduce_scatter | solution.py:290
  (26 other events, 50.5 us)
Sparse Core Ops, SparseCore 0:
  9.6 44.1 all-gather.7
  55.3 29.5 all-gather.9
  88.5 42.2 all-reduce.5
  132.2 50.3 all-gather.13
  184.6 43.6 all-gather.11
  229.7 50.3 all-gather.15
  281.6 43.6 all-gather.19
  326.9 50.3 all-gather.17
  399.9 10.3 reduce-scatter.48
  448.1 42.4 reduce-scatter.32
  493.0 42.8 all-reduce.7
  554.5 14.6 reduce-scatter.34
  572.0 43.3 reduce-scatter.30
  617.7 68.6 all-reduce.9
  688.5 35.3 reduce-scatter.42
  726.6 18.0 reduce-scatter.36
  747.5 27.4 reduce-scatter.52
  777.2 46.7 reduce-scatter.58
  826.4 47.5 reduce-scatter.56
  876.2 47.5 reduce-scatter.60
  926.8 28.6 reduce-scatter.38
  957.8 11.8 reduce-scatter.44
  972.5 10.9 reduce-scatter.50
  985.5 12.0 reduce-scatter.54
  999.8 12.0 reduce-scatter.40
  1014.3 20.8 reduce-scatter.46

commit v2 on v1

--- a/solution.py
+++ b/solution.py
@@ -1,6 +1,12 @@
+import functools
+import math
+
 import jax
 import jax.numpy as jnp
+import numpy as np
 from jax import lax
+from jax.experimental import pallas as pl
+from jax.experimental.pallas import tpu as pltpu
 from jax.sharding import PartitionSpec as P
 
 QUERY_HEADS = 12
@@ -65,7 +71,7 @@
     return jnp.concatenate([front * cosine - back * sine, back * cosine + front * sine], -1)
 
 
-def shards(
+def general_shards(
     tokens,
     cotangent,
     seg_start,
@@ -304,6 +310,1678 @@
     )
 
 
+MESH = pl.DeviceIdType.MESH
+NT = (((1,), (1,)), ((), ()))
+NN = (((1,), (0,)), ((), ()))
+TN = (((0,), (0,)), ((), ()))
+CHUNKS = 4
+
+
+def mm(left, right, dims=NN):
+    return lax.dot_general(left, right, dims, preferred_element_type=F32)
+
+
+class Place:
+    def __init__(self):
+        self.z = lax.axis_index("dp")
+        self.x = lax.axis_index("expert")
+        self.t = lax.axis_index("tensor")
+        self.y = self.t // 2
+        self.c = self.t % 2
+
+    def at_z(self, z):
+        return (z, self.x, self.t)
+
+    def x_peer(self):
+        return (self.z, 1 - self.x, self.t)
+
+    def y_peer(self):
+        return (self.z, self.x, (self.t + 2) % 4)
+
+    def core_peer(self):
+        return (self.z, self.x, self.t + 1 - 2 * self.c)
+
+
+def remote(src, dst, sems, at, device):
+    return pltpu.make_async_remote_copy(
+        src_ref=src,
+        dst_ref=dst,
+        send_sem=sems.at[0, at],
+        recv_sem=sems.at[1, at],
+        device_id=device,
+        device_id_type=MESH,
+    )
+
+
+def greet(devices):
+    barrier = pltpu.get_barrier_semaphore()
+    for device in devices:
+        pl.semaphore_signal(barrier, inc=1, device_id=device, device_id_type=MESH)
+    pl.semaphore_wait(barrier, len(devices))
+
+
+def tree_tables(starts, parents, tree, first, rows, length, frequency):
+    count = starts.shape[1]
+    place = first + lax.broadcasted_iota(jnp.int32, (rows, HEAD_SIZE), 0)
+    start = [starts[tree, k] for k in range(count)]
+    parent = [parents[tree, k] for k in range(count)]
+    size = [(start[k + 1] if k + 1 < count else length) - start[k] for k in range(count)]
+
+    def pick(table, at):
+        total = jnp.zeros_like(at)
+        for k in range(count):
+            total = total + jnp.where(at == k, table[k], 0)
+        return total
+
+    def segment_of(at):
+        total = jnp.zeros_like(at)
+        for k in range(1, count):
+            total = total + jnp.where(at >= start[k], 1, 0)
+        return total
+
+    segment = segment_of(place)
+    above = pick(parent, segment)
+    further = pick(parent, above)
+    depth = (
+        place
+        - pick(start, segment)
+        + jnp.where(segment != 0, pick(size, above), 0)
+        + jnp.where(above != 0, pick(size, further), 0)
+    )
+    turning = depth.astype(F32) * frequency
+    lane = lax.broadcasted_iota(jnp.int32, (rows, HEAD_SIZE), 1)
+    cosine = jnp.cos(turning)
+    sine = jnp.sin(turning)
+    sine = jnp.where(lane < HEAD_SIZE // 2, -sine, sine)
+    key_place = lax.broadcasted_iota(jnp.int32, (8, length), 1)
+    key_segment = jnp.broadcast_to(segment_of(key_place)[:1], (rows, length))
+    key_place = jnp.broadcast_to(key_place[:1], (rows, length))
+    wide = length // HEAD_SIZE
+
+    def widen(array):
+        return jnp.concatenate([array] * wide, 1)
+
+    visible = (
+        (key_segment == widen(segment))
+        | (key_segment == widen(above))
+        | (key_segment == widen(further))
+    ) & (key_place <= widen(place))
+    return jnp.where(visible, 1.0, 0.0), cosine, sine
+
+
+def turn(head, cosine, sine):
+    return head * cosine + pltpu.roll(head, HEAD_SIZE // 2, 1) * sine
+
+
+def attend_kernel(
+    starts,
+    parents,
+    frequency,
+    tokens,
+    cotangent,
+    routes,
+    w_query,
+    w_key,
+    w_value,
+    w_output,
+    small,
+    hid_one,
+    wqkv,
+    wout,
+    smalls,
+    queries,
+    keys,
+    values,
+    probs,
+    context,
+    tables,
+    after,
+    hid_two,
+    ups,
+    mixes,
+    mask,
+    part,
+    core_in,
+    y_out,
+    y_in,
+    local_sem,
+    small_sem,
+    up_sem,
+    dn_sem,
+    side_sem,
+    up_sem2,
+    dn_sem2,
+    side_sem2,
+    kv_sem,
+    cot_x_sem,
+    cot_c_sem,
+    cot_f_sem,
+    core_sem,
+    y_sem,
+    hx_sem,
+    hc_sem,
+    hf_sem,
+    mix_sem,
+):
+    me = Place()
+    z, x, y, c = me.z, me.x, me.y, me.c
+    deep = wqkv.shape[0]
+    trees, rows, width = tokens.shape
+    length = keys.shape[1]
+    shard = wqkv.shape[1]
+    half = shard // 2
+    heads = queries.shape[1]
+    step = rows // CHUNKS
+    inv_root = HEAD_SIZE ** (-0.5)
+
+    local = [
+        pltpu.make_async_copy(w_query, wqkv.at[z, :, pl.ds(0, heads * HEAD_SIZE)], local_sem.at[0]),
+        pltpu.make_async_copy(
+            w_key.at[:, pl.ds(pl.multiple_of(y * HEAD_SIZE, HEAD_SIZE), HEAD_SIZE)],
+            wqkv.at[z, :, pl.ds(heads * HEAD_SIZE, HEAD_SIZE)],
+            local_sem.at[1],
+        ),
+        pltpu.make_async_copy(
+            w_value.at[:, pl.ds(pl.multiple_of(y * HEAD_SIZE, HEAD_SIZE), HEAD_SIZE)],
+            wqkv.at[z, :, pl.ds((heads + 1) * HEAD_SIZE, HEAD_SIZE)],
+            local_sem.at[2],
+        ),
+        pltpu.make_async_copy(w_output, wout.at[z], local_sem.at[3]),
+        pltpu.make_async_copy(small, smalls.at[z], local_sem.at[4]),
+        pltpu.make_async_copy(cotangent.at[0], ups.at[0, x], local_sem.at[5]),
+        pltpu.make_async_copy(cotangent.at[1], ups.at[1, x], local_sem.at[6]),
+    ]
+    for copy in local:
+        copy.start()
+    others = [me.at_z((z + k) % deep) for k in range(1, deep)]
+    greet(others + [me.x_peer(), me.y_peer(), me.core_peer()])
+    for copy in local:
+        copy.wait()
+
+    small_out = [
+        remote(small, smalls.at[z], small_sem, k - 1, me.at_z((z + k) % deep))
+        for k in range(1, deep)
+    ]
+    for copy in small_out:
+        copy.start()
+
+    def relay(buffer, ups_sem, dns_sem, sides_sem):
+        def piece(source, by):
+            return buffer.at[source, pl.ds(pl.multiple_of(by * half, half), half)]
+
+        def hop_up(source, at):
+            return remote(piece(source, x), piece(source, x), ups_sem, at, me.at_z(jnp.minimum(z + 1, deep - 1)))
+
+        def hop_dn(source, at):
+            return remote(piece(source, x), piece(source, x), dns_sem, at, me.at_z(jnp.maximum(z - 1, 0)))
+
+        def hop_side(source, at):
+            return remote(piece(source, x), piece(source, x), sides_sem, at, me.x_peer())
+
+        def begin():
+            @pl.when(z < deep - 1)
+            def _():
+                hop_up(z, 0).start()
+
+            @pl.when(z > 0)
+            def _():
+                hop_dn(z, 0).start()
+
+        def step_on(s):
+            @pl.when(z - 1 - s >= 0)
+            def _():
+                source = z - 1 - s
+                hop_up(source, s).wait_recv()
+
+                @pl.when(z < deep - 1)
+                def _():
+                    hop_up(source, s + 1).start()
+
+                hop_side(source, s).start()
+
+            @pl.when(z + 1 + s < deep)
+            def _():
+                source = z + 1 + s
+                hop_dn(source, s).wait_recv()
+
+                @pl.when(z > 0)
+                def _():
+                    hop_dn(source, s + 1).start()
+
+                hop_side(source, deep - 1 + s).start()
+
+        def finish():
+            for s in range(deep - 1):
+                @pl.when(z - 1 - s >= 0)
+                def _():
+                    source = z - 1 - s
+                    copy = remote(piece(source, x), piece(source, 1 - x), sides_sem, s, me.x_peer())
+                    copy.wait_recv()
+
+                @pl.when(z + 1 + s < deep)
+                def _():
+                    source = z + 1 + s
+                    copy = remote(
+                        piece(source, x), piece(source, 1 - x), sides_sem, deep - 1 + s, me.x_peer()
+                    )
+                    copy.wait_recv()
+
+        def drain():
+            for s in range(deep):
+                @pl.when((z - s >= 0) & (z < deep - 1))
+                def _():
+                    hop_up(z - s, s).wait_send()
+
+                @pl.when((z + s < deep) & (z > 0))
+                def _():
+                    hop_dn(z + s, s).wait_send()
+
+            for s in range(deep - 1):
+                @pl.when(z - 1 - s >= 0)
+                def _():
+                    hop_side(z - 1 - s, s).wait_send()
+
+                @pl.when(z + 1 + s < deep)
+                def _():
+                    hop_side(z + 1 + s, deep - 1 + s).wait_send()
+
+        return begin, step_on, finish, drain
+
+    begin1, step1, finish1, drain1 = relay(wqkv, up_sem, dn_sem, side_sem)
+    begin2, step2, finish2, drain2 = relay(wout, up_sem2, dn_sem2, side_sem2)
+    begin1()
+
+    for tree in range(trees):
+        seen, cosine, sine = tree_tables(
+            starts, parents, tree, x * rows, rows, length, frequency[:1, :]
+        )
+        mask[tree] = seen
+        tables[0, tree] = cosine
+        tables[1, tree] = sine
+    step1(0)
+    step1(1)
+    for k in range(1, deep):
+        source = (z + deep - k) % deep
+        remote(small, smalls.at[source], small_sem, k - 1, me.at_z(source)).wait_recv()
+    gain_one = jnp.concatenate([smalls[k, :1, :] for k in range(deep)], 1).astype(F32)
+    gain_two = jnp.concatenate([smalls[k, 1:2, :] for k in range(deep)], 1).astype(F32)
+    router = jnp.concatenate([smalls[k, 8:, :] for k in range(deep)], 1)
+
+    def first_norm(at, carry):
+        tree, row = at // CHUNKS, pl.multiple_of(at % CHUNKS * step, step)
+        value = tokens[tree, pl.ds(row, step), :].astype(F32)
+        factor = lax.rsqrt(jnp.mean(value * value, -1, keepdims=True) + EPS)
+        hid_one[tree, pl.ds(row, step), :] = (value * factor * gain_one).astype(BF16)
+        return carry
+
+    lax.fori_loop(0, trees * CHUNKS, first_norm, 0)
+    step1(2)
+    begin2()
+    finish1()
+
+    for tree in range(trees):
+        total = jnp.zeros((rows, wqkv.shape[2]), F32)
+        for k in range(deep):
+            total = total + mm(hid_one[tree, :, pl.ds(k * shard, shard)], wqkv[k])
+        cosine, sine = tables[0, tree], tables[1, tree]
+        for head in range(heads):
+            part_q = total[:, head * HEAD_SIZE : (head + 1) * HEAD_SIZE]
+            queries[tree, head] = turn(part_q, cosine, sine).astype(BF16)
+        part_k = total[:, heads * HEAD_SIZE : (heads + 1) * HEAD_SIZE]
+        own = pl.ds(pl.multiple_of(x * rows, rows), rows)
+        keys[tree, own, :] = turn(part_k, cosine, sine).astype(BF16)
+        values[tree, own, :] = total[:, (heads + 1) * HEAD_SIZE :].astype(BF16)
+        for which, array in enumerate((keys, values)):
+            remote(
+                array.at[tree, own], array.at[tree, own], kv_sem, 2 * tree + which, me.x_peer()
+            ).start()
+    step2(0)
+    away = pl.ds(pl.multiple_of((1 - x) * rows, rows), rows)
+    for tree in range(trees):
+        for which, array in enumerate((keys, values)):
+            remote(
+                array.at[tree, away], array.at[tree, away], kv_sem, 2 * tree + which, me.x_peer()
+            ).wait_recv()
+
+    def attend(tree):
+        def one(head, carry):
+            score = mm(queries[tree, head], keys[tree], NT) * inv_root
+            score = jnp.where(mask[tree] > 0.5, score, NEG)
+            top = jnp.max(score, -1, keepdims=True)
+            raised = jnp.exp(score - top)
+            prob = raised / jnp.sum(raised, -1, keepdims=True)
+            prob = prob.astype(BF16)
+            probs[tree, head] = prob
+            seen = mm(prob, values[tree])
+            context[tree, head] = seen.astype(BF16)
+            return carry
+
+        lax.fori_loop(0, heads, one, 0)
+
+    attend(0)
+    step2(1)
+    attend(1)
+    step2(2)
+    finish2()
+
+    own_up = remote(cotangent.at[c], ups.at[c, x], cot_x_sem, 0, me.x_peer())
+    own_up.start()
+
+    def project(tree, row):
+        pieces = []
+        for k in range(deep):
+            piece = jnp.zeros((step, shard), F32)
+            for head in range(heads):
+                piece = piece + mm(
+                    context[tree, head, pl.ds(row, step), :],
+                    wout[k, pl.ds(head * HEAD_SIZE, HEAD_SIZE), :],
+                )
+            pieces.append(piece)
+        return pieces
+
+    def spread(k):
+        return pl.ds(k * shard, shard)
+
+    def away_rows(chunk):
+        return part.at[pl.ds(chunk * step, step)]
+
+    def core_copy(chunk):
+        return remote(
+            away_rows(chunk), core_in.at[pl.ds(chunk * step, step)], core_sem, chunk, me.core_peer()
+        )
+
+    for chunk in range(CHUNKS):
+        for k, piece in enumerate(project(1 - c, chunk * step)):
+            part[pl.ds(chunk * step, step), spread(k)] = piece.astype(BF16)
+        core_copy(chunk).start()
+
+    def y_copy(chunk):
+        at = pl.ds(chunk * step, step)
+        return remote(y_out.at[at], y_in.at[at], y_sem, chunk, me.y_peer())
+
+    for chunk in range(CHUNKS):
+        pieces = project(c, chunk * step)
+        core_copy(chunk).wait_recv()
+        for k, piece in enumerate(pieces):
+            both = piece.astype(BF16).astype(F32) + core_in[
+                pl.ds(chunk * step, step), spread(k)
+            ].astype(F32)
+            y_out[pl.ds(chunk * step, step), spread(k)] = both.astype(BF16)
+        y_copy(chunk).start()
+
+    def two_copy(which, sems, chunk, device):
+        at = hid_two.at[c, which, pl.ds(chunk * step, step)]
+        return remote(at, at, sems, chunk, device)
+
+    for chunk in range(CHUNKS):
+        y_copy(chunk).wait_recv()
+        at = pl.ds(chunk * step, step)
+        value = tokens[c, at, :].astype(F32) + (y_out[at, :].astype(F32) + y_in[at, :].astype(F32))
+        after[at, :] = value
+        factor = lax.rsqrt(jnp.mean(value * value, -1, keepdims=True) + EPS)
+        hid_two[c, x, at, :] = (value * factor * gain_two).astype(BF16)
+        two_copy(x, hx_sem, chunk, me.x_peer()).start()
+        two_copy(x, hc_sem, chunk, me.core_peer()).start()
+
+    logits = mm(router, hid_two[c, x], NT)
+    expert = lax.broadcasted_iota(jnp.int32, logits.shape, 0)
+    chosen = expert < 0
+    for k in range(routes.shape[1]):
+        chosen = chosen | (expert == routes[c, k : k + 1, :])
+    logits = jnp.where(chosen, logits, NEG)
+    raised = jnp.where(chosen, jnp.exp(logits - jnp.max(logits, 0, keepdims=True)), 0.0)
+    mixes[c, x] = raised / jnp.sum(raised, 0, keepdims=True)
+    own_mix = mixes.at[c, x]
+    mix_x = remote(own_mix, own_mix, mix_sem, 0, me.x_peer())
+    mix_c = remote(own_mix, own_mix, mix_sem, 1, me.core_peer())
+    mix_x.start()
+    mix_c.start()
+
+    up_away = ups.at[c, 1 - x]
+    remote(cotangent.at[c], up_away, cot_x_sem, 0, me.x_peer()).wait_recv()
+    up_on = remote(up_away, up_away, cot_f_sem, 0, me.core_peer())
+    up_on.start()
+    for chunk in range(CHUNKS):
+        two_copy(1 - x, hx_sem, chunk, me.x_peer()).wait_recv()
+        two_copy(1 - x, hf_sem, chunk, me.core_peer()).start()
+    mix_away = mixes.at[c, 1 - x]
+    remote(mix_away, mix_away, mix_sem, 0, me.x_peer()).wait_recv()
+    mix_on = remote(mix_away, mix_away, mix_sem, 2, me.core_peer())
+    mix_on.start()
+
+    up_peer = ups.at[1 - c, 1 - x]
+    remote(up_peer, up_peer, cot_f_sem, 0, me.core_peer()).wait_recv()
+    for chunk in range(CHUNKS):
+        for which, sems in ((x, hc_sem), (1 - x, hf_sem)):
+            at = hid_two.at[1 - c, which, pl.ds(chunk * step, step)]
+            remote(at, at, sems, chunk, me.core_peer()).wait_recv()
+    for which, number in ((x, 1), (1 - x, 2)):
+        at = mixes.at[1 - c, which]
+        remote(at, at, mix_sem, number, me.core_peer()).wait_recv()
+
+    for copy in small_out + [own_up, up_on, mix_x, mix_c, mix_on]:
+        copy.wait_send()
+    drain1()
+    drain2()
+    for tree in range(trees):
+        for which, array in enumerate((keys, values)):
+            own = pl.ds(pl.multiple_of(x * rows, rows), rows)
+            remote(
+                array.at[tree, own], array.at[tree, own], kv_sem, 2 * tree + which, me.x_peer()
+            ).wait_send()
+    for chunk in range(CHUNKS):
+        core_copy(chunk).wait_send()
+        y_copy(chunk).wait_send()
+        two_copy(x, hx_sem, chunk, me.x_peer()).wait_send()
+        two_copy(x, hc_sem, chunk, me.core_peer()).wait_send()
+        two_copy(1 - x, hf_sem, chunk, me.core_peer()).wait_send()
+
+
+def sems(count):
+    return pltpu.SemaphoreType.DMA((2, count))
+
+
+def attend_call(seg_start, seg_parent, tokens, cotangent, routes, w_query, w_key, w_value, w_output, small, deep):
+    trees, rows, width = tokens.shape
+    shard, mine = w_query.shape
+    heads = mine // HEAD_SIZE
+    length = rows * 2
+    experts = small.shape[0] - 8
+    half = HEAD_SIZE // 2
+    frequency = ROPE_BASE ** (-2.0 * np.arange(half, dtype=np.float32) / np.float32(HEAD_SIZE))
+    frequency = jnp.asarray(np.tile(np.concatenate([frequency] * 2)[None], (8, 1)).astype(np.float32))
+    vmem = pl.BlockSpec(memory_space=pltpu.VMEM)
+    smem = pl.BlockSpec(memory_space=pltpu.SMEM)
+
+    def out(shape, dtype):
+        return jax.ShapeDtypeStruct(shape, dtype)
+
+    return pl.pallas_call(
+        attend_kernel,
+        out_shape=(
+            out((trees, rows, width), BF16),
+            out((deep, shard, mine + 2 * HEAD_SIZE), BF16),
+            out((deep, mine, shard), BF16),
+            out((deep,) + small.shape, BF16),
+            out((trees, heads, rows, HEAD_SIZE), BF16),
+            out((trees, length, HEAD_SIZE), BF16),
+            out((trees, length, HEAD_SIZE), BF16),
+            out((trees, heads, rows, length), BF16),
+            out((trees, heads, rows, HEAD_SIZE), BF16),
+            out((2, trees, rows, HEAD_SIZE), F32),
+            out((rows, width), F32),
+            out((trees, 2, rows, width), BF16),
+            out((trees, 2, rows, width), BF16),
+            out((trees, 2, experts, rows), F32),
+        ),
+        in_specs=[smem, smem] + [vmem] * 9,
+        out_specs=[vmem] * 14,
+        scratch_shapes=[
+            pltpu.VMEM((trees, rows, length), F32),
+            pltpu.VMEM((rows, width), BF16),
+            pltpu.VMEM((rows, width), BF16),
+            pltpu.VMEM((rows, width), BF16),
+            pltpu.VMEM((rows, width), BF16),
+            pltpu.SemaphoreType.DMA((7,)),
+            sems(deep - 1),
+            sems(deep),
+            sems(deep),
+            sems(2 * deep - 2),
+            sems(deep),
+            sems(deep),
+            sems(2 * deep - 2),
+            sems(2 * trees),
+            sems(1),
+            sems(1),
+            sems(1),
+            sems(CHUNKS),
+            sems(CHUNKS),
+            sems(CHUNKS),
+            sems(CHUNKS),
+            sems(CHUNKS),
+            sems(3),
+        ],
+        compiler_params=pltpu.CompilerParams(
+            collective_id=0, has_side_effects=True, vmem_limit_bytes=60 * 2**20
+        ),
+        name="attend",
+    )(seg_start, seg_parent, frequency, tokens, cotangent, routes, w_query, w_key, w_value, w_output, small)
+
+
+ROOT_2_PI = math.sqrt(2.0 / math.pi)
+CUBIC = 0.044715
+
+
+def expert_acts(mats, hid, ups, mixes, acts, gates, group, held, x, quarter):
+    blocks, rows = mixes.shape[0], mixes.shape[2]
+    units = held * quarter
+    local = mixes.shape[1] // 2
+    base = group * held
+
+    def mat(kind):
+        return mats[pl.ds((3 * group + kind) * units, units), :]
+
+    def block(at, carry):
+        first = pl.multiple_of(at * rows, rows)
+        tokens = pl.ds(first, rows)
+        hidden_rows = hid[tokens, :]
+        pre_gate = mm(mat(0), hidden_rows, NT)
+        pre_up = mm(mat(1), hidden_rows, NT)
+        back = mm(mat(2), ups[tokens, :], NT)
+        own = jnp.where(x == 0, mixes[at, :local, :], mixes[at, local:, :])
+        weight = jnp.concatenate(
+            [
+                jnp.broadcast_to(own[base + i : base + i + 1, :], (quarter, rows))
+                for i in range(held)
+            ],
+            0,
+        )
+        square = pre_gate * pre_gate
+        bent = jnp.tanh(ROOT_2_PI * pre_gate * (1.0 + CUBIC * square))
+        slope = 0.5 * (1.0 + bent)
+        active = pre_gate * slope
+        rise = slope + 0.5 * pre_gate * (1.0 - bent * bent) * ROOT_2_PI * (
+            1.0 + 3.0 * CUBIC * square
+        )
+        hidden = active * pre_up
+        share = hidden * back
+        for i in range(held):
+            gates[pl.ds(i, 1), tokens] = jnp.sum(
+                share[i * quarter : (i + 1) * quarter], 0, keepdims=True
+            )
+        back = weight * back
+        acts[3 * group + 0, :, tokens] = (back * pre_up * rise).astype(BF16)
+        acts[3 * group + 1, :, tokens] = (back * active).astype(BF16)
+        acts[3 * group + 2, :, tokens] = (weight * hidden).astype(BF16)
+        return carry
+
+    lax.fori_loop(0, blocks, block, 0)
+
+
+class Chain:
+    def __init__(self, me, stage, from_dn, from_up, dn_sems, up_sems, tile):
+        self.me, self.stage, self.tile = me, stage, tile
+        self.from_dn, self.from_up = from_dn, from_up
+        self.dn_sems, self.up_sems = dn_sems, up_sems
+        self.deep, self.count = stage.shape[0], stage.shape[1]
+
+    def rise(self, target, m):
+        up = jnp.minimum(self.me.z + 1, self.deep - 1)
+        return remote(
+            self.stage.at[target, m],
+            self.from_dn.at[target - 1, m],
+            self.dn_sems,
+            (target - 1) * self.count + m,
+            self.me.at_z(up),
+        )
+
+    def fall(self, target, m):
+        down = jnp.maximum(self.me.z - 1, 0)
+        return remote(
+            self.stage.at[target, m],
+            self.from_up.at[target, m],
+            self.up_sems,
+            target * self.count + m,
+            self.me.at_z(down),
+        )
+
+    def add(self, target, m, landed):
+        def step(at, carry):
+            rows = pl.ds(pl.multiple_of(at * self.tile, self.tile), self.tile)
+            total = self.stage[target, m, rows, :].astype(F32) + landed[rows, :].astype(F32)
+            self.stage[target, m, rows, :] = total.astype(BF16)
+            return carry
+
+        lax.fori_loop(0, self.stage.shape[2] // self.tile, step, 0)
+
+    def begin(self, m):
+        for k in range(self.deep - 1):
+
+            @pl.when(self.me.z == 0)
+            def _():
+                self.rise(self.deep - 1 - k, m).start()
+
+            @pl.when(self.me.z == self.deep - 1)
+            def _():
+                self.fall(k, m).start()
+
+    def advance(self, m, steps=None):
+        z = self.me.z
+        for k in range(self.deep - 1) if steps is None else steps:
+            far, near = self.deep - 1 - k, k
+
+            @pl.when((z >= 1) & (z < far))
+            def _():
+                self.rise(far, m).wait_recv()
+                self.add(far, m, self.from_dn.at[far - 1, m])
+                self.rise(far, m).start()
+
+            @pl.when((z < self.deep - 1) & (z > near))
+            def _():
+                self.fall(near, m).wait_recv()
+                self.add(near, m, self.from_up.at[near, m])
+                self.fall(near, m).start()
+
+    def finish(self, m, write):
+        z = self.me.z
+
+        @pl.when(z > 0)
+        def _():
+            self.rise(jnp.maximum(z, 1), m).wait_recv()
+
+        @pl.when(z < self.deep - 1)
+        def _():
+            self.fall(jnp.minimum(z, self.deep - 2), m).wait_recv()
+
+        below, above = jnp.maximum(z - 1, 0), jnp.minimum(z, self.deep - 2)
+
+        def step(at, carry):
+            rows = pl.ds(pl.multiple_of(at * self.tile, self.tile), self.tile)
+            own = self.stage[z, m, rows, :].astype(F32)
+            lower = self.from_dn[below, m, rows, :].astype(F32)
+            upper = self.from_up[above, m, rows, :].astype(F32)
+            total = own + jnp.where(z > 0, lower, 0.0) + jnp.where(z < self.deep - 1, upper, 0.0)
+            write(rows, total)
+            return carry
+
+        lax.fori_loop(0, self.stage.shape[2] // self.tile, step, 0)
+
+    def drain(self, m):
+        z = self.me.z
+        for k in range(self.deep - 1):
+            far, near = self.deep - 1 - k, k
+
+            @pl.when(z < far)
+            def _():
+                self.rise(far, m).wait_send()
+
+            @pl.when(z > near)
+            def _():
+                self.fall(near, m).wait_send()
+
+
+def expert_grads(which, group, acts, rows_of, stage):
+    columns = stage.shape[3]
+
+    def shard(k, carry):
+        at = pl.ds(pl.multiple_of(k * columns, columns), columns)
+        stage[k, which] = mm(acts[3 * group + which], rows_of[:, at]).astype(BF16)
+        return carry
+
+    lax.fori_loop(0, stage.shape[0], shard, 0)
+
+
+def experts_kernel(
+    quarter,
+    mats,
+    hid,
+    ups,
+    mixes,
+    acts,
+    gates,
+    grads,
+    stage,
+    from_dn,
+    from_up,
+    dn_sems,
+    up_sems,
+):
+    me = Place()
+    deep = stage.shape[0]
+    greet([me.at_z((me.z + k) % deep) for k in range(1, deep)])
+    chain = Chain(me, stage, from_dn, from_up, dn_sems, up_sems, 64)
+    gates[...] = jnp.zeros_like(gates)
+    expert_acts(mats, hid, ups, mixes, acts, gates, 0, 2, me.x, quarter)
+    for m in range(3):
+        expert_grads(m, 0, acts, ups if m == 2 else hid, stage)
+        chain.begin(m)
+
+    for m in range(3):
+        chain.advance(m)
+
+    for m in range(3):
+
+        def write(rows, value):
+            grads[m, rows, :] = value
+
+        chain.finish(m, write)
+
+    for m in range(3):
+        chain.drain(m)
+
+
+def experts_call(mats, hid, ups, mixes, deep):
+    units, width = mats.shape[0] // 3, mats.shape[1]
+    tokens = hid.shape[0]
+    columns = width // deep
+    quarter = units // 2
+    vmem = pl.BlockSpec(memory_space=pltpu.VMEM)
+    return pl.pallas_call(
+        functools.partial(experts_kernel, quarter),
+        out_shape=(
+            jax.ShapeDtypeStruct((3, units, tokens), BF16),
+            jax.ShapeDtypeStruct((8, tokens), F32),
+            jax.ShapeDtypeStruct((3, units, columns), F32),
+        ),
+        in_specs=[vmem] * 4,
+        out_specs=[vmem] * 3,
+        scratch_shapes=[
+            pltpu.VMEM((deep, 3, units, columns), BF16),
+            pltpu.VMEM((deep - 1, 3, units, columns), BF16),
+            pltpu.VMEM((deep - 1, 3, units, columns), BF16),
+            sems((deep - 1) * 3),
+            sems((deep - 1) * 3),
+        ],
+        compiler_params=pltpu.CompilerParams(
+            collective_id=1, has_side_effects=True, vmem_limit_bytes=60 * 2**20
+        ),
+        name="experts",
+    )(mats, hid, ups, mixes)
+
+
+class PlaneSum:
+    def __init__(self, me, rows, tile, bufs, landing, sem_set):
+        self.me, self.rows, self.tile = me, rows, tile
+        self.core_out, self.x_out, self.acc, self.y_out = bufs
+        self.core_in, self.x_in, self.y_in = landing
+        self.core_sems, self.x_sems, self.y_sems = sem_set
+        self.tiles = rows // tile
+        self.step = rows // CHUNKS
+        self.per_tile = tile // self.step
+
+    def at(self, number, size):
+        return pl.ds(pl.multiple_of(number * size, size), size)
+
+    def core_copy(self, number):
+        at = self.at(number, self.tile)
+        return remote(
+            self.core_out.at[at], self.core_in.at[at], self.core_sems, number, self.me.core_peer()
+        )
+
+    def x_copy(self, number):
+        at = self.at(number, self.step)
+        return remote(self.x_out.at[at], self.x_in.at[at], self.x_sems, number, self.me.x_peer())
+
+    def y_copy(self, number):
+        at = self.at(number, self.step)
+        return remote(self.y_out.at[at], self.y_in.at[at], self.y_sems, number, self.me.y_peer())
+
+    def first(self, tree, x, number):
+        return pl.multiple_of((tree * 2 + x) * self.rows + number * self.tile, self.tile)
+
+    def outward(self, make):
+        me = self.me
+
+        def one(number, carry):
+            x = jnp.where(number < self.tiles, 1 - me.x, me.x)
+            value = make(self.first(1 - me.c, x, number % self.tiles))
+            self.core_out[self.at(number, self.tile), :] = value.astype(BF16)
+            self.core_copy(number).start()
+            return carry
+
+        lax.fori_loop(0, 2 * self.tiles, one, 0)
+
+    def across(self, make):
+        me = self.me
+
+        def one(number, carry):
+            value = make(self.first(me.c, 1 - me.x, number)).astype(BF16).astype(F32)
+            self.core_copy(number).wait_recv()
+            at = self.at(number, self.tile)
+            self.x_out[at, :] = (value + self.core_in[at, :].astype(F32)).astype(BF16)
+            for k in range(self.per_tile):
+                self.x_copy(number * self.per_tile + k).start()
+            return carry
+
+        lax.fori_loop(0, self.tiles, one, 0)
+
+    def inward(self, make):
+        me = self.me
+
+        def one(number, carry):
+            value = make(self.first(me.c, me.x, number)).astype(BF16).astype(F32)
+            self.core_copy(self.tiles + number).wait_recv()
+            self.acc[self.at(number, self.tile), :] = value + self.core_in[
+                self.at(self.tiles + number, self.tile), :
+            ].astype(F32)
+            return carry
+
+        lax.fori_loop(0, self.tiles, one, 0)
+
+    def pass_on(self):
+        def one(number, carry):
+            at = self.at(number, self.step)
+            self.x_copy(number).wait_recv()
+            self.y_out[at, :] = (self.acc[at, :] + self.x_in[at, :].astype(F32)).astype(BF16)
+            self.y_copy(number).start()
+            return carry
+
+        lax.fori_loop(0, CHUNKS, one, 0)
+
+    def total(self, number):
+        at = self.at(number, self.step)
+        self.y_copy(number).wait_recv()
+        return self.y_out[at, :].astype(F32) + self.y_in[at, :].astype(F32)
+
+    def drain(self):
+        for number in range(2 * self.tiles):
+            self.core_copy(number).wait_send()
+        for number in range(CHUNKS):
+            self.x_copy(number).wait_send()
+            self.y_copy(number).wait_send()
+
+
+def rest_kernel(
+    quarter,
+    mats_a,
+    mats_b,
+    acts_a,
+    gates_a,
+    hid_in,
+    ups_in,
+    mixes,
+    hid_one_in,
+    tokens_in,
+    wqkv_in,
+    wout_in,
+    smalls,
+    queries_in,
+    keys_in,
+    values_in,
+    probs_in,
+    context_in,
+    tables_in,
+    after_in,
+    mixed,
+    d_tokens,
+    grads,
+    d_qo,
+    d_kv,
+    d_small,
+    mats,
+    acts,
+    hid,
+    ups,
+    wqkv,
+    wout,
+    queries,
+    keys,
+    values,
+    probs,
+    context,
+    tables,
+    after,
+    gates_b,
+    gates_out,
+    gates_in,
+    core_out,
+    x_out,
+    acc,
+    y_out,
+    two_core_in,
+    two_x_in,
+    two_y_in,
+    mo_core_in,
+    mo_x_in,
+    mo_y_in,
+    one_core_in,
+    one_y_in,
+    agrad,
+    alow,
+    qlow,
+    kv_out,
+    kv_in,
+    kv_own,
+    kvx_out,
+    kvx_in,
+    kvlow,
+    dkv_out,
+    dkv_in,
+    xs_out,
+    xs_in,
+    stage,
+    from_dn,
+    from_up,
+    stage2,
+    from_dn2,
+    from_up2,
+    small_own,
+    small_core,
+    small_x,
+    small_z,
+    kv_last,
+    load_sem,
+    gate_sem,
+    two_core_sem,
+    two_x_sem,
+    two_y_sem,
+    mo_core_sem,
+    mo_x_sem,
+    mo_y_sem,
+    one_core_sem,
+    one_y_sem,
+    low_sem,
+    kv_sem,
+    kvx_sem,
+    dkv_sem,
+    xs_sem,
+    dn_sem,
+    up_sem,
+    dn_sem2,
+    up_sem2,
+    out_sem,
+    mixed_sem,
+    token_sem,
+    small_c_sem,
+    small_x_sem,
+    small_z_sem,
+    last_sem,
+):
+    me = Place()
+    z, x, y, c = me.z, me.x, me.y, me.c
+    deep, shard = wqkv.shape[0], wqkv.shape[1]
+    trees, heads, rows, length = probs.shape
+    width = hid.shape[1]
+    units = acts.shape[1]
+    mine = heads * HEAD_SIZE
+    half = shard // 2
+    inv_root = HEAD_SIZE ** (-0.5)
+    step = rows // CHUNKS
+    tile = 128
+    own_block = c * 2 + x
+    own_rows = pl.ds(pl.multiple_of(own_block * rows, rows), rows)
+
+    def load(source, target, at):
+        return pltpu.make_async_copy(source, target, load_sem.at[at])
+
+    loads = [
+        load(mats_b, mats.at[pl.ds(3 * units, 3 * units)], 0),
+        load(hid_in, hid, 1),
+        load(ups_in, ups, 2),
+        load(mats_a, mats.at[pl.ds(0, 3 * units)], 3),
+        load(acts_a, acts.at[pl.ds(0, 3)], 4),
+        load(after_in, after, 5),
+        load(wqkv_in, wqkv, 6),
+        load(wout_in, wout, 7),
+        load(queries_in, queries, 8),
+        load(keys_in, keys, 9),
+        load(values_in, values, 10),
+        load(probs_in, probs, 11),
+        load(context_in, context, 12),
+        load(tables_in, tables, 13),
+    ]
+    for copy in loads:
+        copy.start()
+
+    lin = x * 4 + me.t
+
+    def plane(number):
+        return (z, number // 4, number % 4)
+
+    greet(
+        [me.at_z((z + k) % deep) for k in range(1, deep)]
+        + [plane((lin + k) % 8) for k in range(1, 8)]
+    )
+    for copy in loads[:3]:
+        copy.wait()
+
+    gates_b[...] = jnp.zeros_like(gates_b)
+    expert_acts(mats, hid, ups, mixes, acts, gates_b, 1, 2, x, quarter)
+    for copy in loads[3:]:
+        copy.wait()
+
+    for block in range(2 * trees):
+        at = pl.ds(block * rows, rows)
+        gates_out[block] = jnp.concatenate(
+            [gates_a[:2, at], gates_b[:2, at], jnp.zeros((4, rows), F32)], 0
+        )
+
+    def gate_copy(k):
+        there = (lin + k) % 8
+        block = (there % 2) * 2 + there // 4
+        return remote(gates_out.at[block], gates_in.at[lin], gate_sem, k - 1, plane(there))
+
+    for k in range(1, 8):
+        gate_copy(k).start()
+    gates_in[lin] = gates_out[own_block]
+
+    def mat(group, kind):
+        return mats[pl.ds((3 * group + kind) * units, units), :]
+
+    def two_tile(first):
+        at = pl.ds(first, tile)
+        total = mm(acts[0, :, at], mat(0, 0), TN)
+        total = total + mm(acts[1, :, at], mat(0, 1), TN)
+        total = total + mm(acts[3, :, at], mat(1, 0), TN)
+        return total + mm(acts[4, :, at], mat(1, 1), TN)
+
+    def mo_tile(first):
+        at = pl.ds(first, tile)
+        return mm(acts[2, :, at], mat(0, 2), TN) + mm(acts[5, :, at], mat(1, 2), TN)
+
+    two = PlaneSum(
+        me,
+        rows,
+        tile,
+        (core_out, x_out, acc, y_out),
+        (two_core_in, two_x_in, two_y_in),
+        (two_core_sem, two_x_sem, two_y_sem),
+    )
+    two.outward(two_tile)
+    two.across(two_tile)
+    two.inward(two_tile)
+
+    chain = Chain(me, stage, from_dn, from_up, dn_sem, up_sem, 64)
+    for m in range(3):
+        expert_grads(m, 1, acts, ups if m == 2 else hid, stage)
+        chain.begin(m)
+
+    for k in range(1, 8):
+        source = (lin + 8 - k) % 8
+        remote(gates_out.at[0], gates_in.at[source], gate_sem, k - 1, plane(source)).wait_recv()
+    sums = []
+    for side in range(2):
+        total = gates_in[side * 4]
+        for k in range(1, 4):
+            total = total + gates_in[side * 4 + k]
+        sums.append(total[:4])
+    mix_grad = jnp.concatenate(sums, 0)
+    mix = mixes[own_block]
+    picked = mix * (mix_grad - jnp.sum(mix * mix_grad, 0, keepdims=True))
+    logit_grad = picked.astype(BF16)
+    router = jnp.concatenate([smalls[k, 8:, :] for k in range(deep)], 1)
+    gain_one = jnp.concatenate([smalls[k, :1, :] for k in range(deep)], 1).astype(F32)
+    gain_two = jnp.concatenate([smalls[k, 1:2, :] for k in range(deep)], 1).astype(F32)
+    agrad[...] = mm(logit_grad, router, TN)
+    small_own[pl.ds(0, 8), :] = jnp.zeros((8, width), F32)
+    small_own[pl.ds(8, 8), :] = mm(logit_grad, hid[own_rows, :])
+
+    for number in range(2 * two.tiles):
+        two.core_copy(number).wait_send()
+    mo = PlaneSum(
+        me,
+        rows,
+        tile,
+        (core_out, hid.at[pl.ds(rows, rows)], acc, hid.at[pl.ds(0, rows)]),
+        (mo_core_in, mo_x_in, mo_y_in),
+        (mo_core_sem, mo_x_sem, mo_y_sem),
+    )
+    mo.outward(mo_tile)
+    mo.across(mo_tile)
+    two.pass_on()
+    mo.inward(mo_tile)
+    late = [
+        load(hid_one_in.at[0], mats.at[pl.ds(0, rows)], 0),
+        load(hid_one_in.at[1], mats.at[pl.ds(rows, rows)], 1),
+        load(tokens_in.at[c], mats.at[pl.ds(2 * rows, rows)], 2),
+    ]
+    for copy in late:
+        copy.start()
+
+    def low_copy(number):
+        at = alow.at[c, pl.ds(pl.multiple_of(number * step, step), step)]
+        return remote(at, at, low_sem, number, me.core_peer())
+
+    def second_norm(number, gain_grad):
+        at = pl.ds(pl.multiple_of(number * step, step), step)
+        upstream = two.total(number) + agrad[at, :]
+        value = after[at, :]
+        factor = lax.rsqrt(jnp.mean(value * value, -1, keepdims=True) + EPS)
+        scaled = upstream * gain_two
+        inner = jnp.mean(scaled * value, -1, keepdims=True)
+        cot = ups[pl.ds(pl.multiple_of(own_block * rows + number * step, step), step), :]
+        total = cot.astype(F32) + (factor * scaled - value * (factor * factor * factor * inner))
+        agrad[at, :] = total
+        alow[c, at, :] = total.astype(BF16)
+        low_copy(number).start()
+        return gain_grad + jnp.sum(upstream * value * factor, 0, keepdims=True)
+
+    gain_two_grad = lax.fori_loop(0, CHUNKS, second_norm, jnp.zeros((1, width), F32))
+    small_own[pl.ds(1, 1), :] = gain_two_grad
+    mo.pass_on()
+
+    def attend_back(tree):
+        back = jnp.zeros((rows, mine), F32)
+        for k in range(deep):
+            back = back + mm(alow[tree, :, pl.ds(k * shard, shard)], wout[k], NT)
+        back = back.astype(BF16)
+        cosine, sine = tables[0, tree], tables[1, tree]
+        key_grad = jnp.zeros((length, HEAD_SIZE), F32)
+        value_grad = jnp.zeros((length, HEAD_SIZE), F32)
+        for head in range(heads):
+            lanes = pl.ds(head * HEAD_SIZE, HEAD_SIZE)
+            back_head = back[:, head * HEAD_SIZE : (head + 1) * HEAD_SIZE]
+            prob = probs[tree, head]
+            value_grad = value_grad + mm(prob, back_head, TN)
+            prob = prob.astype(F32)
+            share = prob * mm(back_head, values[tree], NT)
+            score = (share - prob * jnp.sum(share, -1, keepdims=True)).astype(BF16)
+            query_grad = mm(score, keys[tree]) * inv_root
+            qlow[tree, :, lanes] = turn(query_grad, cosine, -sine).astype(BF16)
+            key_grad = key_grad + mm(score, queries[tree, head], TN)
+        return jnp.concatenate([key_grad * inv_root, value_grad], 1)
+
+    kv_own[...] = attend_back(c)
+    for number in range(CHUNKS):
+        at = alow.at[1 - c, pl.ds(number * step, step)]
+        remote(at, at, low_sem, number, me.core_peer()).wait_recv()
+    kv_out[...] = attend_back(1 - c).astype(BF16)
+    kv_copy = remote(kv_out, kv_in, kv_sem, 0, me.core_peer())
+    kv_copy.start()
+    chain.advance(0)
+
+    def one_tile(tree, number):
+        at = pl.ds(pl.multiple_of(number * step, step), step)
+        return [mm(qlow[tree, at, :], wqkv[k, :, pl.ds(0, mine)], NT) for k in range(deep)]
+
+    one_out = core_out.at[pl.ds(0, rows)]
+    for number in range(2 * mo.tiles):
+        mo.core_copy(number).wait_send()
+
+    def one_copy(number):
+        at = pl.ds(pl.multiple_of(number * step, step), step)
+        return remote(one_out.at[at], one_core_in.at[at], one_core_sem, number, me.core_peer())
+
+    def one_outward(number, carry):
+        at = pl.ds(pl.multiple_of(number * step, step), step)
+        for k, piece in enumerate(one_tile(1 - c, number)):
+            one_out[at, pl.ds(k * shard, shard)] = piece.astype(BF16)
+        one_copy(number).start()
+        return carry
+
+    lax.fori_loop(0, CHUNKS, one_outward, 0)
+
+    kv_copy.wait_recv()
+    kvx_out[...] = (
+        jnp.where(x == 0, kv_own[pl.ds(rows, rows), :], kv_own[pl.ds(0, rows), :])
+        + jnp.where(x == 0, kv_in[pl.ds(rows, rows), :], kv_in[pl.ds(0, rows), :]).astype(F32)
+    ).astype(BF16)
+    kvx_copy = remote(kvx_out, kvx_in, kvx_sem, 0, me.x_peer())
+    kvx_copy.start()
+
+    for copy in late:
+        copy.wait()
+
+    def hid_one(tree, lanes):
+        return mats[pl.ds(pl.multiple_of(tree * rows, rows), rows), lanes]
+
+    def halves(value):
+        low, high = value[:half], value[half:]
+        return jnp.where(x == 0, low, high), jnp.where(x == 0, high, low)
+
+    ctx = [
+        jnp.concatenate([context[tree, head] for head in range(heads)], 1) for tree in range(trees)
+    ]
+
+    def xs_copy(part):
+        lanes = (pl.ds(0, mine), pl.ds(mine, mine), pl.ds(2 * mine, HEAD_SIZE))[part]
+        return remote(xs_out.at[:, :, lanes], xs_in.at[:, :, lanes], xs_sem, part, me.x_peer())
+
+    def shard_lanes(k):
+        return pl.ds(pl.multiple_of(k * shard, shard), shard)
+
+    def output_grad(k, carry):
+        value = sum(mm(alow[tree, :, shard_lanes(k)], ctx[tree], TN) for tree in range(trees))
+        keep, away = halves(value)
+        stage2[k, 0, :, pl.ds(mine, mine)] = keep.astype(BF16)
+        xs_out[k, :, pl.ds(mine, mine)] = away.astype(BF16)
+        return carry
+
+    lax.fori_loop(0, deep, output_grad, 0)
+    xs_copy(1).start()
+
+    def query_weight_grad(k, carry):
+        value = sum(mm(hid_one(tree, shard_lanes(k)), qlow[tree], TN) for tree in range(trees))
+        keep, away = halves(value)
+        stage2[k, 0, :, pl.ds(0, mine)] = keep.astype(BF16)
+        xs_out[k, :, pl.ds(0, mine)] = away.astype(BF16)
+        return carry
+
+    lax.fori_loop(0, deep, query_weight_grad, 0)
+    xs_copy(0).start()
+
+    kvx_copy.wait_recv()
+    own_kv = (
+        jnp.where(x == 0, kv_own[pl.ds(0, rows), :], kv_own[pl.ds(rows, rows), :])
+        + jnp.where(x == 0, kv_in[pl.ds(0, rows), :], kv_in[pl.ds(rows, rows), :]).astype(F32)
+        + kvx_in[...].astype(F32)
+    )
+    kvlow[:, pl.ds(0, HEAD_SIZE)] = turn(
+        own_kv[:, :HEAD_SIZE], tables[0, c], -tables[1, c]
+    ).astype(BF16)
+    kvlow[:, pl.ds(HEAD_SIZE, HEAD_SIZE)] = own_kv[:, HEAD_SIZE:].astype(BF16)
+
+    for number in range(CHUNKS):
+        two.y_copy(number).wait_send()
+
+    def y_copy(number):
+        at = pl.ds(pl.multiple_of(number * step, step), step)
+        return remote(y_out.at[at], one_y_in.at[at], one_y_sem, number, me.y_peer())
+
+    def one_inward(number, carry):
+        at = pl.ds(pl.multiple_of(number * step, step), step)
+        one_copy(number).wait_recv()
+        for k, piece in enumerate(one_tile(c, number)):
+            lanes = pl.ds(k * shard, shard)
+            piece = piece + mm(kvlow[at, :], wqkv[k, :, pl.ds(mine, 2 * HEAD_SIZE)], NT)
+            y_out[at, lanes] = (piece + one_core_in[at, lanes].astype(F32)).astype(BF16)
+        y_copy(number).start()
+        return carry
+
+    lax.fori_loop(0, CHUNKS, one_inward, 0)
+
+    def kv_weight_grad(k, carry):
+        value = mm(hid_one(c, shard_lanes(k)), kvlow[...], TN)
+        low, high = value[:, :HEAD_SIZE], value[:, HEAD_SIZE:]
+        dkv_out[0, k] = jnp.where(c == 0, high, low).astype(BF16)
+        dkv_out[1, k] = jnp.where(c == 0, low, high).astype(BF16)
+        return carry
+
+    lax.fori_loop(0, deep, kv_weight_grad, 0)
+    dkv_copy = remote(dkv_out.at[0], dkv_in, dkv_sem, 0, me.core_peer())
+    dkv_copy.start()
+    chain.advance(1)
+    dkv_copy.wait_recv()
+
+    def kv_weight_sum(k, carry):
+        keep, away = halves(dkv_out[1, k].astype(F32) + dkv_in[k].astype(F32))
+        stage2[k, 0, :, pl.ds(2 * mine, HEAD_SIZE)] = keep.astype(BF16)
+        xs_out[k, :, pl.ds(2 * mine, HEAD_SIZE)] = away.astype(BF16)
+        return carry
+
+    lax.fori_loop(0, deep, kv_weight_sum, 0)
+    xs_copy(2).start()
+
+    for number in range(CHUNKS):
+        two.x_copy(number).wait_send()
+
+    def out_copies(buffer, target, sem_at, peer_sems, number):
+        at = pl.ds(pl.multiple_of(number * step, step), step)
+        here = pltpu.make_async_copy(buffer.at[at], target.at[c, at], out_sem.at[sem_at + number])
+        there = remote(buffer.at[at], target.at[c, at], peer_sems, number, me.core_peer())
+        return here, there
+
+    def mix_out(number, carry):
+        at = pl.ds(pl.multiple_of(number * step, step), step)
+        x_out[at, :] = (after[at, :] + mo.total(number)).astype(BF16)
+        for copy in out_copies(x_out, mixed, 0, mixed_sem, number):
+            copy.start()
+        return carry
+
+    lax.fori_loop(0, CHUNKS, mix_out, 0)
+
+    def first_norm(number, gain_grad):
+        at = pl.ds(pl.multiple_of(number * step, step), step)
+        y_copy(number).wait_recv()
+        upstream = y_out[at, :].astype(F32) + one_y_in[at, :].astype(F32)
+        value = mats[pl.ds(pl.multiple_of(2 * rows + number * step, step), step), :].astype(F32)
+        factor = lax.rsqrt(jnp.mean(value * value, -1, keepdims=True) + EPS)
+        scaled = upstream * gain_one
+        inner = jnp.mean(scaled * value, -1, keepdims=True)
+        acc[at, :] = agrad[at, :] + (
+            factor * scaled - value * (factor * factor * factor * inner)
+        )
+        for copy in out_copies(acc, d_tokens, CHUNKS, token_sem, number):
+            copy.start()
+        return gain_grad + jnp.sum(upstream * value * factor, 0, keepdims=True)
+
+    gain_one_grad = lax.fori_loop(0, CHUNKS, first_norm, jnp.zeros((1, width), F32))
+    small_own[pl.ds(0, 1), :] = gain_one_grad
+    small_c = remote(small_own, small_core, small_c_sem, 0, me.core_peer())
+    small_c.start()
+    chain.advance(2)
+
+    for part in range(3):
+        xs_copy(part).wait_recv()
+
+    def side_sum(k, carry):
+        stage2[k, 0] = (stage2[k, 0].astype(F32) + xs_in[k].astype(F32)).astype(BF16)
+        return carry
+
+    lax.fori_loop(0, deep, side_sum, 0)
+    chain2 = Chain(me, stage2, from_dn2, from_up2, dn_sem2, up_sem2, 64)
+    chain2.begin(0)
+
+    small_c.wait_recv()
+    small_c.wait_send()
+    small_own[...] = small_own[...] + small_core[...]
+    small_x_copy = remote(small_own, small_x, small_x_sem, 0, me.x_peer())
+    small_x_copy.start()
+    chain2.advance(0)
+    small_x_copy.wait_recv()
+    small_x_copy.wait_send()
+    small_own[...] = small_own[...] + small_x[...]
+
+    def small_copy(k):
+        there = (z + k) % deep
+        return remote(
+            small_own.at[:, shard_lanes(there)], small_z.at[z], small_z_sem, k - 1, me.at_z(there)
+        )
+
+    for k in range(1, deep):
+        small_copy(k).start()
+    small_z[z] = small_own[:, shard_lanes(z)]
+    for m in range(3):
+
+        def write(at, value):
+            grads[m, at, :] = value
+
+        chain.finish(m, write)
+
+    def write2(at, value):
+        d_qo[at, :] = value[:, : 2 * mine]
+        kv_last[at, :] = value[:, 2 * mine :]
+
+    chain2.finish(0, write2)
+
+    share = half // 4
+    columns = pl.ds(pl.multiple_of((c * 2 + y) * HEAD_SIZE, HEAD_SIZE), HEAD_SIZE)
+
+    def last_copy(k):
+        there = (me.t + k) % 4
+        return remote(
+            kv_last.at[pl.ds(pl.multiple_of(there * share, 8), share)],
+            d_kv.at[:, columns],
+            last_sem,
+            k - 1,
+            (z, x, there),
+        )
+
+    for k in range(1, 4):
+        last_copy(k).start()
+    d_kv[:, columns] = kv_last[pl.ds(pl.multiple_of(me.t * share, 8), share), :]
+    for k in range(1, deep):
+        source = (z + deep - k) % deep
+        remote(
+            small_own.at[:, shard_lanes(0)], small_z.at[source], small_z_sem, k - 1, me.at_z(source)
+        ).wait_recv()
+    total = small_z[0]
+    for k in range(1, deep):
+        total = total + small_z[k]
+    d_small[...] = total
+    for k in range(1, 4):
+        source = (me.t + 4 - k) % 4
+        there = pl.ds(pl.multiple_of(((source % 2) * 2 + source // 2) * HEAD_SIZE, HEAD_SIZE), HEAD_SIZE)
+        remote(
+            kv_last.at[pl.ds(0, share)], d_kv.at[:, there], last_sem, k - 1, (z, x, source)
+        ).wait_recv()
+
+    for number in range(CHUNKS):
+        at = pl.ds(number * step, step)
+        remote(
+            x_out.at[at], mixed.at[1 - c, at], mixed_sem, number, me.core_peer()
+        ).wait_recv()
+        remote(
+            acc.at[at], d_tokens.at[1 - c, at], token_sem, number, me.core_peer()
+        ).wait_recv()
+        for buffer, target, first, peer_sems in (
+            (x_out, mixed, 0, mixed_sem),
+            (acc, d_tokens, CHUNKS, token_sem),
+        ):
+            here, there = out_copies(buffer, target, first, peer_sems, number)
+            here.wait()
+            there.wait_send()
+        mo.x_copy(number).wait_send()
+        mo.y_copy(number).wait_send()
+        y_copy(number).wait_send()
+        one_copy(number).wait_send()
+        low_copy(number).wait_send()
+    for k in range(1, 8):
+        gate_copy(k).wait_send()
+    for k in range(1, deep):
+        small_copy(k).wait_send()
+    for k in range(1, 4):
+        last_copy(k).wait_send()
+    for part in range(3):
+        xs_copy(part).wait_send()
+    for copy in (kv_copy, kvx_copy, dkv_copy):
+        copy.wait_send()
+    for m in range(3):
+        chain.drain(m)
+    chain2.drain(0)
+
+
+def rest_call(mats_a, mats_b, acts_a, gates_a, hid, ups, mixes, made, tokens, deep, quarter):
+    hid_one, wqkv, wout, smalls, queries, keys, values, probs, context, tables, after = made
+    units, width = mats_a.shape[0] // 3, mats_a.shape[1]
+    count = hid.shape[0]
+    trees, heads, rows, length = probs.shape
+    shard = width // deep
+    half = shard // 2
+    mine = heads * HEAD_SIZE
+    lanes = 2 * mine + HEAD_SIZE
+    vmem = pl.BlockSpec(memory_space=pltpu.VMEM)
+    anywhere = pl.BlockSpec(memory_space=pl.ANY)
+
+    def like(array):
+        return pltpu.VMEM(array.shape, array.dtype)
+
+    def plain(*shape):
+        return pltpu.VMEM(shape, BF16)
+
+    def wide(*shape):
+        return pltpu.VMEM(shape, F32)
+
+    hbm, on_chip = anywhere, vmem
+    return pl.pallas_call(
+        functools.partial(rest_kernel, quarter),
+        out_shape=(
+            jax.ShapeDtypeStruct((trees, rows, width), BF16),
+            jax.ShapeDtypeStruct((trees, rows, width), F32),
+            jax.ShapeDtypeStruct((3, units, shard), F32),
+            jax.ShapeDtypeStruct((half, 2 * mine), F32),
+            jax.ShapeDtypeStruct((half // 4, 2 * KEY_VALUE_HEADS * HEAD_SIZE), F32),
+            jax.ShapeDtypeStruct((smalls.shape[1], shard), F32),
+        ),
+        in_specs=[hbm, hbm, hbm, on_chip, hbm, hbm, on_chip, hbm, hbm, hbm, hbm, on_chip]
+        + [hbm] * 7,
+        out_specs=[hbm, hbm] + [on_chip] * 4,
+        scratch_shapes=[
+            plain(6 * units, width),
+            plain(6, units, count),
+            plain(count, width),
+            plain(count, width),
+            like(wqkv),
+            like(wout),
+            like(queries),
+            like(keys),
+            like(values),
+            like(probs),
+            like(context),
+            like(tables),
+            like(after),
+            wide(8, count),
+            wide(2 * trees, 8, rows),
+            wide(8, 8, rows),
+            plain(2 * rows, width),
+            plain(rows, width),
+            wide(rows, width),
+            plain(rows, width),
+            plain(2 * rows, width),
+            plain(rows, width),
+            plain(rows, width),
+            plain(2 * rows, width),
+            plain(rows, width),
+            plain(rows, width),
+            plain(rows, width),
+            plain(rows, width),
+            wide(rows, width),
+            plain(trees, rows, width),
+            plain(trees, rows, mine),
+            plain(length, 2 * HEAD_SIZE),
+            plain(length, 2 * HEAD_SIZE),
+            wide(length, 2 * HEAD_SIZE),
+            plain(rows, 2 * HEAD_SIZE),
+            plain(rows, 2 * HEAD_SIZE),
+            plain(rows, 2 * HEAD_SIZE),
+            plain(2, deep, shard, HEAD_SIZE),
+            plain(deep, shard, HEAD_SIZE),
+            plain(deep, half, lanes),
+            plain(deep, half, lanes),
+            plain(deep, 3, units, shard),
+            plain(deep - 1, 3, units, shard),
+            plain(deep - 1, 3, units, shard),
+            plain(deep, 1, half, lanes),
+            plain(deep - 1, 1, half, lanes),
+            plain(deep - 1, 1, half, lanes),
+            wide(smalls.shape[1], width),
+            wide(smalls.shape[1], width),
+            wide(smalls.shape[1], width),
+            wide(deep, smalls.shape[1], shard),
+            wide(half, HEAD_SIZE),
+            pltpu.SemaphoreType.DMA((14,)),
+            sems(7),
+            sems(4),
+            sems(CHUNKS),
+            sems(CHUNKS),
+            sems(4),
+            sems(CHUNKS),
+            sems(CHUNKS),
+            sems(CHUNKS),
+            sems(CHUNKS),
+            sems(CHUNKS),
+            sems(1),
+            sems(1),
+            sems(1),
+            sems(3),
+            sems((deep - 1) * 3),
+            sems((deep - 1) * 3),
+            sems(deep - 1),
+            sems(deep - 1),
+            pltpu.SemaphoreType.DMA((2 * CHUNKS,)),
+            sems(CHUNKS),
+            sems(CHUNKS),
+            sems(1),
+            sems(1),
+            sems(deep - 1),
+            sems(3),
+        ],
+        compiler_params=pltpu.CompilerParams(
+            collective_id=2, has_side_effects=True, vmem_limit_bytes=64 * 2**20
+        ),
+        name="rest",
+    )(
+        mats_a,
+        mats_b,
+        acts_a,
+        gates_a,
+        hid,
+        ups,
+        mixes,
+        hid_one,
+        tokens,
+        wqkv,
+        wout,
+        smalls,
+        queries,
+        keys,
+        values,
+        probs,
+        context,
+        tables,
+        after,
+    )
+
+
+def plane_shards(
+    tokens,
+    cotangent,
+    seg_start,
+    seg_parent,
+    routes,
+    attn_gain,
+    w_query,
+    w_key,
+    w_value,
+    w_output,
+    moe_gain,
+    w_router,
+    w_gate,
+    w_up,
+    w_down,
+):
+    trees, rows, width = tokens.shape
+    deep = lax.axis_size("dp")
+    held, quarter = w_gate.shape[0], w_gate.shape[2]
+    group = held // 2
+    heads = w_query.shape[1] // HEAD_SIZE
+    mine = heads * HEAD_SIZE
+    gate_t, up_t = jnp.swapaxes(w_gate, 1, 2), jnp.swapaxes(w_up, 1, 2)
+
+    def gathered(first):
+        some = slice(first, first + group)
+        own = jnp.concatenate([gate_t[some], up_t[some], w_down[some]], 0)
+        full = lax.all_gather(own, "dp", axis=2, tiled=True)
+        return full.reshape(3 * group * quarter, width)
+
+    mats_a, mats_b = gathered(0), gathered(group)
+    small = jnp.concatenate(
+        [attn_gain[None], moe_gain[None], jnp.zeros((6, attn_gain.shape[0]), BF16), w_router.T], 0
+    )
+    made = attend_call(
+        seg_start,
+        seg_parent,
+        tokens,
+        cotangent,
+        jnp.swapaxes(routes, 1, 2),
+        w_query,
+        w_key,
+        w_value,
+        w_output,
+        small,
+        deep,
+    )
+    hid, ups, mixes = made[11:]
+    count = trees * 2 * rows
+    hid, ups = hid.reshape(count, width), ups.reshape(count, width)
+    mixes = mixes.reshape(trees * 2, -1, rows)
+    acts_a, gates_a, grads_a = experts_call(mats_a, hid, ups, mixes, deep)
+    mixed, d_tokens, grads_b, d_qo, d_kv, d_small = rest_call(
+        mats_a,
+        mats_b,
+        acts_a,
+        gates_a,
+        hid,
+        ups,
+        mixes,
+        made[:11],
+        tokens,
+        deep,
+        quarter,
+    )
+    both = jnp.concatenate(
+        [
+            grads_a.reshape(3, group, quarter, width // deep),
+            grads_b.reshape(3, group, quarter, width // deep),
+        ],
+        1,
+    )
+    part = width // deep // 2
+    d_small = lax.dynamic_slice_in_dim(d_small, lax.axis_index("expert") * part, part, 1)
+    kv = KEY_VALUE_HEADS * HEAD_SIZE
+    return (
+        mixed,
+        d_tokens,
+        d_small[0],
+        d_qo[:, :mine],
+        d_kv[:, :kv],
+        d_kv[:, kv:],
+        d_qo[:, mine:].T,
+        d_small[1],
+        d_small[8:].T,
+        jnp.swapaxes(both[0], 1, 2),
+        jnp.swapaxes(both[1], 1, 2),
+        both[2],
+    )
+
+
+def shards(*arrays):
+    sizes = lax.axis_size("expert"), lax.axis_size("tensor"), arrays[0].shape[0]
+    if sizes == (2, 4, 2):
+        return plane_shards(*arrays)
+    return general_shards(*arrays)
+
+
 def solution(mesh):
     placed = (
         P("dp", "expert", None),

time: 1050 us -> 402 us (0.38)
  waiting for transfers between devices: 729 us -> 0.08 us
  Pallas kernels: 0 us -> 368 us
  matrix products: 103 us -> 0 us
  local copies, waits for them, and re-layouts: 80.6 us -> 11.9 us
  blocking collectives: 57.8 us -> 0 us
  other arithmetic: 55.9 us -> 6.68 us
    pallas_call x0 -> x3, Pallas kernels: none -> 368 us  [the longest x1 139 us: rest_call(): pl.pallas_call(functools.partial(rest_kernel, quarter), out_shape=(jax.Sh...]
    all_gather x7 -> x2, waiting for transfers between devices: 231 us -> 0.04 us  [gathered(): full = lax.all_gather(own, 'dp', axis=2, tiled=True)]
    unnamed x33 -> x2, waiting for transfers between devices: 204 us -> 0.03 us
    psum x3 -> x0, waiting for transfers between devices: 147 us -> none  [the longest x2 108 us: to_owner(): return lax.psum(part, 'tensor').reshape(trees * rows, -1)]
    reduce_scatter x9 -> x0, waiting for transfers between devices: 147 us -> none  [the longest x2 68.7 us: to_owner(): part = lax.psum_scatter(array, 'expert', scatter_dimension=1, tiled=True)]
    dot_general x26 -> x0, matrix products: 99 us -> none  [the longest x21 90.6 us: dot(): lax.dot_general(left, right, (dims, ((), ())), preferred_element_type=F32)]
    all_gather x3 -> x0, blocking collectives: 45.3 us -> none  [the longest x1 32.7 us: over_dp(): return lax.all_gather(array, 'dp', axis=axis, tiled=True)]
    unnamed x121 -> x16, local copies, waits for them, and re-layouts: 48.4 us -> 4.29 us
  transfers between devices with their start and end apart: 27 -> 2, of which waited for: 24 -> 0; matrix products, arithmetic and copies ran while one was open for 16% -> 0% of each run, Pallas kernels for 0% -> 57%
where the time goes in v2:
time: 402 us; the launch traced here: 401 us
  Pallas kernels  368 us (92%)
  between operations  14.2 us (4%)
  local copies, waits for them, and re-layouts  11.9 us (3%)
  other arithmetic  6.68 us (2%)
    pallas_call x1, Pallas kernels, rest_call(): pl.pallas_call(functools.partial(rest_kernel, quarter), out_shape=(jax.Sh...  139 us
    pallas_call x1, Pallas kernels, attend_call(): pl.pallas_call(attend_kernel, out_shape=(out((trees, rows, width), BF16),...  138 us
    pallas_call x1, Pallas kernels, experts_call(): pl.pallas_call(functools.partial(experts_kernel, quarter), out_shape=(jax...  92.2 us
  transfers between devices with their start and end apart: 2, of which 0 were waited for; matrix products, arithmetic and copies ran while one was open for 0% of the time, Pallas kernels for 57%

profile of v2, /device:TPU:0, one launch (start us, length us, event | category | flops | bytes accessed | tf_op | source)
XLA Modules:
  0.0 401.2 jit_solution(17627905142402927309)
XLA Ops:
  7.2 0.0 copy-start.2
  7.2 0.0 copy-start.3
  7.2 0.0 all-gather.3.cloned.1.call-start
  7.2 1.2 fusion.7
  8.4 0.0 copy-done.2
  8.5 0.1 copy-done.3
  8.6 0.1 fusion.5
  8.7 1.0 pad_maximum_fusion.1
  9.8 0.0 copy-start.5
  9.8 0.0 copy-start.6
  9.8 0.0 copy-start.4
  9.8 0.0 all-gather.3.cloned.1.call-update
  9.8 0.0 all-gather.5.cloned.1.call-start
  9.8 1.0 pad_maximum_fusion.2
  10.9 0.0 all-gather.5.cloned.1.call-update
  10.9 0.0 copy-done.5
  10.9 0.0 copy-done.6
  11.0 0.1 pad.4.clone
  11.0 0.0 copy-done.4
  11.0 0.7 pad_maximum_fusion.3.small
  11.7 137.7 %attend.1 = (bf16[2,256,1536]{2,1,0:T(8,128)(2,1)}, bf16[4,384,640]{2,1,0:T(8,128)(2,1)}, bf16[4,384,384]{2,1,0:T(8,128)(2,1)}, bf16[4,16,384]{2,1,0:T(8,128)(2,...) custom-call(s32[2,9]{1,0:T(2,128)} %starts.1, ...), custom_call_target="tpu_custom_call" | custom-call | tf_op jit(solution)/shard_map/attend/pallas_call | solution.py:799
  149.4 0.0 all-gather.3.cloned.1.call-done
  149.4 92.2 %experts.1 = (bf16[3,384,1024]{2,1,0:T(8,128)(2,1)}, f32[8,1024]{1,0:T(8,128)}, f32[3,384,384]{2,1,0:T(8,128)}) custom-call(bf16[1152,1536]{1,0:T(8,128)(2,1)} %bitcast.27, bf16[1024,1536]{1,0:T(8,128)(2,1)} %bitcast.29, bf16[1024,1536]{1,0:T(8,128)(2,1)} %bitcast.31, f32[4,8,256]{2,1,0:T(8,128)} %bitcast.38), custom_call_target="tpu_custom_call" | custom-call | tf_op jit(solution)/shard_map/experts/pallas_call | solution.py:1059
  241.6 0.0 all-gather.5.cloned.1.call-done
  241.6 138.6 %rest.1 = (bf16[2,256,1536]{2,1,0:T(8,128)(2,1)}, f32[2,256,1536]{2,1,0:T(8,128)}, f32[3,384,384]{2,1,0:T(8,128)}, f32[192,768]{1,0:T(8,128)}, f32[48,512]{1,0:T(8,128)}, /*index=5*/f32[16,384]{1,0:T(8,128)}) custom-call(bf16[1152,1536]{1,0:T(8,128)(2,1)} %bitcast.28, bf16[1152,1536]{1,0:T(8,128)(2,1)} %bitcast.33, ...), custom_call_target="tpu_custom_call" | custom-call | tf_op jit(solution)/shard_map/rest/pallas_call | solution.py:1766
  380.2 1.9 slice_bitcast_fusion
  382.1 1.5 fusion.8
  383.5 1.4 dynamic-slice_bitcast_fusion
  384.9 1.4 fusion.9
  386.3 0.0 copy-start.1
  386.3 3.9 fusion.4
  390.3 0.0 copy-done.1
  390.3 0.0 copy-start
  390.3 1.1 copy.30
  391.4 1.3 copy-done
  392.7 1.7 copy.31
  (3 shorter events, 0.0 us)
Async XLA Ops:
  7.2 1.3 copy-start.2
  7.2 1.4 copy-start.3
  7.2 142.2 %all-gather.3.cloned.1.call-start = ((), (), s32[]{:S(2)}) async-start(), calls=%async_computation | async-start | bytes 4423680 | tf_op jit(solution)/shard_map/all_gather | solution.py:1914
  9.8 1.1 copy-start.5
  9.8 1.2 copy-start.6
  9.8 1.3 copy-start.4
  9.8 231.8 %all-gather.5.cloned.1.call-start = ((), (), s32[]{:S(2)}) async-start(), calls=%async_computation.1 | async-start | bytes 4423680 | tf_op jit(solution)/shard_map/all_gather | solution.py:1914
  386.3 3.9 copy-start.1
  390.3 2.5 copy-start
Sparse Core Ops, SparseCore 0:
  10.2 91.5 all-gather.2
  103.9 71.7 all-gather.4

commit v3 on v1

--- a/solution.py
+++ b/solution.py
@@ -1,6 +1,12 @@
+import functools
+import math
+
 import jax
 import jax.numpy as jnp
+import numpy as np
 from jax import lax
+from jax.experimental import pallas as pl
+from jax.experimental.pallas import tpu as pltpu
 from jax.sharding import PartitionSpec as P
 
 QUERY_HEADS = 12
@@ -65,7 +71,7 @@
     return jnp.concatenate([front * cosine - back * sine, back * cosine + front * sine], -1)
 
 
-def shards(
+def general_shards(
     tokens,
     cotangent,
     seg_start,
@@ -302,6 +308,1663 @@
         jnp.swapaxes(d_up, 1, 2),
         d_down,
     )
+
+
+MESH = pl.DeviceIdType.MESH
+NT = (((1,), (1,)), ((), ()))
+NN = (((1,), (0,)), ((), ()))
+TN = (((0,), (0,)), ((), ()))
+CHUNKS = 4
+TILE = 128
+KINDS = 3
+ROOT_2_PI = math.sqrt(2.0 / math.pi)
+CUBIC = 0.044715
+
+
+def mm(left, right, dims=NN):
+    return lax.dot_general(left, right, dims, preferred_element_type=F32)
+
+
+def rows_at(number, size):
+    return pl.ds(pl.multiple_of(number * size, size), size)
+
+
+class Place:
+    def __init__(self):
+        self.z = lax.axis_index("dp")
+        self.x = lax.axis_index("expert")
+        self.t = lax.axis_index("tensor")
+        self.y = self.t // 2
+        self.c = self.t % 2
+
+    def at_z(self, z):
+        return (z, self.x, self.t)
+
+    def x_peer(self):
+        return (self.z, 1 - self.x, self.t)
+
+    def y_peer(self):
+        return (self.z, self.x, (self.t + 2) % 4)
+
+    def core_peer(self):
+        return (self.z, self.x, self.t + 1 - 2 * self.c)
+
+
+def remote(src, dst, sems, at, device):
+    return pltpu.make_async_remote_copy(
+        src_ref=src,
+        dst_ref=dst,
+        send_sem=sems.at[0, at],
+        recv_sem=sems.at[1, at],
+        device_id=device,
+        device_id_type=MESH,
+    )
+
+
+def signal(sem, device):
+    pl.semaphore_signal(sem, inc=1, device_id=device, device_id_type=MESH)
+
+
+def await_signal(sem):
+    pl.semaphore_wait(sem, 1)
+
+
+def greet(devices):
+    barrier = pltpu.get_barrier_semaphore()
+    for device in devices:
+        pl.semaphore_signal(barrier, inc=1, device_id=device, device_id_type=MESH)
+    pl.semaphore_wait(barrier, len(devices))
+
+
+def tree_tables(starts, parents, tree, first, rows, length, frequency):
+    count = starts.shape[1]
+    place = first + lax.broadcasted_iota(jnp.int32, (rows, HEAD_SIZE), 0)
+    start = [starts[tree, k] for k in range(count)]
+    parent = [parents[tree, k] for k in range(count)]
+    size = [(start[k + 1] if k + 1 < count else length) - start[k] for k in range(count)]
+
+    def pick(table, at):
+        total = jnp.zeros_like(at)
+        for k in range(count):
+            total = total + jnp.where(at == k, table[k], 0)
+        return total
+
+    def segment_of(at):
+        total = jnp.zeros_like(at)
+        for k in range(1, count):
+            total = total + jnp.where(at >= start[k], 1, 0)
+        return total
+
+    segment = segment_of(place)
+    above = pick(parent, segment)
+    further = pick(parent, above)
+    depth = (
+        place
+        - pick(start, segment)
+        + jnp.where(segment != 0, pick(size, above), 0)
+        + jnp.where(above != 0, pick(size, further), 0)
+    )
+    turning = depth.astype(F32) * frequency
+    lane = lax.broadcasted_iota(jnp.int32, (rows, HEAD_SIZE), 1)
+    cosine = jnp.cos(turning)
+    sine = jnp.sin(turning)
+    sine = jnp.where(lane < HEAD_SIZE // 2, -sine, sine)
+    key_place = lax.broadcasted_iota(jnp.int32, (8, length), 1)
+    key_segment = jnp.broadcast_to(segment_of(key_place)[:1], (rows, length))
+    key_place = jnp.broadcast_to(key_place[:1], (rows, length))
+    wide = length // HEAD_SIZE
+
+    def widen(array):
+        return jnp.concatenate([array] * wide, 1)
+
+    visible = (
+        (key_segment == widen(segment))
+        | (key_segment == widen(above))
+        | (key_segment == widen(further))
+    ) & (key_place <= widen(place))
+    return jnp.where(visible, 1.0, 0.0), cosine, sine
+
+
+def turn(head, cosine, sine):
+    return head * cosine + pltpu.roll(head, HEAD_SIZE // 2, 1) * sine
+
+
+class Relay:
+    def __init__(self, me, deep, piece, up_sems, dn_sems, side_sems=None):
+        self.me, self.deep, self.piece = me, deep, piece
+        self.up_sems, self.dn_sems, self.side_sems = up_sems, dn_sems, side_sems
+
+    def up(self, source, part, hop):
+        above = self.me.at_z(jnp.minimum(self.me.z + 1, self.deep - 1))
+        at = self.piece(source, part, self.me.x)
+        return remote(at, at, self.up_sems, part * self.deep + hop, above)
+
+    def dn(self, source, part, hop):
+        below = self.me.at_z(jnp.maximum(self.me.z - 1, 0))
+        at = self.piece(source, part, self.me.x)
+        return remote(at, at, self.dn_sems, part * self.deep + hop, below)
+
+    def side(self, source, part, hop, x):
+        at = self.piece(source, part, x)
+        return remote(at, at, self.side_sems, part * 2 * self.deep + hop, self.me.x_peer())
+
+    def begin(self, part, ends=None):
+        z, last = self.me.z, self.deep - 1
+        at_end = (z == 0) | (z == last)
+        now = z >= 0 if ends is None else at_end if ends else jnp.logical_not(at_end)
+
+        @pl.when((z < last) & now)
+        def _():
+            self.up(z, part, 0).start()
+
+        @pl.when((z > 0) & now)
+        def _():
+            self.dn(z, part, 0).start()
+
+    def pass_on(self, part, hop):
+        z, deep = self.me.z, self.deep
+        sides = self.side_sems is not None
+        upward = (z - 1 - hop >= 0) & (z < deep - 1)
+        downward = (z + 1 + hop < deep) & (z > 0)
+        if sides:
+
+            @pl.when(z - 1 - hop >= 0)
+            def _():
+                self.up(z - 1 - hop, part, hop).wait_recv()
+                self.side(z - 1 - hop, part, hop, self.me.x).start()
+
+            @pl.when(z + 1 + hop < deep)
+            def _():
+                self.dn(z + 1 + hop, part, hop).wait_recv()
+                self.side(z + 1 + hop, part, deep + hop, self.me.x).start()
+
+        @pl.when(upward)
+        def _():
+            if not sides:
+                self.up(z - 1 - hop, part, hop).wait_recv()
+            self.up(z - 1 - hop, part, hop + 1).start()
+
+        @pl.when(downward)
+        def _():
+            if not sides:
+                self.dn(z + 1 + hop, part, hop).wait_recv()
+            self.dn(z + 1 + hop, part, hop + 1).start()
+
+    def finish(self, part):
+        z, deep = self.me.z, self.deep
+        for hop in range(deep - 1):
+            if self.side_sems is not None:
+
+                @pl.when(z - 1 - hop >= 0)
+                def _():
+                    self.side(z - 1 - hop, part, hop, 1 - self.me.x).wait_recv()
+
+                @pl.when(z + 1 + hop < deep)
+                def _():
+                    self.side(z + 1 + hop, part, deep + hop, 1 - self.me.x).wait_recv()
+
+            else:
+
+                @pl.when(z == deep - 1)
+                def _():
+                    self.up(z - 1 - hop, part, hop).wait_recv()
+
+                @pl.when(z == 0)
+                def _():
+                    self.dn(z + 1 + hop, part, hop).wait_recv()
+
+    def drain(self, part):
+        z, deep = self.me.z, self.deep
+        for hop in range(deep):
+
+            @pl.when((z - hop >= 0) & (z < deep - 1))
+            def _():
+                self.up(z - hop, part, hop).wait_send()
+
+            @pl.when((z + hop < deep) & (z > 0))
+            def _():
+                self.dn(z + hop, part, hop).wait_send()
+
+        if self.side_sems is not None:
+            for hop in range(deep - 1):
+
+                @pl.when(z - 1 - hop >= 0)
+                def _():
+                    self.side(z - 1 - hop, part, hop, self.me.x).wait_send()
+
+                @pl.when(z + 1 + hop < deep)
+                def _():
+                    self.side(z + 1 + hop, part, deep + hop, self.me.x).wait_send()
+
+
+class PlaneSum:
+    def __init__(self, me, rows, make, bufs, landing, sem_set):
+        self.me, self.rows, self.make = me, rows, make
+        self.core_out, self.x_out, self.acc, self.y_out = bufs
+        self.core_in, self.x_in, self.y_in = landing
+        self.core_sems, self.x_sems, self.y_sems = sem_set
+        self.tiles = rows // TILE
+        self.step = rows // CHUNKS
+        self.per_tile = TILE // self.step
+
+    def core_copy(self, number):
+        at = rows_at(number, TILE)
+        return remote(
+            self.core_out.at[at], self.core_in.at[at], self.core_sems, number, self.me.core_peer()
+        )
+
+    def x_copy(self, number):
+        at = rows_at(number, self.step)
+        return remote(self.x_out.at[at], self.x_in.at[at], self.x_sems, number, self.me.x_peer())
+
+    def y_copy(self, number):
+        at = rows_at(number, self.step)
+        return remote(self.y_out.at[at], self.y_in.at[at], self.y_sems, number, self.me.y_peer())
+
+    def tile(self, tree, x, number):
+        first = pl.multiple_of((tree * 2 + x) * self.rows + number * TILE, TILE)
+        return self.make(first)
+
+    def outward(self, side):
+        me = self.me
+        x = me.x if side else 1 - me.x
+
+        def one(number, carry):
+            value = self.tile(1 - me.c, x, number)
+            slot = side * self.tiles + number
+            self.core_out[rows_at(slot, TILE), :] = value.astype(BF16)
+            self.core_copy(slot).start()
+            return carry
+
+        lax.fori_loop(0, self.tiles, one, 0)
+
+    def across(self):
+        me = self.me
+
+        def one(number, carry):
+            value = self.tile(me.c, 1 - me.x, number).astype(BF16).astype(F32)
+            self.core_copy(number).wait_recv()
+            at = rows_at(number, TILE)
+            self.x_out[at, :] = (value + self.core_in[at, :].astype(F32)).astype(BF16)
+            for k in range(self.per_tile):
+                self.x_copy(number * self.per_tile + k).start()
+            return carry
+
+        lax.fori_loop(0, self.tiles, one, 0)
+
+    def inward(self):
+        me = self.me
+
+        def one(number, carry):
+            value = self.tile(me.c, me.x, number).astype(BF16).astype(F32)
+            slot = self.tiles + number
+            self.core_copy(slot).wait_recv()
+            self.acc[rows_at(number, TILE), :] = value + self.core_in[
+                rows_at(slot, TILE), :
+            ].astype(F32)
+            return carry
+
+        lax.fori_loop(0, self.tiles, one, 0)
+
+    def pass_on(self, first, last):
+        def one(number, carry):
+            at = rows_at(number, self.step)
+            self.x_copy(number).wait_recv()
+            self.y_out[at, :] = (self.acc[at, :] + self.x_in[at, :].astype(F32)).astype(BF16)
+            self.y_copy(number).start()
+            return carry
+
+        lax.fori_loop(first, last, one, 0)
+
+    def total(self, number):
+        at = rows_at(number, self.step)
+        self.y_copy(number).wait_recv()
+        return self.y_out[at, :].astype(F32) + self.y_in[at, :].astype(F32)
+
+    def core_sent(self):
+        for number in range(2 * self.tiles):
+            self.core_copy(number).wait_send()
+
+    def x_sent(self):
+        for number in range(CHUNKS):
+            self.x_copy(number).wait_send()
+
+    def y_sent(self):
+        for number in range(CHUNKS):
+            self.y_copy(number).wait_send()
+
+
+class Fold:
+    def __init__(self, me, groups, bufs, sem_set, tile):
+        self.me, self.groups, self.tile = me, groups, tile
+        self.own, self.stage, self.land = bufs
+        self.send_sems, self.recv_sems, self.free = sem_set
+        self.sets, self.count, self.rows = self.stage.shape[0], self.own.shape[1], self.own.shape[2]
+        z = me.z
+        self.end = jnp.where(z < 2, 0, 3)
+        self.mid = jnp.where(z < 2, 1, 2)
+        self.is_end = z == self.end
+        self.is_mid = z == self.mid
+        self.targets = (3 - self.end, 3 - self.mid, jnp.where(self.is_end, self.mid, self.end))
+
+    def place(self, target):
+        return (target + 3 - self.me.z) % 4
+
+    def free_at(self, group, which, m):
+        return self.free.at[((group % self.sets) * 3 + which) * self.count + m]
+
+    def copy(self, group, which, m, slot=None):
+        at = group % self.sets
+        target = self.targets[which]
+        there = jnp.where(self.is_end, which, (3, 3, 2)[which]) if slot is None else slot
+        return pltpu.make_async_remote_copy(
+            src_ref=self.stage.at[at, self.place(target), m],
+            dst_ref=self.land.at[at, there, m],
+            send_sem=self.send_sems.at[(at * 3 + which) * self.count + m],
+            recv_sem=self.recv_sems.at[(at * 4 + there) * self.count + m],
+            device_id=self.me.at_z(jnp.where(self.is_end, self.mid, target)),
+            device_id_type=MESH,
+        )
+
+    def send(self, group, which, m):
+        if group >= self.sets:
+            await_signal(self.free_at(group, which, m))
+        self.copy(group, which, m).start()
+
+    def used(self, group, which, m, sender):
+        if group + self.sets < self.groups:
+            signal(self.free_at(group, which, m), self.me.at_z(sender))
+
+    def begin(self, group, m, hold):
+        @pl.when(self.is_end)
+        def _():
+            for which in range(3):
+                self.send(group, which, m)
+
+        if not hold:
+
+            @pl.when(self.is_mid)
+            def _():
+                self.send(group, 2, m)
+
+    def advance(self, group, m, hold):
+        at = group % self.sets
+
+        @pl.when(self.is_mid)
+        def _():
+            for which in (0, 1):
+                self.copy(group, which, m, which).wait_recv()
+                term = self.stage.at[at, self.place(self.targets[which]), m]
+                landed = self.land.at[at, which, m]
+
+                def step(number, carry):
+                    rows = rows_at(number, self.tile)
+                    total = term[rows, :].astype(F32) + landed[rows, :].astype(F32)
+                    term[rows, :] = total.astype(BF16)
+                    return carry
+
+                lax.fori_loop(0, self.rows // self.tile, step, 0)
+                self.used(group, which, m, self.end)
+                if which == 1 or not hold:
+                    self.send(group, which, m)
+
+    def let_go(self, group, m):
+        @pl.when(self.is_mid)
+        def _():
+            self.send(group, 2, m)
+            self.send(group, 0, m)
+
+    def finish(self, group, m, write):
+        at = group % self.sets
+        for slot in (2, 3):
+            self.copy(group, 2, m, slot).wait_recv()
+        own = self.own.at[group, m]
+        near, far = self.land.at[at, 2, m], self.land.at[at, 3, m]
+
+        def step(number, carry):
+            rows = rows_at(number, self.tile)
+            total = own[rows, :].astype(F32) + near[rows, :].astype(F32)
+            write(rows, total + far[rows, :].astype(F32))
+            return carry
+
+        lax.fori_loop(0, self.rows // self.tile, step, 0)
+
+        @pl.when(self.is_end)
+        def _():
+            self.used(group, 2, m, self.mid)
+            self.used(group, 0, m, 3 - self.mid)
+
+        @pl.when(self.is_mid)
+        def _():
+            self.used(group, 2, m, self.end)
+            self.used(group, 1, m, 3 - self.mid)
+
+    def drain(self, group, m):
+        for which in range(3):
+            self.copy(group, which, m).wait_send()
+
+
+def layer_kernel(
+    starts,
+    parents,
+    frequency,
+    routes,
+    small,
+    tokens_in,
+    cotangent_in,
+    w_query,
+    w_key,
+    w_value,
+    w_output,
+    gate_in,
+    up_in,
+    down_in,
+    mixed,
+    d_tokens,
+    d_gate,
+    d_up,
+    d_down,
+    d_qo,
+    d_kv,
+    d_small,
+    mats,
+    acts,
+    hid,
+    ups,
+    wqkv,
+    wout,
+    smalls,
+    queries,
+    keys,
+    values,
+    probs,
+    context,
+    tables,
+    after,
+    mixes,
+    gates,
+    gates_out,
+    gates_in,
+    core_out,
+    x_out,
+    acc,
+    y_out,
+    two_core_in,
+    two_x_in,
+    two_y_in,
+    mo_core_in,
+    mo_x_in,
+    mo_y_in,
+    agrad,
+    alow,
+    qlow,
+    kv_out,
+    kv_in,
+    kv_own,
+    kvx_out,
+    kvx_in,
+    kvlow,
+    dkv_out,
+    dkv_in,
+    xs_in,
+    own,
+    stage,
+    land,
+    bounce,
+    own_o,
+    stage_o,
+    land_o,
+    own_q,
+    stage_q,
+    land_q,
+    small_own,
+    small_core,
+    small_x,
+    small_z,
+    kv_last,
+    load_sem,
+    small_sem,
+    up1_sem,
+    dn1_sem,
+    side1_sem,
+    up2_sem,
+    dn2_sem,
+    side2_sem,
+    up3_sem,
+    dn3_sem,
+    kv_sem,
+    cot_sem,
+    core_sem,
+    y_sem,
+    hx_sem,
+    hc_sem,
+    hf_sem,
+    mix_sem,
+    gate_sem,
+    two_core_sem,
+    two_x_sem,
+    two_y_sem,
+    mo_core_sem,
+    mo_x_sem,
+    mo_y_sem,
+    one_core_sem,
+    one_y_sem,
+    low_sem,
+    kvg_sem,
+    xs_sem,
+    fold_send,
+    fold_recv,
+    fold_free,
+    fold_send_o,
+    fold_recv_o,
+    fold_send_q,
+    fold_recv_q,
+    out_sem,
+    mixed_sem,
+    token_sem,
+    grad_sem,
+    small_c_sem,
+    small_x_sem,
+    small_z_sem,
+    last_sem,
+):
+    me = Place()
+    z, x, y, c = me.z, me.x, me.y, me.c
+    deep, shard = wqkv.shape[0], wqkv.shape[1]
+    trees, heads, rows, length = probs.shape
+    width = hid.shape[1]
+    groups = gates.shape[0]
+    units = mats.shape[1] // groups
+    mine = heads * HEAD_SIZE
+    half = shard // 2
+    step = rows // CHUNKS
+    inv_root = HEAD_SIZE ** (-0.5)
+    own_block = c * 2 + x
+    is_end = (z == 0) | (z == deep - 1)
+
+    def block_rows(tree, side):
+        return rows_at(tree * 2 + side, rows)
+
+    def shard_lanes(k):
+        return rows_at(k, shard)
+
+    def load(source, target, at):
+        return pltpu.make_async_copy(source, target, load_sem.at[at])
+
+    head_lanes = rows_at(y, HEAD_SIZE)
+    loads = [
+        load(w_query, wqkv.at[z, :, pl.ds(0, mine)], 0),
+        load(w_key.at[:, head_lanes], wqkv.at[z, :, pl.ds(mine, HEAD_SIZE)], 1),
+        load(w_value.at[:, head_lanes], wqkv.at[z, :, pl.ds(mine + HEAD_SIZE, HEAD_SIZE)], 2),
+        load(small, smalls.at[z], 3),
+        load(w_output, wout.at[z], 4),
+        load(tokens_in, alow, 5),
+        load(cotangent_in.at[0], ups.at[block_rows(0, x)], 6),
+        load(cotangent_in.at[1], ups.at[block_rows(1, x)], 7),
+        load(gate_in, mats.at[0, :, shard_lanes(z)], 8),
+        load(up_in, mats.at[1, :, shard_lanes(z)], 9),
+        load(down_in, mats.at[2, :, shard_lanes(z)], 10),
+    ]
+    for copy in loads:
+        copy.start()
+    lin = x * 4 + me.t
+
+    def plane(number):
+        return (z, number // 4, number % 4)
+
+    greet(
+        [me.at_z((z + k) % deep) for k in range(1, deep)]
+        + [plane((lin + k) % 8) for k in range(1, 8)]
+    )
+    for copy in loads[:4]:
+        copy.wait()
+
+    def halved(buffer):
+        def piece(source, part, by):
+            return buffer.at[source, rows_at(by, half)]
+
+        return piece
+
+    def expert_piece(source, part, by):
+        return mats.at[:, pl.ds(part * units, units), shard_lanes(source)]
+
+    take_qkv = Relay(me, deep, halved(wqkv), up1_sem, dn1_sem, side1_sem)
+    take_out = Relay(me, deep, halved(wout), up2_sem, dn2_sem, side2_sem)
+    take = Relay(me, deep, expert_piece, up3_sem, dn3_sem)
+
+    def small_out(k):
+        there = (z + k) % deep
+        return remote(smalls.at[z], smalls.at[z], small_sem, k - 1, me.at_z(there))
+
+    take_qkv.begin(0)
+    for k in range(1, deep):
+        small_out(k).start()
+
+    def mask(tree):
+        return agrad[:, pl.ds(tree * length, length)]
+
+    for tree in range(trees):
+        seen, cosine, sine = tree_tables(
+            starts, parents, tree, x * rows, rows, length, frequency[:1, :]
+        )
+        agrad[:, pl.ds(tree * length, length)] = seen
+        tables[0, tree] = cosine
+        tables[1, tree] = sine
+    take_qkv.pass_on(0, 0)
+    for copy in loads[4:]:
+        copy.wait()
+    take_out.begin(0)
+    for k in range(1, deep):
+        source = (z + deep - k) % deep
+        remote(
+            smalls.at[source], smalls.at[source], small_sem, k - 1, me.at_z(source)
+        ).wait_recv()
+    gain_one = jnp.concatenate([smalls[k, :1, :] for k in range(deep)], 1).astype(F32)
+    gain_two = jnp.concatenate([smalls[k, 1:2, :] for k in range(deep)], 1).astype(F32)
+    router = jnp.concatenate([smalls[k, 8:, :] for k in range(deep)], 1)
+
+    def norm_rows(source, target, at):
+        value = source[at, :].astype(F32)
+        factor = lax.rsqrt(jnp.mean(value * value, -1, keepdims=True) + EPS)
+        target[at, :] = (value * factor * gain_one).astype(BF16)
+
+    for tree in range(trees):
+
+        def first_norm(number, carry):
+            at = rows_at(number, step)
+            norm_rows(alow.at[tree], core_out.at[pl.ds(tree * rows, rows)], at)
+            return carry
+
+        lax.fori_loop(0, CHUNKS, first_norm, 0)
+    take_qkv.pass_on(0, 1)
+    take_out.pass_on(0, 0)
+    take.begin(0)
+    take_qkv.pass_on(0, 2)
+    take_qkv.finish(0)
+    take_out.pass_on(0, 1)
+
+    own_place = rows_at(x, rows)
+    away_place = rows_at(1 - x, rows)
+
+    def kv_copy(tree, which, place):
+        at = (keys, values)[which].at[tree, place]
+        return remote(at, at, kv_sem, 2 * tree + which, me.x_peer())
+
+    for tree in range(trees):
+        total = jnp.zeros((rows, wqkv.shape[2]), F32)
+        for k in range(deep):
+            total = total + mm(
+                core_out[pl.ds(tree * rows, rows), pl.ds(k * shard, shard)], wqkv[k]
+            )
+        cosine, sine = tables[0, tree], tables[1, tree]
+        for head in range(heads):
+            part_q = total[:, head * HEAD_SIZE : (head + 1) * HEAD_SIZE]
+            queries[tree, head] = turn(part_q, cosine, sine).astype(BF16)
+        part_k = total[:, mine : mine + HEAD_SIZE]
+        keys[tree, own_place, :] = turn(part_k, cosine, sine).astype(BF16)
+        values[tree, own_place, :] = total[:, mine + HEAD_SIZE :].astype(BF16)
+        for which in range(2):
+            kv_copy(tree, which, own_place).start()
+    take_out.pass_on(0, 2)
+    for tree in range(trees):
+        for which in range(2):
+            kv_copy(tree, which, away_place).wait_recv()
+
+    def attend(tree):
+        def one(head, carry):
+            score = mm(queries[tree, head], keys[tree], NT) * inv_root
+            score = jnp.where(mask(tree) > 0.5, score, NEG)
+            top = jnp.max(score, -1, keepdims=True)
+            raised = jnp.exp(score - top)
+            prob = (raised / jnp.sum(raised, -1, keepdims=True)).astype(BF16)
+            probs[tree, head] = prob
+            context[tree, head] = mm(prob, values[tree]).astype(BF16)
+            return carry
+
+        lax.fori_loop(0, heads, one, 0)
+
+    attend(0)
+    take.pass_on(0, 0)
+    take.begin(1, False)
+    for part in range(1, groups):
+        take.begin(part, True)
+    attend(1)
+    take_out.finish(0)
+
+    own_up, away_up = ups.at[block_rows(c, x)], ups.at[block_rows(c, 1 - x)]
+    peer_up = ups.at[block_rows(1 - c, 1 - x)]
+    cot_x = remote(own_up, own_up, cot_sem, 0, me.x_peer())
+    cot_x.start()
+
+    def project(tree, row):
+        pieces = []
+        for k in range(deep):
+            piece = jnp.zeros((step, shard), F32)
+            for head in range(heads):
+                piece = piece + mm(
+                    context[tree, head, pl.ds(row, step), :],
+                    wout[k, pl.ds(head * HEAD_SIZE, HEAD_SIZE), :],
+                )
+            pieces.append(piece)
+        return pieces
+
+    def core_copy(number):
+        at = rows_at(number, step)
+        return remote(core_out.at[at], mo_core_in.at[at], core_sem, number, me.core_peer())
+
+    def y_copy(number):
+        at = rows_at(number, step)
+        return remote(y_out.at[at], mo_y_in.at[at], y_sem, number, me.y_peer())
+
+    for chunk in range(CHUNKS):
+        at = pl.ds(chunk * step, step)
+        for k, piece in enumerate(project(1 - c, chunk * step)):
+            core_out[at, pl.ds(k * shard, shard)] = piece.astype(BF16)
+        core_copy(chunk).start()
+    for chunk in range(CHUNKS):
+        at = pl.ds(chunk * step, step)
+        pieces = project(c, chunk * step)
+        core_copy(chunk).wait_recv()
+        for k, piece in enumerate(pieces):
+            lanes = pl.ds(k * shard, shard)
+            both = piece.astype(BF16).astype(F32) + mo_core_in[at, lanes].astype(F32)
+            y_out[at, lanes] = both.astype(BF16)
+        y_copy(chunk).start()
+    take.pass_on(0, 1)
+
+    def two_rows(tree, side, number):
+        first = (tree * 2 + side) * rows + number * step
+        return pl.ds(pl.multiple_of(first, step), step)
+
+    def hid_copy(tree, side, sems, number, device):
+        at = hid.at[two_rows(tree, side, number)]
+        return remote(at, at, sems, number, device)
+
+    def second(number, carry):
+        at = rows_at(number, step)
+        y_copy(number).wait_recv()
+        value = alow[c, at, :].astype(F32) + (y_out[at, :].astype(F32) + mo_y_in[at, :].astype(F32))
+        after[at, :] = value
+        factor = lax.rsqrt(jnp.mean(value * value, -1, keepdims=True) + EPS)
+        hid[two_rows(c, x, number), :] = (value * factor * gain_two).astype(BF16)
+        hid_copy(c, x, hx_sem, number, me.x_peer()).start()
+        hid_copy(c, x, hc_sem, number, me.core_peer()).start()
+        return carry
+
+    lax.fori_loop(0, 2, second, 0)
+    take.pass_on(1, 0)
+    take.begin(2, False)
+    lax.fori_loop(2, CHUNKS, second, 0)
+
+    logits = mm(router, hid[block_rows(c, x), :], NT)
+    expert = lax.broadcasted_iota(jnp.int32, logits.shape, 0)
+    chosen = expert < 0
+    for k in range(routes.shape[1]):
+        chosen = chosen | (expert == routes[c, k : k + 1, :])
+    logits = jnp.where(chosen, logits, NEG)
+    raised = jnp.where(chosen, jnp.exp(logits - jnp.max(logits, 0, keepdims=True)), 0.0)
+    mixes[own_block] = raised / jnp.sum(raised, 0, keepdims=True)
+
+    def mix_copy(tree, side, at, device):
+        block = mixes.at[tree * 2 + side]
+        return remote(block, block, mix_sem, at, device)
+
+    mix_copy(c, x, 0, me.x_peer()).start()
+    mix_copy(c, x, 1, me.core_peer()).start()
+    cot_x_in = remote(away_up, away_up, cot_sem, 0, me.x_peer())
+    cot_x_in.wait_recv()
+    cot_on = remote(away_up, away_up, cot_sem, 1, me.core_peer())
+    cot_on.start()
+    for number in range(CHUNKS):
+        hid_copy(c, 1 - x, hx_sem, number, me.x_peer()).wait_recv()
+        hid_copy(c, 1 - x, hf_sem, number, me.core_peer()).start()
+    mix_copy(c, 1 - x, 0, me.x_peer()).wait_recv()
+    mix_copy(c, 1 - x, 2, me.core_peer()).start()
+    remote(peer_up, peer_up, cot_sem, 1, me.core_peer()).wait_recv()
+    for number in range(CHUNKS):
+        hid_copy(1 - c, x, hc_sem, number, me.core_peer()).wait_recv()
+        hid_copy(1 - c, 1 - x, hf_sem, number, me.core_peer()).wait_recv()
+    mix_copy(1 - c, x, 1, me.core_peer()).wait_recv()
+    mix_copy(1 - c, 1 - x, 2, me.core_peer()).wait_recv()
+    take.pass_on(1, 1)
+    take.finish(0)
+
+    def expert_block(group, block):
+        tokens = rows_at(block, rows)
+        some = pl.ds(group * units, units)
+        pre_gate = mm(mats[0, some, :], hid[tokens, :], NT)
+        pre_up = mm(mats[1, some, :], hid[tokens, :], NT)
+        back = mm(mats[2, some, :], ups[tokens, :], NT)
+        first, second_half = mixes[block, group : group + 1, :], mixes[
+            block, groups + group : groups + group + 1, :
+        ]
+        weight = jnp.broadcast_to(jnp.where(x == 0, first, second_half), (units, rows))
+        square = pre_gate * pre_gate
+        bent = jnp.tanh(ROOT_2_PI * pre_gate * (1.0 + CUBIC * square))
+        slope = 0.5 * (1.0 + bent)
+        active = pre_gate * slope
+        rise = slope + 0.5 * pre_gate * (1.0 - bent * bent) * ROOT_2_PI * (
+            1.0 + 3.0 * CUBIC * square
+        )
+        hidden = active * pre_up
+        gates[pl.ds(group, 1), tokens] = jnp.sum(hidden * back, 0, keepdims=True)
+        back = weight * back
+        acts[0, some, tokens] = (back * pre_up * rise).astype(BF16)
+        acts[1, some, tokens] = (back * active).astype(BF16)
+        acts[2, some, tokens] = (weight * hidden).astype(BF16)
+
+    fold = Fold(me, groups, (own, stage, land), (fold_send, fold_recv, fold_free), 64)
+    held_back = 2
+
+    def expert_grad(group, m):
+        source = ups if m == 2 else hid
+        some = acts.at[m, pl.ds(group * units, units)]
+
+        def one(k, carry):
+            value = mm(some[...], source[:, shard_lanes(k)]).astype(BF16)
+
+            @pl.when(k == z)
+            def _():
+                own[group, m] = value
+
+            @pl.when(k != z)
+            def _():
+                stage[group % fold.sets, fold.place(k), m] = value
+
+            return carry
+
+        lax.fori_loop(0, deep, one, 0)
+        fold.begin(group, m, group < held_back)
+
+    def expert_group(group):
+        def one(block, carry):
+            expert_block(group, block)
+            return carry
+
+        lax.fori_loop(0, 2 * trees, one, 0)
+        for m in range(KINDS):
+            expert_grad(group, m)
+
+    expert_outs = (d_gate, d_up, d_down)
+
+    def grad_out(group, m):
+        return pltpu.make_async_copy(
+            bounce.at[m], expert_outs[m].at[pl.ds(group * units, units)], grad_sem.at[m]
+        )
+
+    def finish_group(group, ends):
+        @pl.when(is_end if ends else jnp.logical_not(is_end))
+        def _():
+            for m in range(KINDS):
+                if group > 0:
+                    grad_out(group - 1, m).wait()
+
+                def write(at, value):
+                    bounce[m, at, :] = value
+
+                fold.finish(group, m, write)
+                grad_out(group, m).start()
+
+    def advance(group):
+        for m in range(KINDS):
+            fold.advance(group, m, group < held_back)
+
+    def drain(group):
+        for m in range(KINDS):
+            fold.drain(group, m)
+
+    take.pass_on(2, 0)
+    take.begin(3, False)
+    expert_group(0)
+    take.pass_on(2, 1)
+    take.pass_on(3, 0)
+    take.finish(1)
+    expert_group(1)
+    take.pass_on(3, 1)
+    advance(0)
+    take.finish(2)
+    expert_group(2)
+    finish_group(0, False)
+    advance(1)
+    for group in range(held_back):
+        for m in range(KINDS):
+            fold.let_go(group, m)
+    take.finish(3)
+
+    def two_make(first):
+        at = pl.ds(first, TILE)
+        return mm(acts[0, :, at], mats[0], TN) + mm(acts[1, :, at], mats[1], TN)
+
+    def mo_make(first):
+        return mm(acts[2, :, pl.ds(first, TILE)], mats[2], TN)
+
+    two = PlaneSum(
+        me,
+        rows,
+        two_make,
+        (core_out, x_out, acc, y_out),
+        (two_core_in, two_x_in, two_y_in),
+        (two_core_sem, two_x_sem, two_y_sem),
+    )
+    mo = PlaneSum(
+        me,
+        rows,
+        mo_make,
+        (core_out, hid.at[pl.ds(rows, rows)], acc, hid.at[pl.ds(0, rows)]),
+        (mo_core_in, mo_x_in, mo_y_in),
+        (mo_core_sem, mo_x_sem, mo_y_sem),
+    )
+    last = groups - 1
+    for number in range(CHUNKS):
+        core_copy(number).wait_send()
+        y_copy(number).wait_send()
+    expert_block(last, (1 - c) * 2 + 1 - x)
+    two.outward(0)
+    expert_block(last, (1 - c) * 2 + x)
+    two.outward(1)
+    expert_block(last, c * 2 + 1 - x)
+    two.across()
+    expert_block(last, own_block)
+
+    for block in range(2 * trees):
+        gates_out[block, pl.ds(0, groups), :] = gates[:, pl.ds(block * rows, rows)]
+
+    def gate_copy(k):
+        there = (lin + k) % 8
+        block = (there % 2) * 2 + there // 4
+        return remote(gates_out.at[block], gates_in.at[lin], gate_sem, k - 1, plane(there))
+
+    for k in range(1, 8):
+        gate_copy(k).start()
+    gates_in[lin] = gates_out[own_block]
+    two.inward()
+    finish_group(1, False)
+    drain(0)
+    expert_grad(last, 0)
+    two.pass_on(0, 1)
+    expert_grad(last, 1)
+    two.pass_on(1, 2)
+    expert_grad(last, 2)
+    two.pass_on(2, 3)
+
+    for k in range(1, 8):
+        source = (lin + 8 - k) % 8
+        remote(gates_out.at[0], gates_in.at[source], gate_sem, k - 1, plane(source)).wait_recv()
+    sums = []
+    for side in range(2):
+        total = gates_in[side * 4]
+        for k in range(1, 4):
+            total = total + gates_in[side * 4 + k]
+        sums.append(total[:groups])
+    mix_grad = jnp.concatenate(sums, 0)
+    mix = mixes[own_block]
+    picked = mix * (mix_grad - jnp.sum(mix * mix_grad, 0, keepdims=True))
+    logit_grad = picked.astype(BF16)
+    agrad[...] = mm(logit_grad, router, TN)
+    small_own[pl.ds(0, 8), :] = jnp.zeros((8, width), F32)
+    small_own[pl.ds(8, 8), :] = mm(logit_grad, hid[block_rows(c, x), :])
+
+    for number in range(CHUNKS):
+        hid_copy(c, x, hx_sem, number, me.x_peer()).wait_send()
+        hid_copy(c, x, hc_sem, number, me.core_peer()).wait_send()
+        hid_copy(c, 1 - x, hf_sem, number, me.core_peer()).wait_send()
+    two.core_sent()
+    mo.outward(0)
+    mo.outward(1)
+    two.pass_on(3, 4)
+    mo.across()
+    mo.inward()
+
+    for part in range(groups):
+        take.drain(part)
+    spare = mats.at[0]
+    late = [
+        load(tokens_in.at[0], spare.at[pl.ds(0, rows)], 0),
+        load(tokens_in.at[1], spare.at[pl.ds(rows, rows)], 1),
+    ]
+    for copy in late:
+        copy.start()
+    finish_group(0, True)
+    finish_group(1, True)
+    advance(2)
+
+    def low_copy(number):
+        at = alow.at[c, rows_at(number, step)]
+        return remote(at, at, low_sem, number, me.core_peer())
+
+    def second_norm(number, gain_grad):
+        at = rows_at(number, step)
+        upstream = two.total(number) + agrad[at, :]
+        value = after[at, :]
+        factor = lax.rsqrt(jnp.mean(value * value, -1, keepdims=True) + EPS)
+        scaled = upstream * gain_two
+        inner = jnp.mean(scaled * value, -1, keepdims=True)
+        cot = ups[two_rows(c, x, number), :]
+        total = cot.astype(F32) + (factor * scaled - value * (factor * factor * factor * inner))
+        agrad[at, :] = total
+        alow[c, at, :] = total.astype(BF16)
+        low_copy(number).start()
+        return gain_grad + jnp.sum(upstream * value * factor, 0, keepdims=True)
+
+    gain_two_grad = lax.fori_loop(0, CHUNKS, second_norm, jnp.zeros((1, width), F32))
+    small_own[pl.ds(1, 1), :] = gain_two_grad
+
+    def attend_back(tree):
+        back = jnp.zeros((rows, mine), F32)
+        for k in range(deep):
+            back = back + mm(alow[tree, :, pl.ds(k * shard, shard)], wout[k], NT)
+        back = back.astype(BF16)
+        cosine, sine = tables[0, tree], tables[1, tree]
+        key_grad = jnp.zeros((length, HEAD_SIZE), F32)
+        value_grad = jnp.zeros((length, HEAD_SIZE), F32)
+        for head in range(heads):
+            lanes = pl.ds(head * HEAD_SIZE, HEAD_SIZE)
+            back_head = back[:, head * HEAD_SIZE : (head + 1) * HEAD_SIZE]
+            prob = probs[tree, head]
+            value_grad = value_grad + mm(prob, back_head, TN)
+            prob = prob.astype(F32)
+            share = prob * mm(back_head, values[tree], NT)
+            score = (share - prob * jnp.sum(share, -1, keepdims=True)).astype(BF16)
+            query_grad = mm(score, keys[tree]) * inv_root
+            qlow[tree, :, lanes] = turn(query_grad, cosine, -sine).astype(BF16)
+            key_grad = key_grad + mm(score, queries[tree, head], TN)
+        return jnp.concatenate([key_grad * inv_root, value_grad], 1)
+
+    kv_own[...] = attend_back(c)
+    for number in range(CHUNKS):
+        at = alow.at[1 - c, pl.ds(number * step, step)]
+        remote(at, at, low_sem, number, me.core_peer()).wait_recv()
+    kv_out[...] = attend_back(1 - c).astype(BF16)
+    kvg_copy = remote(kv_out, kv_in, kvg_sem, 0, me.core_peer())
+    kvg_copy.start()
+
+    ctx = [
+        jnp.concatenate([context[tree, head] for head in range(heads)], 1) for tree in range(trees)
+    ]
+
+    def halves(value):
+        low, high = value[:half], value[half:]
+        return jnp.where(x == 0, low, high), jnp.where(x == 0, high, low)
+
+    def xs_out(k, lanes):
+        return ups.at[pl.ds(k * half, half), lanes]
+
+    xs_lanes = (pl.ds(0, mine), pl.ds(mine, mine), pl.ds(2 * mine, HEAD_SIZE))
+
+    def xs_copy(part):
+        lanes = xs_lanes[part]
+        return remote(
+            ups.at[pl.ds(0, deep * half), lanes], xs_in.at[:, lanes], xs_sem, part, me.x_peer()
+        )
+
+    cot_x.wait_send()
+    cot_on.wait_send()
+
+    def keep_own(buffer_own, buffer_stage, k, lanes, value):
+        @pl.when(k == z)
+        def _():
+            buffer_own[0, 0, :, lanes] = value.astype(BF16)
+
+        @pl.when(k != z)
+        def _():
+            buffer_stage[0, fold.place(k), 0, :, lanes] = value.astype(BF16)
+
+    def output_grad(k, carry):
+        value = sum(mm(alow[tree, :, shard_lanes(k)], ctx[tree], TN) for tree in range(trees))
+        keep, away = halves(value)
+        keep_own(own_o, stage_o, k, pl.ds(0, mine), keep)
+        ups[rows_at(k, half), xs_lanes[1]] = away.astype(BF16)
+        return carry
+
+    lax.fori_loop(0, deep, output_grad, 0)
+    xs_copy(1).start()
+
+    def one_tile(tree, at):
+        return [mm(qlow[tree, at, :], wqkv[k, :, pl.ds(0, mine)], NT) for k in range(deep)]
+
+    mo.core_sent()
+
+    def one_copy(number):
+        at = rows_at(number, step)
+        return remote(core_out.at[at], two_core_in.at[at], one_core_sem, number, me.core_peer())
+
+    def one_outward(number, carry):
+        at = rows_at(number, step)
+        for k, piece in enumerate(one_tile(1 - c, at)):
+            core_out[at, pl.ds(k * shard, shard)] = piece.astype(BF16)
+        one_copy(number).start()
+        return carry
+
+    lax.fori_loop(0, CHUNKS, one_outward, 0)
+
+    kvg_copy.wait_recv()
+
+    def of_side(ref, side):
+        low, high = ref[pl.ds(0, rows), :], ref[pl.ds(rows, rows), :]
+        return jnp.where(side == 0, low, high).astype(F32)
+
+    kvx_out[...] = (of_side(kv_own, 1 - x) + of_side(kv_in, 1 - x)).astype(BF16)
+    kvx_copy = remote(kvx_out, kvx_in, kvg_sem, 1, me.x_peer())
+    kvx_copy.start()
+
+    for copy in late:
+        copy.wait()
+    for tree in range(trees):
+
+        def norm_again(number, carry):
+            at = rows_at(number, step)
+            norm_rows(
+                spare.at[pl.ds(tree * rows, rows)], mats.at[1, pl.ds(tree * rows, rows)], at
+            )
+            return carry
+
+        lax.fori_loop(0, CHUNKS, norm_again, 0)
+
+    def hid_one(tree, lanes):
+        return mats[1, rows_at(tree, rows), lanes]
+
+    def query_weight_grad(k, carry):
+        value = sum(mm(hid_one(tree, shard_lanes(k)), qlow[tree], TN) for tree in range(trees))
+        keep, away = halves(value)
+        keep_own(own_q, stage_q, k, pl.ds(0, mine), keep)
+        ups[rows_at(k, half), xs_lanes[0]] = away.astype(BF16)
+        return carry
+
+    lax.fori_loop(0, deep, query_weight_grad, 0)
+    xs_copy(0).start()
+    kvx_copy.wait_recv()
+    own_kv = of_side(kv_own, x) + of_side(kv_in, x) + kvx_in[...].astype(F32)
+    kvlow[:, pl.ds(0, HEAD_SIZE)] = turn(
+        own_kv[:, :HEAD_SIZE], tables[0, c], -tables[1, c]
+    ).astype(BF16)
+    kvlow[:, pl.ds(HEAD_SIZE, HEAD_SIZE)] = own_kv[:, HEAD_SIZE:].astype(BF16)
+
+    two.y_sent()
+
+    def one_y(number):
+        at = rows_at(number, step)
+        return remote(y_out.at[at], two_x_in.at[at], one_y_sem, number, me.y_peer())
+
+    def one_inward(number, carry):
+        at = rows_at(number, step)
+        one_copy(number).wait_recv()
+        for k, piece in enumerate(one_tile(c, at)):
+            lanes = pl.ds(k * shard, shard)
+            piece = piece + mm(kvlow[at, :], wqkv[k, :, pl.ds(mine, 2 * HEAD_SIZE)], NT)
+            y_out[at, lanes] = (piece + two_core_in[at, lanes].astype(F32)).astype(BF16)
+        one_y(number).start()
+        return carry
+
+    lax.fori_loop(0, CHUNKS, one_inward, 0)
+
+    def kv_weight_grad(k, carry):
+        value = mm(hid_one(c, shard_lanes(k)), kvlow[...], TN)
+        low, high = value[:, :HEAD_SIZE], value[:, HEAD_SIZE:]
+        dkv_out[0, k] = jnp.where(c == 0, high, low).astype(BF16)
+        dkv_out[1, k] = jnp.where(c == 0, low, high).astype(BF16)
+        return carry
+
+    lax.fori_loop(0, deep, kv_weight_grad, 0)
+    dkv_copy = remote(dkv_out.at[0], dkv_in, kvg_sem, 2, me.core_peer())
+    dkv_copy.start()
+    dkv_copy.wait_recv()
+
+    def kv_weight_sum(k, carry):
+        keep, away = halves(dkv_out[1, k].astype(F32) + dkv_in[k].astype(F32))
+        keep_own(own_q, stage_q, k, pl.ds(mine, HEAD_SIZE), keep)
+        ups[rows_at(k, half), xs_lanes[2]] = away.astype(BF16)
+        return carry
+
+    lax.fori_loop(0, deep, kv_weight_sum, 0)
+    xs_copy(2).start()
+
+    mo.pass_on(0, CHUNKS)
+    finish_group(2, False)
+    finish_group(2, True)
+
+    fold_o = Fold(me, 1, (own_o, stage_o, land_o), (fold_send_o, fold_recv_o, None), 64)
+    fold_q = Fold(me, 1, (own_q, stage_q, land_q), (fold_send_q, fold_recv_q, None), 64)
+
+    def side_sum(buffer_own, buffer_stage, lanes_in, lanes):
+        def one(k, carry):
+            more = xs_in[rows_at(k, half), lanes_in].astype(F32)
+
+            @pl.when(k == z)
+            def _():
+                buffer_own[0, 0, :, lanes] = (
+                    buffer_own[0, 0, :, lanes].astype(F32) + more
+                ).astype(BF16)
+
+            @pl.when(k != z)
+            def _():
+                buffer_stage[0, fold.place(k), 0, :, lanes] = (
+                    buffer_stage[0, fold.place(k), 0, :, lanes].astype(F32) + more
+                ).astype(BF16)
+
+            return carry
+
+        lax.fori_loop(0, deep, one, 0)
+
+    xs_copy(1).wait_recv()
+    side_sum(own_o, stage_o, xs_lanes[1], pl.ds(0, mine))
+    fold_o.begin(0, 0, False)
+
+    def out_copies(buffer, target, first, peer_sems, number):
+        at = rows_at(number, step)
+        here = pltpu.make_async_copy(buffer.at[at], target.at[c, at], out_sem.at[first + number])
+        there = remote(buffer.at[at], target.at[c, at], peer_sems, number, me.core_peer())
+        return here, there
+
+    def first_norm_back(number, gain_grad):
+        at = rows_at(number, step)
+        one_y(number).wait_recv()
+        upstream = y_out[at, :].astype(F32) + two_x_in[at, :].astype(F32)
+        first = pl.multiple_of(c * rows + number * step, step)
+        value = mats[0, pl.ds(first, step), :].astype(F32)
+        factor = lax.rsqrt(jnp.mean(value * value, -1, keepdims=True) + EPS)
+        scaled = upstream * gain_one
+        inner = jnp.mean(scaled * value, -1, keepdims=True)
+        acc[at, :] = agrad[at, :] + (
+            factor * scaled - value * (factor * factor * factor * inner)
+        )
+        for copy in out_copies(acc, d_tokens, CHUNKS, token_sem, number):
+            copy.start()
+        return gain_grad + jnp.sum(upstream * value * factor, 0, keepdims=True)
+
+    gain_one_grad = lax.fori_loop(0, CHUNKS, first_norm_back, jnp.zeros((1, width), F32))
+    small_own[pl.ds(0, 1), :] = gain_one_grad
+    small_c = remote(small_own, small_core, small_c_sem, 0, me.core_peer())
+    small_c.start()
+    fold_o.advance(0, 0, False)
+    xs_copy(0).wait_recv()
+    side_sum(own_q, stage_q, xs_lanes[0], pl.ds(0, mine))
+    xs_copy(2).wait_recv()
+    side_sum(own_q, stage_q, xs_lanes[2], pl.ds(mine, HEAD_SIZE))
+    fold_q.begin(0, 0, False)
+    advance(3)
+
+    small_c.wait_recv()
+    small_c.wait_send()
+    small_own[...] = small_own[...] + small_core[...]
+    small_x_copy = remote(small_own, small_x, small_x_sem, 0, me.x_peer())
+    small_x_copy.start()
+
+    two.x_sent()
+
+    def mix_out(number, carry):
+        at = rows_at(number, step)
+        x_out[at, :] = (after[at, :] + mo.total(number)).astype(BF16)
+        for copy in out_copies(x_out, mixed, 0, mixed_sem, number):
+            copy.start()
+        return carry
+
+    lax.fori_loop(0, CHUNKS, mix_out, 0)
+    fold_q.advance(0, 0, False)
+    small_x_copy.wait_recv()
+    small_x_copy.wait_send()
+    small_own[...] = small_own[...] + small_x[...]
+
+    def small_copy(k):
+        there = (z + k) % deep
+        return remote(
+            small_own.at[:, shard_lanes(there)], small_z.at[z], small_z_sem, k - 1, me.at_z(there)
+        )
+
+    for k in range(1, deep):
+        small_copy(k).start()
+    small_z[z] = small_own[:, shard_lanes(z)]
+    finish_group(3, False)
+    finish_group(3, True)
+
+    def write_o(at, value):
+        d_qo[at, pl.ds(mine, mine)] = value
+
+    fold_o.finish(0, 0, write_o)
+
+    def write_q(at, value):
+        d_qo[at, pl.ds(0, mine)] = value[:, :mine]
+        kv_last[at, :] = value[:, mine:]
+
+    fold_q.finish(0, 0, write_q)
+
+    share = half // 4
+
+    def kv_columns(t):
+        return rows_at((t % 2) * 2 + t // 2, HEAD_SIZE)
+
+    def share_rows(t):
+        return pl.ds(pl.multiple_of(t * share, 8), share)
+
+    def last_copy(k):
+        there = (me.t + k) % 4
+        return remote(
+            kv_last.at[share_rows(there)],
+            d_kv.at[:, kv_columns(me.t)],
+            last_sem,
+            k - 1,
+            (z, x, there),
+        )
+
+    for k in range(1, 4):
+        last_copy(k).start()
+    d_kv[:, kv_columns(me.t)] = kv_last[share_rows(me.t), :]
+    for k in range(1, deep):
+        source = (z + deep - k) % deep
+        remote(
+            small_own.at[:, shard_lanes(0)], small_z.at[source], small_z_sem, k - 1, me.at_z(source)
+        ).wait_recv()
+    total = small_z[0]
+    for k in range(1, deep):
+        total = total + small_z[k]
+    d_small[...] = total
+    for k in range(1, 4):
+        source = (me.t + 4 - k) % 4
+        remote(
+            kv_last.at[pl.ds(0, share)],
+            d_kv.at[:, kv_columns(source)],
+            last_sem,
+            k - 1,
+            (z, x, source),
+        ).wait_recv()
+
+    for number in range(CHUNKS):
+        at = pl.ds(number * step, step)
+        remote(x_out.at[at], mixed.at[1 - c, at], mixed_sem, number, me.core_peer()).wait_recv()
+        remote(acc.at[at], d_tokens.at[1 - c, at], token_sem, number, me.core_peer()).wait_recv()
+        for buffer, target, first, peer_sems in (
+            (x_out, mixed, 0, mixed_sem),
+            (acc, d_tokens, CHUNKS, token_sem),
+        ):
+            here, there = out_copies(buffer, target, first, peer_sems, number)
+            here.wait()
+            there.wait_send()
+        one_y(number).wait_send()
+        one_copy(number).wait_send()
+        low_copy(number).wait_send()
+    mo.x_sent()
+    mo.y_sent()
+    for m in range(KINDS):
+        grad_out(groups - 1, m).wait()
+    for k in range(1, 8):
+        gate_copy(k).wait_send()
+    for k in range(1, deep):
+        small_copy(k).wait_send()
+        small_out(k).wait_send()
+    for k in range(1, 4):
+        last_copy(k).wait_send()
+    for part in range(3):
+        xs_copy(part).wait_send()
+    for copy in (kvg_copy, kvx_copy, dkv_copy):
+        copy.wait_send()
+    for tree in range(trees):
+        for which in range(2):
+            kv_copy(tree, which, own_place).wait_send()
+    mix_copy(c, x, 0, me.x_peer()).wait_send()
+    mix_copy(c, x, 1, me.core_peer()).wait_send()
+    mix_copy(c, 1 - x, 2, me.core_peer()).wait_send()
+    take_qkv.drain(0)
+    take_out.drain(0)
+    for group in range(1, groups):
+        drain(group)
+    fold_o.drain(0, 0)
+    fold_q.drain(0, 0)
+
+
+def sems(count):
+    return pltpu.SemaphoreType.DMA((2, count))
+
+
+def layer_call(
+    seg_start,
+    seg_parent,
+    routes,
+    small,
+    tokens,
+    cotangent,
+    w_query,
+    w_key,
+    w_value,
+    w_output,
+    gate_t,
+    up_t,
+    w_down,
+    deep,
+):
+    trees, rows, width = tokens.shape
+    shard, mine = w_query.shape
+    heads = mine // HEAD_SIZE
+    length = rows * 2
+    held, units = w_down.shape[0], w_down.shape[1]
+    total_units = held * units
+    experts = small.shape[0] - 8
+    blocks = 2 * trees
+    half = shard // 2
+    count = blocks * rows
+    sets = 3
+    angle = HEAD_SIZE // 2
+    frequency = ROPE_BASE ** (-2.0 * np.arange(angle, dtype=np.float32) / np.float32(HEAD_SIZE))
+    frequency = np.tile(np.concatenate([frequency] * 2)[None], (8, 1)).astype(np.float32)
+    vmem = pl.BlockSpec(memory_space=pltpu.VMEM)
+    smem = pl.BlockSpec(memory_space=pltpu.SMEM)
+    hbm = pl.BlockSpec(memory_space=pl.ANY)
+
+    def plain(*shape):
+        return pltpu.VMEM(shape, BF16)
+
+    def wide(*shape):
+        return pltpu.VMEM(shape, F32)
+
+    def out(*shape, dtype=F32):
+        return jax.ShapeDtypeStruct(shape, dtype)
+
+    lanes = 2 * mine + HEAD_SIZE
+    last = deep - 1
+    return pl.pallas_call(
+        layer_kernel,
+        out_shape=(
+            out(trees, rows, width, dtype=BF16),
+            out(trees, rows, width),
+            out(total_units, shard),
+            out(total_units, shard),
+            out(total_units, shard),
+            out(half, 2 * mine),
+            out(half // 4, 2 * KEY_VALUE_HEADS * HEAD_SIZE),
+            out(small.shape[0], shard),
+        ),
+        in_specs=[smem, smem, vmem, vmem] + [hbm] * 10,
+        out_specs=[hbm] * 5 + [vmem] * 3,
+        scratch_shapes=[
+            plain(KINDS, total_units, width),
+            plain(KINDS, total_units, count),
+            plain(count, width),
+            plain(count, width),
+            plain(deep, shard, mine + 2 * HEAD_SIZE),
+            plain(deep, mine, shard),
+            plain(deep, small.shape[0], shard),
+            plain(trees, heads, rows, HEAD_SIZE),
+            plain(trees, length, HEAD_SIZE),
+            plain(trees, length, HEAD_SIZE),
+            plain(trees, heads, rows, length),
+            plain(trees, heads, rows, HEAD_SIZE),
+            wide(2, trees, rows, HEAD_SIZE),
+            wide(rows, width),
+            wide(blocks, experts, rows),
+            wide(held, count),
+            wide(blocks, 8, rows),
+            wide(8, 8, rows),
+            plain(2 * rows, width),
+            plain(rows, width),
+            wide(rows, width),
+            plain(rows, width),
+            plain(2 * rows, width),
+            plain(rows, width),
+            plain(rows, width),
+            plain(2 * rows, width),
+            plain(rows, width),
+            plain(rows, width),
+            wide(rows, width),
+            plain(trees, rows, width),
+            plain(trees, rows, mine),
+            plain(length, 2 * HEAD_SIZE),
+            plain(length, 2 * HEAD_SIZE),
+            wide(length, 2 * HEAD_SIZE),
+            plain(rows, 2 * HEAD_SIZE),
+            plain(rows, 2 * HEAD_SIZE),
+            plain(rows, 2 * HEAD_SIZE),
+            plain(2, deep, shard, HEAD_SIZE),
+            plain(deep, shard, HEAD_SIZE),
+            plain(deep * half, lanes),
+            plain(held, KINDS, units, shard),
+            plain(sets, last, KINDS, units, shard),
+            plain(sets, deep, KINDS, units, shard),
+            wide(KINDS, units, shard),
+            plain(1, 1, half, mine),
+            plain(1, last, 1, half, mine),
+            plain(1, deep, 1, half, mine),
+            plain(1, 1, half, mine + HEAD_SIZE),
+            plain(1, last, 1, half, mine + HEAD_SIZE),
+            plain(1, deep, 1, half, mine + HEAD_SIZE),
+            wide(small.shape[0], width),
+            wide(small.shape[0], width),
+            wide(small.shape[0], width),
+            wide(deep, small.shape[0], shard),
+            wide(half, HEAD_SIZE),
+            pltpu.SemaphoreType.DMA((11,)),
+            sems(last),
+            sems(deep),
+            sems(deep),
+            sems(2 * deep),
+            sems(deep),
+            sems(deep),
+            sems(2 * deep),
+            sems(held * deep),
+            sems(held * deep),
+            sems(2 * trees),
+            sems(2),
+            sems(CHUNKS),
+            sems(CHUNKS),
+            sems(CHUNKS),
+            sems(CHUNKS),
+            sems(CHUNKS),
+            sems(3),
+            sems(7),
+            sems(2 * rows // TILE),
+            sems(CHUNKS),
+            sems(CHUNKS),
+            sems(2 * rows // TILE),
+            sems(CHUNKS),
+            sems(CHUNKS),
+            sems(CHUNKS),
+            sems(CHUNKS),
+            sems(CHUNKS),
+            sems(3),
+            sems(3),
+            pltpu.SemaphoreType.DMA((sets * 3 * KINDS,)),
+            pltpu.SemaphoreType.DMA((sets * 4 * KINDS,)),
+            pltpu.SemaphoreType.REGULAR((sets * 3 * KINDS,)),
+            pltpu.SemaphoreType.DMA((3,)),
+            pltpu.SemaphoreType.DMA((4,)),
+            pltpu.SemaphoreType.DMA((3,)),
+            pltpu.SemaphoreType.DMA((4,)),
+            pltpu.SemaphoreType.DMA((2 * CHUNKS,)),
+            sems(CHUNKS),
+            sems(CHUNKS),
+            pltpu.SemaphoreType.DMA((KINDS,)),
+            sems(1),
+            sems(1),
+            sems(last),
+            sems(3),
+        ],
+        compiler_params=pltpu.CompilerParams(
+            collective_id=0, has_side_effects=True, vmem_limit_bytes=64 * 2**20
+        ),
+        name="layer",
+    )(
+        seg_start,
+        seg_parent,
+        jnp.asarray(frequency),
+        routes,
+        small,
+        tokens,
+        cotangent,
+        w_query,
+        w_key,
+        w_value,
+        w_output,
+        gate_t.reshape(total_units, -1),
+        up_t.reshape(total_units, -1),
+        w_down.reshape(total_units, -1),
+    )
+
+
+def plane_shards(
+    tokens,
+    cotangent,
+    seg_start,
+    seg_parent,
+    routes,
+    attn_gain,
+    w_query,
+    w_key,
+    w_value,
+    w_output,
+    moe_gain,
+    w_router,
+    w_gate,
+    w_up,
+    w_down,
+):
+    width = tokens.shape[2]
+    deep = lax.axis_size("dp")
+    held, quarter = w_gate.shape[0], w_gate.shape[2]
+    mine = w_query.shape[1]
+    small = jnp.concatenate(
+        [attn_gain[None], moe_gain[None], jnp.zeros((6, attn_gain.shape[0]), BF16), w_router.T], 0
+    )
+    mixed, d_tokens, d_gate, d_up, d_down, d_qo, d_kv, d_small = layer_call(
+        seg_start,
+        seg_parent,
+        jnp.swapaxes(routes, 1, 2),
+        small,
+        tokens,
+        cotangent,
+        w_query,
+        w_key,
+        w_value,
+        w_output,
+        jnp.swapaxes(w_gate, 1, 2),
+        jnp.swapaxes(w_up, 1, 2),
+        w_down,
+        deep,
+    )
+    part = width // deep // 2
+    d_small = lax.dynamic_slice_in_dim(d_small, lax.axis_index("expert") * part, part, 1)
+    kv = KEY_VALUE_HEADS * HEAD_SIZE
+
+    def experts(array):
+        return array.reshape(held, quarter, width // deep)
+
+    return (
+        mixed,
+        d_tokens,
+        d_small[0],
+        d_qo[:, :mine],
+        d_kv[:, :kv],
+        d_kv[:, kv:],
+        d_qo[:, mine:].T,
+        d_small[1],
+        d_small[8:].T,
+        jnp.swapaxes(experts(d_gate), 1, 2),
+        jnp.swapaxes(experts(d_up), 1, 2),
+        experts(d_down),
+    )
+
+
+def shards(*arrays):
+    axes = tuple(lax.axis_size(name) for name in ("dp", "expert", "tensor"))
+    if axes == (4, 2, 4) and arrays[0].shape[0] == 2:
+        return plane_shards(*arrays)
+    return general_shards(*arrays)
 
 
 def solution(mesh):

time: 1050 us -> 322 us (0.31)
  waiting for transfers between devices: 729 us -> 0 us
  Pallas kernels: 0 us -> 302 us
  matrix products: 103 us -> 0 us
  local copies, waits for them, and re-layouts: 80.6 us -> 16.9 us
  blocking collectives: 57.8 us -> 0 us
  other arithmetic: 55.9 us -> 1.36 us
  between operations: 15.1 us -> 0.67 us
    pallas_call x0 -> x1, Pallas kernels: none -> 302 us  [layer_call(): pl.pallas_call(layer_kernel, out_shape=(out(trees, rows, width, dtype=BF1...]
    all_gather x7 -> x0, waiting for transfers between devices: 231 us -> none  [the longest x5 147 us: over_dp(): return lax.all_gather(array, 'dp', axis=axis, tiled=True)]
    unnamed x33 -> x0, waiting for transfers between devices: 204 us -> none
    psum x3 -> x0, waiting for transfers between devices: 147 us -> none  [the longest x2 108 us: to_owner(): return lax.psum(part, 'tensor').reshape(trees * rows, -1)]
    reduce_scatter x9 -> x0, waiting for transfers between devices: 147 us -> none  [the longest x2 68.7 us: to_owner(): part = lax.psum_scatter(array, 'expert', scatter_dimension=1, tiled=True)]
    dot_general x26 -> x0, matrix products: 99 us -> none  [the longest x21 90.6 us: dot(): lax.dot_general(left, right, (dims, ((), ())), preferred_element_type=F32)]
    all_gather x3 -> x0, blocking collectives: 45.3 us -> none  [the longest x1 32.7 us: over_dp(): return lax.all_gather(array, 'dp', axis=axis, tiled=True)]
    unnamed x121 -> x13, local copies, waits for them, and re-layouts: 48.4 us -> 9.31 us
  transfers between devices with their start and end apart: 27 -> 0, of which waited for: 24 -> 0; matrix products, arithmetic and copies ran while one was open for 16% -> 0% of each run, Pallas kernels for 0% -> 0%
where the time goes in v3:
time: 322 us; the launch traced here: 321 us
  Pallas kernels  302 us (94%)
  local copies, waits for them, and re-layouts  16.9 us (5%)
    pallas_call x1, Pallas kernels, layer_call(): pl.pallas_call(layer_kernel, out_shape=(out(trees, rows, width, dtype=BF1...  302 us
    unnamed x13, local copies, waits for them, and re-layouts  9.31 us

profile of v3, /device:TPU:0, one launch (start us, length us, event | category | flops | bytes accessed | tf_op | source)
XLA Modules:
  0.0 321.2 jit_solution(13760110436807108307)
XLA Ops:
  0.7 0.1 pad.2.clone
  0.7 0.7 broadcast_in_dim.9
  1.4 0.7 broadcast_in_dim.10
  2.1 1.4 pad_maximum_fusion.small
  3.5 302.3 %layer.1 = (bf16[2,256,1536]{2,1,0:T(8,128)(2,1)}, f32[2,256,1536]{2,1,0:T(8,128)}, f32[768,384]{1,0:T(8,128)}, f32[768,384]{1,0:T(8,128)}, f32[768,384]{1,0:T(8...) custom-call(s32[2,9]{1,0:T(2,128)} %starts.1, s32[2,9]{1,0:T(2,128)} %parents.1, ...), custom_call_target="tpu_custom_call" | custom-call | tf_op jit(solution)/shard_map/layer/pallas_call | solution.py:1762
  305.7 1.4 fusion.1
  307.2 1.4 dynamic-slice_bitcast_fusion
  308.6 1.5 fusion
  310.0 1.9 slice_bitcast_fusion
  311.9 0.0 copy-start
  311.9 2.8 copy.33
  314.7 0.0 copy-done
  314.7 0.0 copy-start.3
  314.7 1.7 copy.34
  316.4 0.4 copy-done.3
  316.8 0.0 copy-start.2
  316.8 1.0 copy.35
  317.8 0.7 copy-done.2
  318.5 0.0 copy-start.1
  318.5 1.0 copy.36
  319.5 0.7 copy-done.1
  320.2 1.0 copy.37
  (1 shorter events, 0.0 us)
Async XLA Ops:
  311.9 2.8 copy-start
  314.7 2.1 copy-start.3
  316.8 1.7 copy-start.2
  318.5 1.7 copy-start.1

commit v4 on v3

--- a/solution.py
+++ b/solution.py
@@ -635,17 +635,19 @@
 
 
 class Fold:
-    def __init__(self, me, groups, bufs, sem_set, tile):
-        self.me, self.groups, self.tile = me, groups, tile
+    def __init__(self, me, groups, bufs, sem_set, tile, merge):
+        self.me, self.groups, self.tile, self.merge = me, groups, tile, merge
         self.own, self.stage, self.land = bufs
         self.send_sems, self.recv_sems, self.free = sem_set
         self.sets, self.count, self.rows = self.stage.shape[0], self.own.shape[1], self.own.shape[2]
+        self.slots = self.land.shape[1]
         z = me.z
         self.end = jnp.where(z < 2, 0, 3)
         self.mid = jnp.where(z < 2, 1, 2)
+        self.far_mid = 3 - self.mid
         self.is_end = z == self.end
         self.is_mid = z == self.mid
-        self.targets = (3 - self.end, 3 - self.mid, jnp.where(self.is_end, self.mid, self.end))
+        self.targets = (3 - self.end, self.far_mid, jnp.where(self.is_end, self.mid, self.end))
 
     def place(self, target):
         return (target + 3 - self.me.z) % 4
@@ -656,13 +658,15 @@
     def copy(self, group, which, m, slot=None):
         at = group % self.sets
         target = self.targets[which]
-        there = jnp.where(self.is_end, which, (3, 3, 2)[which]) if slot is None else slot
+        from_mid = (4 if self.merge else 3, 3, 2)[which]
+        there = jnp.where(self.is_end, which, from_mid) if slot is None else slot
+        direct = self.far_mid if which == 0 and self.merge else target
         return pltpu.make_async_remote_copy(
             src_ref=self.stage.at[at, self.place(target), m],
             dst_ref=self.land.at[at, there, m],
             send_sem=self.send_sems.at[(at * 3 + which) * self.count + m],
-            recv_sem=self.recv_sems.at[(at * 4 + there) * self.count + m],
-            device_id=self.me.at_z(jnp.where(self.is_end, self.mid, target)),
+            recv_sem=self.recv_sems.at[(at * self.slots + there) * self.count + m],
+            device_id=self.me.at_z(jnp.where(self.is_end, self.mid, direct)),
             device_id_type=MESH,
         )
 
@@ -675,73 +679,119 @@
         if group + self.sets < self.groups:
             signal(self.free_at(group, which, m), self.me.at_z(sender))
 
-    def begin(self, group, m, hold):
+    def add(self, group, which, m, slot):
+        at = group % self.sets
+        self.copy(group, which, m, slot).wait_recv()
+        term = self.stage.at[at, self.place(self.targets[which]), m]
+        landed = self.land.at[at, slot, m]
+
+        def step(number, carry):
+            rows = rows_at(number, self.tile)
+            total = term[rows, :].astype(F32) + landed[rows, :].astype(F32)
+            term[rows, :] = total.astype(BF16)
+            return carry
+
+        lax.fori_loop(0, self.rows // self.tile, step, 0)
+
+    def begin(self, group, m):
         @pl.when(self.is_end)
         def _():
             for which in range(3):
                 self.send(group, which, m)
 
-        if not hold:
+        if not self.merge:
 
             @pl.when(self.is_mid)
             def _():
                 self.send(group, 2, m)
 
-    def advance(self, group, m, hold):
-        at = group % self.sets
-
+    def advance(self, group, m):
         @pl.when(self.is_mid)
         def _():
             for which in (0, 1):
-                self.copy(group, which, m, which).wait_recv()
-                term = self.stage.at[at, self.place(self.targets[which]), m]
-                landed = self.land.at[at, which, m]
-
-                def step(number, carry):
-                    rows = rows_at(number, self.tile)
-                    total = term[rows, :].astype(F32) + landed[rows, :].astype(F32)
-                    term[rows, :] = total.astype(BF16)
-                    return carry
-
-                lax.fori_loop(0, self.rows // self.tile, step, 0)
+                self.add(group, which, m, which)
                 self.used(group, which, m, self.end)
-                if which == 1 or not hold:
-                    self.send(group, which, m)
+                self.send(group, which, m)
 
     def let_go(self, group, m):
         @pl.when(self.is_mid)
         def _():
+            self.add(group, 2, m, 4)
+            self.used(group, 0, m, self.far_mid)
             self.send(group, 2, m)
-            self.send(group, 0, m)
 
     def finish(self, group, m, write):
         at = group % self.sets
-        for slot in (2, 3):
-            self.copy(group, 2, m, slot).wait_recv()
         own = self.own.at[group, m]
         near, far = self.land.at[at, 2, m], self.land.at[at, 3, m]
-
-        def step(number, carry):
-            rows = rows_at(number, self.tile)
-            total = own[rows, :].astype(F32) + near[rows, :].astype(F32)
-            write(rows, total + far[rows, :].astype(F32))
-            return carry
-
-        lax.fori_loop(0, self.rows // self.tile, step, 0)
-
-        @pl.when(self.is_end)
-        def _():
-            self.used(group, 2, m, self.mid)
-            self.used(group, 0, m, 3 - self.mid)
-
-        @pl.when(self.is_mid)
-        def _():
-            self.used(group, 2, m, self.end)
-            self.used(group, 1, m, 3 - self.mid)
+        self.copy(group, 2, m, 2).wait_recv()
+
+        def run(pieces):
+            def step(number, carry):
+                rows = rows_at(number, self.tile)
+                total = own[rows, :].astype(F32)
+                for piece in pieces:
+                    total = total + piece[rows, :].astype(F32)
+                write(rows, total)
+                return carry
+
+            lax.fori_loop(0, self.rows // self.tile, step, 0)
+
+        if self.merge:
+
+            @pl.when(self.is_end)
+            def _():
+                run([near])
+                self.used(group, 2, m, self.mid)
+
+            @pl.when(self.is_mid)
+            def _():
+                self.copy(group, 1, m, 3).wait_recv()
+                run([near, far])
+                self.used(group, 2, m, self.end)
+                self.used(group, 1, m, self.far_mid)
+
+        else:
+            self.copy(group, 1, m, 3).wait_recv()
+            run([near, far])
 
     def drain(self, group, m):
         for which in range(3):
             self.copy(group, which, m).wait_send()
+
+
+def place_kernel(*refs):
+    count = (len(refs) - 2) // 3
+    sources, targets, middles = refs[:count], refs[count : 2 * count], refs[2 * count : -2]
+    loads, stores = [], []
+    for source, target, middle in zip(sources, targets, middles):
+        size = source.shape[0] // 2
+        for part in range(2):
+            at = pl.ds(part * size, size)
+            number = len(loads)
+            loads.append(pltpu.make_async_copy(source.at[at], middle.at[at], refs[-2].at[number]))
+            stores.append(pltpu.make_async_copy(middle.at[at], target.at[at], refs[-1].at[number]))
+    for load in loads:
+        load.start()
+    for load, store in zip(loads, stores):
+        load.wait()
+        store.start()
+    for store in stores:
+        store.wait()
+
+
+def place_call(arrays):
+    hbm = pl.BlockSpec(memory_space=pl.ANY)
+    done = pltpu.SemaphoreType.DMA((2 * len(arrays),))
+    return pl.pallas_call(
+        place_kernel,
+        out_shape=tuple(jax.ShapeDtypeStruct(a.shape, a.dtype) for a in arrays),
+        in_specs=[hbm] * len(arrays),
+        out_specs=[hbm] * len(arrays),
+        scratch_shapes=[pltpu.VMEM(a.shape, a.dtype) for a in arrays] + [done, done],
+        compiler_params=pltpu.CompilerParams(vmem_limit_bytes=60 * 2**20),
+        name="place",
+    )(*arrays)
 
 
 def layer_kernel(
@@ -764,8 +814,10 @@
     d_gate,
     d_up,
     d_down,
-    d_qo,
-    d_kv,
+    d_query,
+    d_output,
+    d_key,
+    d_value,
     d_small,
     mats,
     acts,
@@ -818,10 +870,10 @@
     stage_q,
     land_q,
     small_own,
-    small_core,
-    small_x,
+    small_in,
     small_z,
     kv_last,
+    kv_land,
     load_sem,
     small_sem,
     up1_sem,
@@ -863,8 +915,7 @@
     mixed_sem,
     token_sem,
     grad_sem,
-    small_c_sem,
-    small_x_sem,
+    small_in_sem,
     small_z_sem,
     last_sem,
 ):
@@ -939,9 +990,6 @@
     take_qkv.begin(0)
     for k in range(1, deep):
         small_out(k).start()
-
-    def mask(tree):
-        return agrad[:, pl.ds(tree * length, length)]
 
     for tree in range(trees):
         seen, cosine, sine = tree_tables(
@@ -986,16 +1034,14 @@
     own_place = rows_at(x, rows)
     away_place = rows_at(1 - x, rows)
 
-    def kv_copy(tree, which, place):
+    def kv_copy(tree, which, place, on):
         at = (keys, values)[which].at[tree, place]
-        return remote(at, at, kv_sem, 2 * tree + which, me.x_peer())
-
-    for tree in range(trees):
+        return remote(at, at, kv_sem, 2 * on + which, me.core_peer() if on else me.x_peer())
+
+    def project_in(tree):
         total = jnp.zeros((rows, wqkv.shape[2]), F32)
         for k in range(deep):
-            total = total + mm(
-                core_out[pl.ds(tree * rows, rows), pl.ds(k * shard, shard)], wqkv[k]
-            )
+            total = total + mm(core_out[rows_at(tree, rows), pl.ds(k * shard, shard)], wqkv[k])
         cosine, sine = tables[0, tree], tables[1, tree]
         for head in range(heads):
             part_q = total[:, head * HEAD_SIZE : (head + 1) * HEAD_SIZE]
@@ -1003,17 +1049,22 @@
         part_k = total[:, mine : mine + HEAD_SIZE]
         keys[tree, own_place, :] = turn(part_k, cosine, sine).astype(BF16)
         values[tree, own_place, :] = total[:, mine + HEAD_SIZE :].astype(BF16)
-        for which in range(2):
-            kv_copy(tree, which, own_place).start()
+
+    project_in(c)
+    for which in range(2):
+        kv_copy(c, which, own_place, 0).start()
+    project_in(1 - c)
     take_out.pass_on(0, 2)
-    for tree in range(trees):
-        for which in range(2):
-            kv_copy(tree, which, away_place).wait_recv()
+    for which in range(2):
+        kv_copy(c, which, away_place, 0).wait_recv()
+        kv_copy(c, which, away_place, 1).start()
 
     def attend(tree):
+        mask = agrad.at[:, rows_at(tree, length)]
+
         def one(head, carry):
             score = mm(queries[tree, head], keys[tree], NT) * inv_root
-            score = jnp.where(mask(tree) > 0.5, score, NEG)
+            score = jnp.where(mask[...] > 0.5, score, NEG)
             top = jnp.max(score, -1, keepdims=True)
             raised = jnp.exp(score - top)
             prob = (raised / jnp.sum(raised, -1, keepdims=True)).astype(BF16)
@@ -1023,12 +1074,14 @@
 
         lax.fori_loop(0, heads, one, 0)
 
-    attend(0)
+    attend(c)
     take.pass_on(0, 0)
     take.begin(1, False)
     for part in range(1, groups):
         take.begin(part, True)
-    attend(1)
+    for which in range(2):
+        kv_copy(1 - c, which, away_place, 1).wait_recv()
+    attend(1 - c)
     take_out.finish(0)
 
     own_up, away_up = ups.at[block_rows(c, x)], ups.at[block_rows(c, 1 - x)]
@@ -1153,8 +1206,7 @@
         acts[1, some, tokens] = (back * active).astype(BF16)
         acts[2, some, tokens] = (weight * hidden).astype(BF16)
 
-    fold = Fold(me, groups, (own, stage, land), (fold_send, fold_recv, fold_free), 64)
-    held_back = 2
+    fold = Fold(me, groups, (own, stage, land), (fold_send, fold_recv, fold_free), 64, True)
 
     def expert_grad(group, m):
         source = ups if m == 2 else hid
@@ -1174,7 +1226,7 @@
             return carry
 
         lax.fori_loop(0, deep, one, 0)
-        fold.begin(group, m, group < held_back)
+        fold.begin(group, m)
 
     def expert_group(group):
         def one(block, carry):
@@ -1207,7 +1259,11 @@
 
     def advance(group):
         for m in range(KINDS):
-            fold.advance(group, m, group < held_back)
+            fold.advance(group, m)
+
+    def let_go(group):
+        for m in range(KINDS):
+            fold.let_go(group, m)
 
     def drain(group):
         for m in range(KINDS):
@@ -1226,9 +1282,7 @@
     expert_group(2)
     finish_group(0, False)
     advance(1)
-    for group in range(held_back):
-        for m in range(KINDS):
-            fold.let_go(group, m)
+    let_go(0)
     take.finish(3)
 
     def two_make(first):
@@ -1279,6 +1333,7 @@
     gates_in[lin] = gates_out[own_block]
     two.inward()
     finish_group(1, False)
+    let_go(1)
     drain(0)
     expert_grad(last, 0)
     two.pass_on(0, 1)
@@ -1324,9 +1379,6 @@
     ]
     for copy in late:
         copy.start()
-    finish_group(0, True)
-    finish_group(1, True)
-    advance(2)
 
     def low_copy(number):
         at = alow.at[c, rows_at(number, step)]
@@ -1370,13 +1422,14 @@
             key_grad = key_grad + mm(score, queries[tree, head], TN)
         return jnp.concatenate([key_grad * inv_root, value_grad], 1)
 
-    kv_own[...] = attend_back(c)
     for number in range(CHUNKS):
         at = alow.at[1 - c, pl.ds(number * step, step)]
         remote(at, at, low_sem, number, me.core_peer()).wait_recv()
     kv_out[...] = attend_back(1 - c).astype(BF16)
     kvg_copy = remote(kv_out, kv_in, kvg_sem, 0, me.core_peer())
     kvg_copy.start()
+    kv_own[...] = attend_back(c)
+    advance(2)
 
     ctx = [
         jnp.concatenate([context[tree, head] for head in range(heads)], 1) for tree in range(trees)
@@ -1519,11 +1572,14 @@
     xs_copy(2).start()
 
     mo.pass_on(0, CHUNKS)
+    finish_group(0, True)
+    finish_group(1, True)
+    let_go(2)
     finish_group(2, False)
-    finish_group(2, True)
-
-    fold_o = Fold(me, 1, (own_o, stage_o, land_o), (fold_send_o, fold_recv_o, None), 64)
-    fold_q = Fold(me, 1, (own_q, stage_q, land_q), (fold_send_q, fold_recv_q, None), 64)
+    advance(3)
+
+    fold_o = Fold(me, 1, (own_o, stage_o, land_o), (fold_send_o, fold_recv_o, None), 64, False)
+    fold_q = Fold(me, 1, (own_q, stage_q, land_q), (fold_send_q, fold_recv_q, None), 64, False)
 
     def side_sum(buffer_own, buffer_stage, lanes_in, lanes):
         def one(k, carry):
@@ -1547,7 +1603,7 @@
 
     xs_copy(1).wait_recv()
     side_sum(own_o, stage_o, xs_lanes[1], pl.ds(0, mine))
-    fold_o.begin(0, 0, False)
+    fold_o.begin(0, 0)
 
     def out_copies(buffer, target, first, peer_sems, number):
         at = rows_at(number, step)
@@ -1573,21 +1629,24 @@
 
     gain_one_grad = lax.fori_loop(0, CHUNKS, first_norm_back, jnp.zeros((1, width), F32))
     small_own[pl.ds(0, 1), :] = gain_one_grad
-    small_c = remote(small_own, small_core, small_c_sem, 0, me.core_peer())
-    small_c.start()
-    fold_o.advance(0, 0, False)
+    spot = x * 2 + c
+
+    def spread(k):
+        there = (spot + k) % 4
+        device = (z, there // 2, 2 * y + there % 2)
+        return remote(small_own, small_in.at[spot], small_in_sem, k - 1, device)
+
+    for k in range(1, 4):
+        spread(k).start()
+    small_in[spot] = small_own[...]
+    fold_o.advance(0, 0)
     xs_copy(0).wait_recv()
     side_sum(own_q, stage_q, xs_lanes[0], pl.ds(0, mine))
     xs_copy(2).wait_recv()
     side_sum(own_q, stage_q, xs_lanes[2], pl.ds(mine, HEAD_SIZE))
-    fold_q.begin(0, 0, False)
-    advance(3)
-
-    small_c.wait_recv()
-    small_c.wait_send()
-    small_own[...] = small_own[...] + small_core[...]
-    small_x_copy = remote(small_own, small_x, small_x_sem, 0, me.x_peer())
-    small_x_copy.start()
+    fold_q.begin(0, 0)
+    let_go(3)
+    finish_group(2, True)
 
     two.x_sent()
 
@@ -1599,10 +1658,13 @@
         return carry
 
     lax.fori_loop(0, CHUNKS, mix_out, 0)
-    fold_q.advance(0, 0, False)
-    small_x_copy.wait_recv()
-    small_x_copy.wait_send()
-    small_own[...] = small_own[...] + small_x[...]
+    fold_q.advance(0, 0)
+    for k in range(1, 4):
+        source = (spot + 4 - k) % 4
+        device = (z, source // 2, 2 * y + source % 2)
+        remote(small_own, small_in.at[source], small_in_sem, k - 1, device).wait_recv()
+        spread(k).wait_send()
+    small_own[...] = (small_in[0] + small_in[1]) + (small_in[2] + small_in[3])
 
     def small_copy(k):
         there = (z + k) % deep
@@ -1617,20 +1679,17 @@
     finish_group(3, True)
 
     def write_o(at, value):
-        d_qo[at, pl.ds(mine, mine)] = value
+        d_output[at, :] = value
 
     fold_o.finish(0, 0, write_o)
 
     def write_q(at, value):
-        d_qo[at, pl.ds(0, mine)] = value[:, :mine]
+        d_query[at, :] = value[:, :mine]
         kv_last[at, :] = value[:, mine:]
 
     fold_q.finish(0, 0, write_q)
 
     share = half // 4
-
-    def kv_columns(t):
-        return rows_at((t % 2) * 2 + t // 2, HEAD_SIZE)
 
     def share_rows(t):
         return pl.ds(pl.multiple_of(t * share, 8), share)
@@ -1638,16 +1697,12 @@
     def last_copy(k):
         there = (me.t + k) % 4
         return remote(
-            kv_last.at[share_rows(there)],
-            d_kv.at[:, kv_columns(me.t)],
-            last_sem,
-            k - 1,
-            (z, x, there),
+            kv_last.at[share_rows(there)], kv_land.at[me.t], last_sem, k - 1, (z, x, there)
         )
 
     for k in range(1, 4):
         last_copy(k).start()
-    d_kv[:, kv_columns(me.t)] = kv_last[share_rows(me.t), :]
+    kv_land[me.t] = kv_last[share_rows(me.t), :]
     for k in range(1, deep):
         source = (z + deep - k) % deep
         remote(
@@ -1656,16 +1711,16 @@
     total = small_z[0]
     for k in range(1, deep):
         total = total + small_z[k]
-    d_small[...] = total
+    d_small[...] = jnp.where(x == 0, total[:, :half], total[:, half:])
     for k in range(1, 4):
         source = (me.t + 4 - k) % 4
         remote(
-            kv_last.at[pl.ds(0, share)],
-            d_kv.at[:, kv_columns(source)],
-            last_sem,
-            k - 1,
-            (z, x, source),
+            kv_last.at[pl.ds(0, share)], kv_land.at[source], last_sem, k - 1, (z, x, source)
         ).wait_recv()
+    for head in range(KEY_VALUE_HEADS):
+        lanes = pl.ds(head * HEAD_SIZE, HEAD_SIZE)
+        d_key[:, lanes] = kv_land[2 * head]
+        d_value[:, lanes] = kv_land[2 * head + 1]
 
     for number in range(CHUNKS):
         at = pl.ds(number * step, step)
@@ -1696,9 +1751,9 @@
         xs_copy(part).wait_send()
     for copy in (kvg_copy, kvx_copy, dkv_copy):
         copy.wait_send()
-    for tree in range(trees):
-        for which in range(2):
-            kv_copy(tree, which, own_place).wait_send()
+    for which in range(2):
+        kv_copy(c, which, own_place, 0).wait_send()
+        kv_copy(c, which, away_place, 1).wait_send()
     mix_copy(c, x, 0, me.x_peer()).wait_send()
     mix_copy(c, x, 1, me.core_peer()).wait_send()
     mix_copy(c, 1 - x, 2, me.core_peer()).wait_send()
@@ -1767,12 +1822,14 @@
             out(total_units, shard),
             out(total_units, shard),
             out(total_units, shard),
-            out(half, 2 * mine),
-            out(half // 4, 2 * KEY_VALUE_HEADS * HEAD_SIZE),
-            out(small.shape[0], shard),
+            out(half, mine),
+            out(half, mine),
+            out(half // 4, KEY_VALUE_HEADS * HEAD_SIZE),
+            out(half // 4, KEY_VALUE_HEADS * HEAD_SIZE),
+            out(small.shape[0], half),
         ),
         in_specs=[smem, smem, vmem, vmem] + [hbm] * 10,
-        out_specs=[hbm] * 5 + [vmem] * 3,
+        out_specs=[hbm] * 5 + [vmem] * 5,
         scratch_shapes=[
             plain(KINDS, total_units, width),
             plain(KINDS, total_units, count),
@@ -1816,7 +1873,7 @@
             plain(deep * half, lanes),
             plain(held, KINDS, units, shard),
             plain(sets, last, KINDS, units, shard),
-            plain(sets, deep, KINDS, units, shard),
+            plain(sets, 5, KINDS, units, shard),
             wide(KINDS, units, shard),
             plain(1, 1, half, mine),
             plain(1, last, 1, half, mine),
@@ -1825,10 +1882,10 @@
             plain(1, last, 1, half, mine + HEAD_SIZE),
             plain(1, deep, 1, half, mine + HEAD_SIZE),
             wide(small.shape[0], width),
-            wide(small.shape[0], width),
-            wide(small.shape[0], width),
+            wide(4, small.shape[0], width),
             wide(deep, small.shape[0], shard),
             wide(half, HEAD_SIZE),
+            wide(4, half // 4, HEAD_SIZE),
             pltpu.SemaphoreType.DMA((11,)),
             sems(last),
             sems(deep),
@@ -1860,7 +1917,7 @@
             sems(3),
             sems(3),
             pltpu.SemaphoreType.DMA((sets * 3 * KINDS,)),
-            pltpu.SemaphoreType.DMA((sets * 4 * KINDS,)),
+            pltpu.SemaphoreType.DMA((sets * 5 * KINDS,)),
             pltpu.SemaphoreType.REGULAR((sets * 3 * KINDS,)),
             pltpu.SemaphoreType.DMA((3,)),
             pltpu.SemaphoreType.DMA((4,)),
@@ -1870,8 +1927,7 @@
             sems(CHUNKS),
             sems(CHUNKS),
             pltpu.SemaphoreType.DMA((KINDS,)),
-            sems(1),
-            sems(1),
+            sems(3),
             sems(last),
             sems(3),
         ],
@@ -1917,11 +1973,10 @@
     width = tokens.shape[2]
     deep = lax.axis_size("dp")
     held, quarter = w_gate.shape[0], w_gate.shape[2]
-    mine = w_query.shape[1]
     small = jnp.concatenate(
         [attn_gain[None], moe_gain[None], jnp.zeros((6, attn_gain.shape[0]), BF16), w_router.T], 0
     )
-    mixed, d_tokens, d_gate, d_up, d_down, d_qo, d_kv, d_small = layer_call(
+    made = layer_call(
         seg_start,
         seg_parent,
         jnp.swapaxes(routes, 1, 2),
@@ -1937,9 +1992,9 @@
         w_down,
         deep,
     )
-    part = width // deep // 2
-    d_small = lax.dynamic_slice_in_dim(d_small, lax.axis_index("expert") * part, part, 1)
-    kv = KEY_VALUE_HEADS * HEAD_SIZE
+    placed = place_call(made[:-1])
+    mixed, d_tokens, d_gate, d_up, d_down, d_query, d_output, d_key, d_value = placed
+    d_small = made[-1]
 
     def experts(array):
         return array.reshape(held, quarter, width // deep)
@@ -1948,10 +2003,10 @@
         mixed,
         d_tokens,
         d_small[0],
-        d_qo[:, :mine],
-        d_kv[:, :kv],
-        d_kv[:, kv:],
-        d_qo[:, mine:].T,
+        d_query,
+        d_key,
+        d_value,
+        d_output.T,
         d_small[1],
         d_small[8:].T,
         jnp.swapaxes(experts(d_gate), 1, 2),

time: 322 us -> 276 us (0.86)
  Pallas kernels: 302 us -> 270 us
  local copies, waits for them, and re-layouts: 16.9 us -> 2.62 us
    pallas_call x1, Pallas kernels: 302 us -> 262 us  [layer_call(): pl.pallas_call(layer_kernel, out_shape=(out(trees, rows, width, dtype=BF1...]
    unnamed x13 -> x2, local copies, waits for them, and re-layouts: 9.31 us -> 0.01 us
    pallas_call x0 -> x1, Pallas kernels: none -> 7.06 us  [place_call(): pl.pallas_call(place_kernel, out_shape=tuple((jax.ShapeDtypeStruct(a.shap...]
where the time goes in v4:
time: 276 us; the launch traced here: 274 us
  Pallas kernels  270 us (98%)
    pallas_call x1, Pallas kernels, layer_call(): pl.pallas_call(layer_kernel, out_shape=(out(trees, rows, width, dtype=BF1...  262 us
    pallas_call x1, Pallas kernels, place_call(): pl.pallas_call(place_kernel, out_shape=tuple((jax.ShapeDtypeStruct(a.shap...  7.06 us

profile of v4, /device:TPU:0, one launch (start us, length us, event | category | flops | bytes accessed | tf_op | source)
XLA Modules:
  0.0 274.2 jit_solution(13381423008045951610)
XLA Ops:
  0.7 0.1 pad.2.clone
  0.7 0.7 broadcast_in_dim.9
  1.4 0.7 broadcast_in_dim.10
  2.1 1.4 pad_maximum_fusion.small
  3.5 262.5 %layer.1 = (bf16[2,256,1536]{2,1,0:T(8,128)(2,1)}, f32[2,256,1536]{2,1,0:T(8,128)}, f32[768,384]{1,0:T(8,128)}, f32[768,384]{1,0:T(8,128)}, f32[768,384]{1,0:T(8...) custom-call(s32[2,9]{1,0:T(2,128)} %starts.1, ...), custom_call_target="tpu_custom_call" | custom-call | tf_op jit(solution)/shard_map/layer/pallas_call | solution.py:1817
  265.9 0.0 copy-start
  265.9 7.1 %place.1 = (bf16[2,256,1536]{2,1,0:T(8,128)(2,1)}, f32[2,256,1536]{2,1,0:T(8,128)}, f32[768,384]{1,0:T(8,128)}, f32[768,384]{1,0:T(8,128)}, f32[768,384]{1,0:T(8...) custom-call(bf16[2,256,1536]{2,1,0:T(8,128)(2,1)} %get-tuple-element.31.refs_0_, ...), custom_call_target="tpu_custom_call" | custom-call | tf_op jit(solution)/shard_map/place/pallas_call | solution.py:786
  273.0 0.0 copy-done
  273.0 0.6 fusion
  273.6 0.6 slice_bitcast_fusion
  (1 shorter events, 0.0 us)
Async XLA Ops:
  265.9 7.1 %copy-start = (f32[16,192]{1,0:T(8,128)S(1)}, f32[16,192]{1,0:T(8,128)}, u32[]{:S(2)}) copy-start(f32[16,192]{1,0:T(8,128)} %get-tuple-element.42) | copy-start | bytes 36868

commit v5 on v4

--- a/solution.py
+++ b/solution.py
@@ -538,8 +538,8 @@
 
 
 class PlaneSum:
-    def __init__(self, me, rows, make, bufs, landing, sem_set):
-        self.me, self.rows, self.make = me, rows, make
+    def __init__(self, me, rows, make, bufs, landing, sem_set, ahead=None):
+        self.me, self.rows, self.make, self.ahead = me, rows, make, ahead
         self.core_out, self.x_out, self.acc, self.y_out = bufs
         self.core_in, self.x_in, self.y_in = landing
         self.core_sems, self.x_sems, self.y_sems = sem_set
@@ -561,18 +561,41 @@
         at = rows_at(number, self.step)
         return remote(self.y_out.at[at], self.y_in.at[at], self.y_sems, number, self.me.y_peer())
 
-    def tile(self, tree, x, number):
-        first = pl.multiple_of((tree * 2 + x) * self.rows + number * TILE, TILE)
-        return self.make(first)
+    def first(self, tree, x, number):
+        return pl.multiple_of((tree * 2 + x) * self.rows + number * TILE, TILE)
+
+    def tile(self, tree, x, number, buffer, at):
+        value = self.make(self.first(tree, x, number))
+        if self.ahead is not None:
+            value = value + buffer[at, :].astype(F32)
+        return value.astype(BF16)
+
+    def prepare(self):
+        me = self.me
+
+        def other(number, carry):
+            x = jnp.where(number < self.tiles, 1 - me.x, me.x)
+            value = self.ahead(self.first(1 - me.c, x, number % self.tiles))
+            self.core_out[rows_at(number, TILE), :] = value.astype(BF16)
+            return carry
+
+        def same(number, carry):
+            at = rows_at(number, TILE)
+            self.x_out[at, :] = self.ahead(self.first(me.c, 1 - me.x, number)).astype(BF16)
+            self.acc[at, :] = self.ahead(self.first(me.c, me.x, number))
+            return carry
+
+        lax.fori_loop(0, 2 * self.tiles, other, 0)
+        lax.fori_loop(0, self.tiles, same, 0)
 
     def outward(self, side):
         me = self.me
         x = me.x if side else 1 - me.x
 
         def one(number, carry):
-            value = self.tile(1 - me.c, x, number)
             slot = side * self.tiles + number
-            self.core_out[rows_at(slot, TILE), :] = value.astype(BF16)
+            at = rows_at(slot, TILE)
+            self.core_out[at, :] = self.tile(1 - me.c, x, number, self.core_out, at)
             self.core_copy(slot).start()
             return carry
 
@@ -582,9 +605,9 @@
         me = self.me
 
         def one(number, carry):
-            value = self.tile(me.c, 1 - me.x, number).astype(BF16).astype(F32)
+            at = rows_at(number, TILE)
+            value = self.tile(me.c, 1 - me.x, number, self.x_out, at).astype(F32)
             self.core_copy(number).wait_recv()
-            at = rows_at(number, TILE)
             self.x_out[at, :] = (value + self.core_in[at, :].astype(F32)).astype(BF16)
             for k in range(self.per_tile):
                 self.x_copy(number * self.per_tile + k).start()
@@ -596,12 +619,11 @@
         me = self.me
 
         def one(number, carry):
-            value = self.tile(me.c, me.x, number).astype(BF16).astype(F32)
+            at = rows_at(number, TILE)
+            value = self.tile(me.c, me.x, number, self.acc, at).astype(F32)
             slot = self.tiles + number
             self.core_copy(slot).wait_recv()
-            self.acc[rows_at(number, TILE), :] = value + self.core_in[
-                rows_at(slot, TILE), :
-            ].astype(F32)
+            self.acc[at, :] = value + self.core_in[rows_at(slot, TILE), :].astype(F32)
             return carry
 
         lax.fori_loop(0, self.tiles, one, 0)
@@ -856,9 +878,13 @@
     kvx_out,
     kvx_in,
     kvlow,
+    kvlow_x,
+    qlow_x,
+    hidx,
+    alx,
+    ctx_x,
     dkv_out,
     dkv_in,
-    xs_in,
     own,
     stage,
     land,
@@ -903,7 +929,10 @@
     one_y_sem,
     low_sem,
     kvg_sem,
-    xs_sem,
+    qx_sem,
+    hidx_sem,
+    alx_sem,
+    ctx_sem,
     fold_send,
     fold_recv,
     fold_free,
@@ -1055,6 +1084,11 @@
         kv_copy(c, which, own_place, 0).start()
     project_in(1 - c)
     take_out.pass_on(0, 2)
+
+    own_up, away_up = ups.at[block_rows(c, x)], ups.at[block_rows(c, 1 - x)]
+    peer_up = ups.at[block_rows(1 - c, 1 - x)]
+    cot_x = remote(own_up, own_up, cot_sem, 0, me.x_peer())
+    cot_x.start()
     for which in range(2):
         kv_copy(c, which, away_place, 0).wait_recv()
         kv_copy(c, which, away_place, 1).start()
@@ -1083,11 +1117,6 @@
         kv_copy(1 - c, which, away_place, 1).wait_recv()
     attend(1 - c)
     take_out.finish(0)
-
-    own_up, away_up = ups.at[block_rows(c, x)], ups.at[block_rows(c, 1 - x)]
-    peer_up = ups.at[block_rows(1 - c, 1 - x)]
-    cot_x = remote(own_up, own_up, cot_sem, 0, me.x_peer())
-    cot_x.start()
 
     def project(tree, row):
         pieces = []
@@ -1180,6 +1209,32 @@
     mix_copy(1 - c, x, 1, me.core_peer()).wait_recv()
     mix_copy(1 - c, 1 - x, 2, me.core_peer()).wait_recv()
     take.pass_on(1, 1)
+
+    def half_lanes(k, side):
+        first = k * shard + side * HEAD_SIZE
+        return pl.ds(pl.multiple_of(first, HEAD_SIZE), 2 * HEAD_SIZE)
+
+    def cross(source, landing, tree, k, on, sems):
+        at = landing.at[tree, k]
+        if on:
+            return remote(at, at, sems, deep + k, me.core_peer())
+        return remote(source.at[:, half_lanes(k, 1 - x)], at, sems, k, me.x_peer())
+
+    def hidx_copy(tree, k, on):
+        return cross(x_out, hidx, tree, k, on, hidx_sem)
+
+    def alx_copy(tree, k, on):
+        return cross(alow.at[tree], alx, tree, k, on, alx_sem)
+
+    def again(number, carry):
+        norm_rows(alow.at[c], x_out, rows_at(number, step))
+        return carry
+
+    lax.fori_loop(0, CHUNKS, again, 0)
+    for k in range(deep):
+        hidx_copy(c, k, 0).start()
+    ctx_copy = remote(context, ctx_x, ctx_sem, 0, me.x_peer())
+    ctx_copy.start()
     take.finish(0)
 
     def expert_block(group, block):
@@ -1257,8 +1312,8 @@
                 fold.finish(group, m, write)
                 grad_out(group, m).start()
 
-    def advance(group):
-        for m in range(KINDS):
+    def advance(group, kinds=range(KINDS)):
+        for m in kinds:
             fold.advance(group, m)
 
     def let_go(group):
@@ -1277,17 +1332,25 @@
     take.finish(1)
     expert_group(1)
     take.pass_on(3, 1)
+    for k in range(deep):
+        hidx_copy(c, k, 0).wait_recv()
+        hidx_copy(c, k, 1).start()
     advance(0)
     take.finish(2)
     expert_group(2)
     finish_group(0, False)
-    advance(1)
-    let_go(0)
-    take.finish(3)
+    last = groups - 1
+
+    def two_units(first, some):
+        at = pl.ds(first, TILE)
+        total = mm(acts[0, some, at], mats[0, some, :], TN)
+        return total + mm(acts[1, some, at], mats[1, some, :], TN)
+
+    def two_ahead(first):
+        return two_units(first, pl.ds(0, last * units))
 
     def two_make(first):
-        at = pl.ds(first, TILE)
-        return mm(acts[0, :, at], mats[0], TN) + mm(acts[1, :, at], mats[1], TN)
+        return two_units(first, pl.ds(last * units, units))
 
     def mo_make(first):
         return mm(acts[2, :, pl.ds(first, TILE)], mats[2], TN)
@@ -1299,6 +1362,7 @@
         (core_out, x_out, acc, y_out),
         (two_core_in, two_x_in, two_y_in),
         (two_core_sem, two_x_sem, two_y_sem),
+        two_ahead,
     )
     mo = PlaneSum(
         me,
@@ -1308,10 +1372,15 @@
         (mo_core_in, mo_x_in, mo_y_in),
         (mo_core_sem, mo_x_sem, mo_y_sem),
     )
-    last = groups - 1
     for number in range(CHUNKS):
         core_copy(number).wait_send()
         y_copy(number).wait_send()
+    for k in range(deep):
+        hidx_copy(c, k, 0).wait_send()
+    two.prepare()
+    advance(1)
+    let_go(0)
+    take.finish(3)
     expert_block(last, (1 - c) * 2 + 1 - x)
     two.outward(0)
     expert_block(last, (1 - c) * 2 + x)
@@ -1332,8 +1401,6 @@
         gate_copy(k).start()
     gates_in[lin] = gates_out[own_block]
     two.inward()
-    finish_group(1, False)
-    let_go(1)
     drain(0)
     expert_grad(last, 0)
     two.pass_on(0, 1)
@@ -1341,6 +1408,7 @@
     two.pass_on(1, 2)
     expert_grad(last, 2)
     two.pass_on(2, 3)
+    advance(2, [0])
 
     for k in range(1, 8):
         source = (lin + 8 - k) % 8
@@ -1363,22 +1431,11 @@
         hid_copy(c, x, hx_sem, number, me.x_peer()).wait_send()
         hid_copy(c, x, hc_sem, number, me.core_peer()).wait_send()
         hid_copy(c, 1 - x, hf_sem, number, me.core_peer()).wait_send()
+    two.pass_on(3, 4)
     two.core_sent()
     mo.outward(0)
     mo.outward(1)
-    two.pass_on(3, 4)
-    mo.across()
-    mo.inward()
-
-    for part in range(groups):
-        take.drain(part)
-    spare = mats.at[0]
-    late = [
-        load(tokens_in.at[0], spare.at[pl.ds(0, rows)], 0),
-        load(tokens_in.at[1], spare.at[pl.ds(rows, rows)], 1),
-    ]
-    for copy in late:
-        copy.start()
+    advance(2, [1])
 
     def low_copy(number):
         at = alow.at[c, rows_at(number, step)]
@@ -1400,6 +1457,8 @@
 
     gain_two_grad = lax.fori_loop(0, CHUNKS, second_norm, jnp.zeros((1, width), F32))
     small_own[pl.ds(1, 1), :] = gain_two_grad
+    for k in range(deep):
+        alx_copy(c, k, 0).start()
 
     def attend_back(tree):
         back = jnp.zeros((rows, mine), F32)
@@ -1429,48 +1488,18 @@
     kvg_copy = remote(kv_out, kv_in, kvg_sem, 0, me.core_peer())
     kvg_copy.start()
     kv_own[...] = attend_back(c)
-    advance(2)
-
-    ctx = [
-        jnp.concatenate([context[tree, head] for head in range(heads)], 1) for tree in range(trees)
-    ]
-
-    def halves(value):
-        low, high = value[:half], value[half:]
-        return jnp.where(x == 0, low, high), jnp.where(x == 0, high, low)
-
-    def xs_out(k, lanes):
-        return ups.at[pl.ds(k * half, half), lanes]
-
-    xs_lanes = (pl.ds(0, mine), pl.ds(mine, mine), pl.ds(2 * mine, HEAD_SIZE))
-
-    def xs_copy(part):
-        lanes = xs_lanes[part]
-        return remote(
-            ups.at[pl.ds(0, deep * half), lanes], xs_in.at[:, lanes], xs_sem, part, me.x_peer()
-        )
-
-    cot_x.wait_send()
-    cot_on.wait_send()
-
-    def keep_own(buffer_own, buffer_stage, k, lanes, value):
-        @pl.when(k == z)
-        def _():
-            buffer_own[0, 0, :, lanes] = value.astype(BF16)
-
-        @pl.when(k != z)
-        def _():
-            buffer_stage[0, fold.place(k), 0, :, lanes] = value.astype(BF16)
-
-    def output_grad(k, carry):
-        value = sum(mm(alow[tree, :, shard_lanes(k)], ctx[tree], TN) for tree in range(trees))
-        keep, away = halves(value)
-        keep_own(own_o, stage_o, k, pl.ds(0, mine), keep)
-        ups[rows_at(k, half), xs_lanes[1]] = away.astype(BF16)
-        return carry
-
-    lax.fori_loop(0, deep, output_grad, 0)
-    xs_copy(1).start()
+
+    def of_side(ref, side):
+        low, high = ref[pl.ds(0, rows), :], ref[pl.ds(rows, rows), :]
+        return jnp.where(side == 0, low, high).astype(F32)
+
+    kvg_copy.wait_recv()
+    kvx_out[...] = (of_side(kv_own, 1 - x) + of_side(kv_in, 1 - x)).astype(BF16)
+    kvx_copy = remote(kvx_out, kvx_in, kvg_sem, 1, me.x_peer())
+    kvx_copy.start()
+    qx_copy = remote(qlow, qlow_x, qx_sem, 0, me.x_peer())
+    qx_copy.start()
+    advance(2, [2])
 
     def one_tile(tree, at):
         return [mm(qlow[tree, at, :], wqkv[k, :, pl.ds(0, mine)], NT) for k in range(deep)]
@@ -1489,48 +1518,18 @@
         return carry
 
     lax.fori_loop(0, CHUNKS, one_outward, 0)
-
-    kvg_copy.wait_recv()
-
-    def of_side(ref, side):
-        low, high = ref[pl.ds(0, rows), :], ref[pl.ds(rows, rows), :]
-        return jnp.where(side == 0, low, high).astype(F32)
-
-    kvx_out[...] = (of_side(kv_own, 1 - x) + of_side(kv_in, 1 - x)).astype(BF16)
-    kvx_copy = remote(kvx_out, kvx_in, kvg_sem, 1, me.x_peer())
-    kvx_copy.start()
-
-    for copy in late:
-        copy.wait()
-    for tree in range(trees):
-
-        def norm_again(number, carry):
-            at = rows_at(number, step)
-            norm_rows(
-                spare.at[pl.ds(tree * rows, rows)], mats.at[1, pl.ds(tree * rows, rows)], at
-            )
-            return carry
-
-        lax.fori_loop(0, CHUNKS, norm_again, 0)
-
-    def hid_one(tree, lanes):
-        return mats[1, rows_at(tree, rows), lanes]
-
-    def query_weight_grad(k, carry):
-        value = sum(mm(hid_one(tree, shard_lanes(k)), qlow[tree], TN) for tree in range(trees))
-        keep, away = halves(value)
-        keep_own(own_q, stage_q, k, pl.ds(0, mine), keep)
-        ups[rows_at(k, half), xs_lanes[0]] = away.astype(BF16)
-        return carry
-
-    lax.fori_loop(0, deep, query_weight_grad, 0)
-    xs_copy(0).start()
+    for k in range(deep):
+        alx_copy(c, k, 0).wait_recv()
+        alx_copy(c, k, 1).start()
+    let_go(1)
     kvx_copy.wait_recv()
     own_kv = of_side(kv_own, x) + of_side(kv_in, x) + kvx_in[...].astype(F32)
     kvlow[:, pl.ds(0, HEAD_SIZE)] = turn(
         own_kv[:, :HEAD_SIZE], tables[0, c], -tables[1, c]
     ).astype(BF16)
     kvlow[:, pl.ds(HEAD_SIZE, HEAD_SIZE)] = own_kv[:, HEAD_SIZE:].astype(BF16)
+    kvl_copy = remote(kvlow, kvlow_x, kvg_sem, 2, me.x_peer())
+    kvl_copy.start()
 
     two.y_sent()
 
@@ -1550,60 +1549,110 @@
 
     lax.fori_loop(0, CHUNKS, one_inward, 0)
 
+    mo.across()
+    mo.inward()
+    for part in range(groups):
+        take.drain(part)
+    spare = mats.at[0]
+    late = [
+        load(tokens_in.at[0], spare.at[pl.ds(0, rows)], 0),
+        load(tokens_in.at[1], spare.at[pl.ds(rows, rows)], 1),
+    ]
+    for copy in late:
+        copy.start()
+
+    def chosen_half(value):
+        return jnp.where(x == 0, value[:half], value[2 * HEAD_SIZE - half :])
+
+    def keep_own(buffer_own, buffer_stage, k, lanes, value):
+        @pl.when(k == z)
+        def _():
+            buffer_own[0, 0, :, lanes] = value.astype(BF16)
+
+        @pl.when(k != z)
+        def _():
+            buffer_stage[0, fold.place(k), 0, :, lanes] = value.astype(BF16)
+
+    def heads_of(array, tree):
+        return jnp.concatenate([array[tree, head] for head in range(heads)], 1)
+
+    fold_o = Fold(me, 1, (own_o, stage_o, land_o), (fold_send_o, fold_recv_o, None), 64, False)
+    fold_q = Fold(me, 1, (own_q, stage_q, land_q), (fold_send_q, fold_recv_q, None), 64, False)
+    for k in range(deep):
+        alx_copy(1 - c, k, 1).wait_recv()
+    remote(context, ctx_x, ctx_sem, 0, me.x_peer()).wait_recv()
+
+    def output_grad(k, carry):
+        value = jnp.zeros((2 * HEAD_SIZE, mine), F32)
+        for tree in range(trees):
+            value = value + mm(alow[tree, :, half_lanes(k, x)], heads_of(context, tree), TN)
+            value = value + mm(alx[tree, k], heads_of(ctx_x, tree), TN)
+        keep_own(own_o, stage_o, k, pl.ds(0, mine), chosen_half(value))
+        return carry
+
+    lax.fori_loop(0, deep, output_grad, 0)
+    fold_o.begin(0, 0)
+    advance(3, [0])
+
+    for copy in late:
+        copy.wait()
+    for tree in range(trees):
+
+        def norm_again(number, carry):
+            at = rows_at(number, step)
+            norm_rows(
+                spare.at[pl.ds(tree * rows, rows)], mats.at[1, pl.ds(tree * rows, rows)], at
+            )
+            return carry
+
+        lax.fori_loop(0, CHUNKS, norm_again, 0)
+
+    def hid_one(tree, k):
+        return mats[1, rows_at(tree, rows), half_lanes(k, x)]
+
+    for k in range(deep):
+        hidx_copy(1 - c, k, 1).wait_recv()
+    qx_copy.wait_recv()
+
+    def query_grad(k, carry):
+        value = jnp.zeros((2 * HEAD_SIZE, mine), F32)
+        for tree in range(trees):
+            value = value + mm(hid_one(tree, k), qlow[tree], TN)
+            value = value + mm(hidx[tree, k], qlow_x[tree], TN)
+        keep_own(own_q, stage_q, k, pl.ds(0, mine), chosen_half(value))
+        return carry
+
+    lax.fori_loop(0, deep, query_grad, 0)
+
+    kvl_copy.wait_recv()
+
     def kv_weight_grad(k, carry):
-        value = mm(hid_one(c, shard_lanes(k)), kvlow[...], TN)
+        value = mm(hid_one(c, k), kvlow[...], TN) + mm(hidx[c, k], kvlow_x[...], TN)
+        value = chosen_half(value)
         low, high = value[:, :HEAD_SIZE], value[:, HEAD_SIZE:]
         dkv_out[0, k] = jnp.where(c == 0, high, low).astype(BF16)
         dkv_out[1, k] = jnp.where(c == 0, low, high).astype(BF16)
         return carry
 
     lax.fori_loop(0, deep, kv_weight_grad, 0)
-    dkv_copy = remote(dkv_out.at[0], dkv_in, kvg_sem, 2, me.core_peer())
+    dkv_copy = remote(dkv_out.at[0], dkv_in, kvg_sem, 3, me.core_peer())
     dkv_copy.start()
     dkv_copy.wait_recv()
 
     def kv_weight_sum(k, carry):
-        keep, away = halves(dkv_out[1, k].astype(F32) + dkv_in[k].astype(F32))
-        keep_own(own_q, stage_q, k, pl.ds(mine, HEAD_SIZE), keep)
-        ups[rows_at(k, half), xs_lanes[2]] = away.astype(BF16)
+        value = dkv_out[1, k].astype(F32) + dkv_in[k].astype(F32)
+        keep_own(own_q, stage_q, k, pl.ds(mine, HEAD_SIZE), value)
         return carry
 
     lax.fori_loop(0, deep, kv_weight_sum, 0)
-    xs_copy(2).start()
-
-    mo.pass_on(0, CHUNKS)
+    fold_q.begin(0, 0)
+
+    advance(3, [1])
+    let_go(2)
     finish_group(0, True)
     finish_group(1, True)
-    let_go(2)
+    finish_group(1, False)
     finish_group(2, False)
-    advance(3)
-
-    fold_o = Fold(me, 1, (own_o, stage_o, land_o), (fold_send_o, fold_recv_o, None), 64, False)
-    fold_q = Fold(me, 1, (own_q, stage_q, land_q), (fold_send_q, fold_recv_q, None), 64, False)
-
-    def side_sum(buffer_own, buffer_stage, lanes_in, lanes):
-        def one(k, carry):
-            more = xs_in[rows_at(k, half), lanes_in].astype(F32)
-
-            @pl.when(k == z)
-            def _():
-                buffer_own[0, 0, :, lanes] = (
-                    buffer_own[0, 0, :, lanes].astype(F32) + more
-                ).astype(BF16)
-
-            @pl.when(k != z)
-            def _():
-                buffer_stage[0, fold.place(k), 0, :, lanes] = (
-                    buffer_stage[0, fold.place(k), 0, :, lanes].astype(F32) + more
-                ).astype(BF16)
-
-            return carry
-
-        lax.fori_loop(0, deep, one, 0)
-
-    xs_copy(1).wait_recv()
-    side_sum(own_o, stage_o, xs_lanes[1], pl.ds(0, mine))
-    fold_o.begin(0, 0)
 
     def out_copies(buffer, target, first, peer_sems, number):
         at = rows_at(number, step)
@@ -1620,10 +1669,10 @@
         factor = lax.rsqrt(jnp.mean(value * value, -1, keepdims=True) + EPS)
         scaled = upstream * gain_one
         inner = jnp.mean(scaled * value, -1, keepdims=True)
-        acc[at, :] = agrad[at, :] + (
+        agrad[at, :] = agrad[at, :] + (
             factor * scaled - value * (factor * factor * factor * inner)
         )
-        for copy in out_copies(acc, d_tokens, CHUNKS, token_sem, number):
+        for copy in out_copies(agrad, d_tokens, CHUNKS, token_sem, number):
             copy.start()
         return gain_grad + jnp.sum(upstream * value * factor, 0, keepdims=True)
 
@@ -1639,12 +1688,9 @@
     for k in range(1, 4):
         spread(k).start()
     small_in[spot] = small_own[...]
+    advance(3, [2])
+    mo.pass_on(0, CHUNKS)
     fold_o.advance(0, 0)
-    xs_copy(0).wait_recv()
-    side_sum(own_q, stage_q, xs_lanes[0], pl.ds(0, mine))
-    xs_copy(2).wait_recv()
-    side_sum(own_q, stage_q, xs_lanes[2], pl.ds(mine, HEAD_SIZE))
-    fold_q.begin(0, 0)
     let_go(3)
     finish_group(2, True)
 
@@ -1725,10 +1771,10 @@
     for number in range(CHUNKS):
         at = pl.ds(number * step, step)
         remote(x_out.at[at], mixed.at[1 - c, at], mixed_sem, number, me.core_peer()).wait_recv()
-        remote(acc.at[at], d_tokens.at[1 - c, at], token_sem, number, me.core_peer()).wait_recv()
+        remote(agrad.at[at], d_tokens.at[1 - c, at], token_sem, number, me.core_peer()).wait_recv()
         for buffer, target, first, peer_sems in (
             (x_out, mixed, 0, mixed_sem),
-            (acc, d_tokens, CHUNKS, token_sem),
+            (agrad, d_tokens, CHUNKS, token_sem),
         ):
             here, there = out_copies(buffer, target, first, peer_sems, number)
             here.wait()
@@ -1747,9 +1793,11 @@
         small_out(k).wait_send()
     for k in range(1, 4):
         last_copy(k).wait_send()
-    for part in range(3):
-        xs_copy(part).wait_send()
-    for copy in (kvg_copy, kvx_copy, dkv_copy):
+    for k in range(deep):
+        hidx_copy(c, k, 1).wait_send()
+        alx_copy(c, k, 0).wait_send()
+        alx_copy(c, k, 1).wait_send()
+    for copy in (kvg_copy, kvx_copy, kvl_copy, dkv_copy, qx_copy, ctx_copy, cot_x, cot_on):
         copy.wait_send()
     for which in range(2):
         kv_copy(c, which, own_place, 0).wait_send()
@@ -1812,7 +1860,6 @@
     def out(*shape, dtype=F32):
         return jax.ShapeDtypeStruct(shape, dtype)
 
-    lanes = 2 * mine + HEAD_SIZE
     last = deep - 1
     return pl.pallas_call(
         layer_kernel,
@@ -1868,9 +1915,13 @@
             plain(rows, 2 * HEAD_SIZE),
             plain(rows, 2 * HEAD_SIZE),
             plain(rows, 2 * HEAD_SIZE),
-            plain(2, deep, shard, HEAD_SIZE),
-            plain(deep, shard, HEAD_SIZE),
-            plain(deep * half, lanes),
+            plain(rows, 2 * HEAD_SIZE),
+            plain(trees, rows, mine),
+            plain(trees, deep, rows, 2 * HEAD_SIZE),
+            plain(trees, deep, rows, 2 * HEAD_SIZE),
+            plain(trees, heads, rows, HEAD_SIZE),
+            plain(2, deep, half, HEAD_SIZE),
+            plain(deep, half, HEAD_SIZE),
             plain(held, KINDS, units, shard),
             plain(sets, last, KINDS, units, shard),
             plain(sets, 5, KINDS, units, shard),
@@ -1914,8 +1965,11 @@
             sems(CHUNKS),
             sems(CHUNKS),
             sems(CHUNKS),
-            sems(3),
-            sems(3),
+            sems(4),
+            sems(1),
+            sems(2 * deep),
+            sems(2 * deep),
+            sems(1),
             pltpu.SemaphoreType.DMA((sets * 3 * KINDS,)),
             pltpu.SemaphoreType.DMA((sets * 5 * KINDS,)),
             pltpu.SemaphoreType.REGULAR((sets * 3 * KINDS,)),

time: 276 us -> 260 us (0.942)
  Pallas kernels: 270 us -> 255 us
    pallas_call x1, Pallas kernels: 262 us -> 248 us  [layer_call(): pl.pallas_call(layer_kernel, out_shape=(out(trees, rows, width, dtype=BF1...]
where the time goes in v5:
time: 260 us
  Pallas kernels  255 us (98%)
  local copies, waits for them, and re-layouts  2.62 us (1%)
    pallas_call x1, Pallas kernels, layer_call(): pl.pallas_call(layer_kernel, out_shape=(out(trees, rows, width, dtype=BF1...  248 us
    pallas_call x1, Pallas kernels, place_call(): pl.pallas_call(place_kernel, out_shape=tuple((jax.ShapeDtypeStruct(a.shap...  7.06 us

profile of v5, /device:TPU:0, one launch (start us, length us, event | category | flops | bytes accessed | tf_op | source)
XLA Modules:
  0.0 260.1 jit_solution(4606267765076901394)
XLA Ops:
  0.7 0.1 pad.2.clone
  0.7 0.7 broadcast_in_dim.9
  1.4 0.7 broadcast_in_dim.10
  2.1 1.4 pad_maximum_fusion.small
  3.5 248.4 %layer.1 = (bf16[2,256,1536]{2,1,0:T(8,128)(2,1)}, f32[2,256,1536]{2,1,0:T(8,128)}, f32[768,384]{1,0:T(8,128)}, f32[768,384]{1,0:T(8,128)}, f32[768,384]{1,0:T(8...) custom-call(s32[2,9]{1,0:T(2,128)} %starts.1, ...), custom_call_target="tpu_custom_call" | custom-call | tf_op jit(solution)/shard_map/layer/pallas_call | solution.py:1864
  251.8 0.0 copy-start
  251.8 7.1 %place.1 = (bf16[2,256,1536]{2,1,0:T(8,128)(2,1)}, f32[2,256,1536]{2,1,0:T(8,128)}, f32[768,384]{1,0:T(8,128)}, f32[768,384]{1,0:T(8,128)}, f32[768,384]{1,0:T(8...) custom-call(bf16[2,256,1536]{2,1,0:T(8,128)(2,1)} %get-tuple-element.31.refs_0_, ...), custom_call_target="tpu_custom_call" | custom-call | tf_op jit(solution)/shard_map/place/pallas_call | solution.py:808
  258.9 0.0 copy-done
  258.9 0.6 fusion
  259.5 0.6 slice_bitcast_fusion
  (1 shorter events, 0.0 us)
Async XLA Ops:
  251.8 7.1 %copy-start = (f32[16,192]{1,0:T(8,128)S(1)}, f32[16,192]{1,0:T(8,128)}, u32[]{:S(2)}) copy-start(f32[16,192]{1,0:T(8,128)} %get-tuple-element.42) | copy-start | bytes 36868

commit v6 on v5

--- a/solution.py
+++ b/solution.py
@@ -601,7 +601,7 @@
 
         lax.fori_loop(0, self.tiles, one, 0)
 
-    def across(self):
+    def across(self, first=0, last=None):
         me = self.me
 
         def one(number, carry):
@@ -613,7 +613,7 @@
                 self.x_copy(number * self.per_tile + k).start()
             return carry
 
-        lax.fori_loop(0, self.tiles, one, 0)
+        lax.fori_loop(first, self.tiles if last is None else last, one, 0)
 
     def inward(self):
         me = self.me
@@ -821,7 +821,9 @@
     parents,
     frequency,
     routes,
-    small,
+    gain_one_in,
+    gain_two_in,
+    router_in,
     tokens_in,
     cotangent_in,
     w_query,
@@ -908,6 +910,7 @@
     up2_sem,
     dn2_sem,
     side2_sem,
+    trade_sem,
     up3_sem,
     dn3_sem,
     kv_sem,
@@ -972,11 +975,9 @@
         return pltpu.make_async_copy(source, target, load_sem.at[at])
 
     head_lanes = rows_at(y, HEAD_SIZE)
+    first_lanes, second_lanes = pl.ds(mine, HEAD_SIZE), pl.ds(mine + HEAD_SIZE, HEAD_SIZE)
     loads = [
         load(w_query, wqkv.at[z, :, pl.ds(0, mine)], 0),
-        load(w_key.at[:, head_lanes], wqkv.at[z, :, pl.ds(mine, HEAD_SIZE)], 1),
-        load(w_value.at[:, head_lanes], wqkv.at[z, :, pl.ds(mine + HEAD_SIZE, HEAD_SIZE)], 2),
-        load(small, smalls.at[z], 3),
         load(w_output, wout.at[z], 4),
         load(tokens_in, alow, 5),
         load(cotangent_in.at[0], ups.at[block_rows(0, x)], 6),
@@ -985,6 +986,20 @@
         load(up_in, mats.at[1, :, shard_lanes(z)], 9),
         load(down_in, mats.at[2, :, shard_lanes(z)], 10),
     ]
+
+    for core, source in enumerate((w_key, w_value)):
+
+        @pl.when(c == core)
+        def _():
+            load(source.at[:, head_lanes], wqkv.at[z, :, first_lanes], 1).start()
+
+    row = lax.broadcasted_iota(jnp.int32, (8, shard), 0)
+    gains = jnp.where(
+        row == 0,
+        jnp.broadcast_to(gain_one_in[...].astype(F32), (8, shard)),
+        jnp.where(row == 1, jnp.broadcast_to(gain_two_in[...].astype(F32), (8, shard)), 0.0),
+    )
+    smalls[z] = jnp.concatenate([gains, router_in[...].astype(F32)], 0).astype(BF16)
     for copy in loads:
         copy.start()
     lin = x * 4 + me.t
@@ -996,20 +1011,20 @@
         [me.at_z((z + k) % deep) for k in range(1, deep)]
         + [plane((lin + k) % 8) for k in range(1, 8)]
     )
-    for copy in loads[:4]:
-        copy.wait()
-
-    def halved(buffer):
-        def piece(source, part, by):
-            return buffer.at[source, rows_at(by, half)]
-
-        return piece
+    loads[0].wait()
+    load(w_key.at[:, head_lanes], wqkv.at[z, :, first_lanes], 1).wait()
+
+    def qkv_piece(source, part, by):
+        return wqkv.at[source, rows_at(by, half), pl.ds(0, mine + HEAD_SIZE)]
+
+    def out_piece(source, part, by):
+        return wout.at[source, rows_at(by, half)]
 
     def expert_piece(source, part, by):
         return mats.at[:, pl.ds(part * units, units), shard_lanes(source)]
 
-    take_qkv = Relay(me, deep, halved(wqkv), up1_sem, dn1_sem, side1_sem)
-    take_out = Relay(me, deep, halved(wout), up2_sem, dn2_sem, side2_sem)
+    take_qkv = Relay(me, deep, qkv_piece, up1_sem, dn1_sem, side1_sem)
+    take_out = Relay(me, deep, out_piece, up2_sem, dn2_sem, side2_sem)
     take = Relay(me, deep, expert_piece, up3_sem, dn3_sem)
 
     def small_out(k):
@@ -1020,17 +1035,23 @@
     for k in range(1, deep):
         small_out(k).start()
 
-    for tree in range(trees):
+    def make_tables(tree):
         seen, cosine, sine = tree_tables(
             starts, parents, tree, x * rows, rows, length, frequency[:1, :]
         )
         agrad[:, pl.ds(tree * length, length)] = seen
         tables[0, tree] = cosine
         tables[1, tree] = sine
+
+    make_tables(0)
     take_qkv.pass_on(0, 0)
-    for copy in loads[4:]:
+    for copy in loads[1:]:
         copy.wait()
     take_out.begin(0)
+    for tree in range(1, trees):
+        make_tables(tree)
+    take_qkv.pass_on(0, 1)
+    take_out.pass_on(0, 0)
     for k in range(1, deep):
         source = (z + deep - k) % deep
         remote(
@@ -1053,12 +1074,15 @@
             return carry
 
         lax.fori_loop(0, CHUNKS, first_norm, 0)
-    take_qkv.pass_on(0, 1)
-    take_out.pass_on(0, 0)
+    take_qkv.pass_on(0, 2)
+    take_out.pass_on(0, 1)
     take.begin(0)
-    take_qkv.pass_on(0, 2)
     take_qkv.finish(0)
-    take_out.pass_on(0, 1)
+    trade = remote(
+        wqkv.at[:, :, first_lanes], wqkv.at[:, :, second_lanes], trade_sem, 0, me.core_peer()
+    )
+    trade.start()
+    trade.wait_recv()
 
     own_place = rows_at(x, rows)
     away_place = rows_at(1 - x, rows)
@@ -1075,9 +1099,10 @@
         for head in range(heads):
             part_q = total[:, head * HEAD_SIZE : (head + 1) * HEAD_SIZE]
             queries[tree, head] = turn(part_q, cosine, sine).astype(BF16)
-        part_k = total[:, mine : mine + HEAD_SIZE]
+        first, second_part = total[:, mine : mine + HEAD_SIZE], total[:, mine + HEAD_SIZE :]
+        part_k = jnp.where(c == 0, first, second_part)
         keys[tree, own_place, :] = turn(part_k, cosine, sine).astype(BF16)
-        values[tree, own_place, :] = total[:, mine + HEAD_SIZE :].astype(BF16)
+        values[tree, own_place, :] = jnp.where(c == 0, second_part, first).astype(BF16)
 
     project_in(c)
     for which in range(2):
@@ -1223,8 +1248,19 @@
     def hidx_copy(tree, k, on):
         return cross(x_out, hidx, tree, k, on, hidx_sem)
 
-    def alx_copy(tree, k, on):
-        return cross(alow.at[tree], alx, tree, k, on, alx_sem)
+    def alx_out(number, k):
+        at = rows_at(number, step)
+        return remote(
+            alow.at[c, at, half_lanes(k, 1 - x)],
+            alx.at[c, k, at],
+            alx_sem,
+            number * deep + k,
+            me.x_peer(),
+        )
+
+    def alx_on(tree, k):
+        at = alx.at[tree, k]
+        return remote(at, at, alx_sem, CHUNKS * deep + k, me.core_peer())
 
     def again(number, carry):
         norm_rows(alow.at[c], x_out, rows_at(number, step))
@@ -1453,12 +1489,12 @@
         agrad[at, :] = total
         alow[c, at, :] = total.astype(BF16)
         low_copy(number).start()
+        for k in range(deep):
+            alx_out(number, k).start()
         return gain_grad + jnp.sum(upstream * value * factor, 0, keepdims=True)
 
     gain_two_grad = lax.fori_loop(0, CHUNKS, second_norm, jnp.zeros((1, width), F32))
     small_own[pl.ds(1, 1), :] = gain_two_grad
-    for k in range(deep):
-        alx_copy(c, k, 0).start()
 
     def attend_back(tree):
         back = jnp.zeros((rows, mine), F32)
@@ -1487,6 +1523,11 @@
     kv_out[...] = attend_back(1 - c).astype(BF16)
     kvg_copy = remote(kv_out, kv_in, kvg_sem, 0, me.core_peer())
     kvg_copy.start()
+
+    def qx_copy(tree, number):
+        return remote(qlow.at[tree], qlow_x.at[tree], qx_sem, number, me.x_peer())
+
+    qx_copy(1 - c, 0).start()
     kv_own[...] = attend_back(c)
 
     def of_side(ref, side):
@@ -1497,8 +1538,7 @@
     kvx_out[...] = (of_side(kv_own, 1 - x) + of_side(kv_in, 1 - x)).astype(BF16)
     kvx_copy = remote(kvx_out, kvx_in, kvg_sem, 1, me.x_peer())
     kvx_copy.start()
-    qx_copy = remote(qlow, qlow_x, qx_sem, 0, me.x_peer())
-    qx_copy.start()
+    qx_copy(c, 1).start()
     advance(2, [2])
 
     def one_tile(tree, at):
@@ -1519,15 +1559,16 @@
 
     lax.fori_loop(0, CHUNKS, one_outward, 0)
     for k in range(deep):
-        alx_copy(c, k, 0).wait_recv()
-        alx_copy(c, k, 1).start()
+        for number in range(CHUNKS):
+            alx_out(number, k).wait_recv()
+        alx_on(c, k).start()
     let_go(1)
     kvx_copy.wait_recv()
     own_kv = of_side(kv_own, x) + of_side(kv_in, x) + kvx_in[...].astype(F32)
-    kvlow[:, pl.ds(0, HEAD_SIZE)] = turn(
-        own_kv[:, :HEAD_SIZE], tables[0, c], -tables[1, c]
-    ).astype(BF16)
-    kvlow[:, pl.ds(HEAD_SIZE, HEAD_SIZE)] = own_kv[:, HEAD_SIZE:].astype(BF16)
+    key_low = turn(own_kv[:, :HEAD_SIZE], tables[0, c], -tables[1, c])
+    value_low = own_kv[:, HEAD_SIZE:]
+    kvlow[:, pl.ds(0, HEAD_SIZE)] = jnp.where(c == 0, key_low, value_low).astype(BF16)
+    kvlow[:, pl.ds(HEAD_SIZE, HEAD_SIZE)] = jnp.where(c == 0, value_low, key_low).astype(BF16)
     kvl_copy = remote(kvlow, kvlow_x, kvg_sem, 2, me.x_peer())
     kvl_copy.start()
 
@@ -1579,7 +1620,7 @@
     fold_o = Fold(me, 1, (own_o, stage_o, land_o), (fold_send_o, fold_recv_o, None), 64, False)
     fold_q = Fold(me, 1, (own_q, stage_q, land_q), (fold_send_q, fold_recv_q, None), 64, False)
     for k in range(deep):
-        alx_copy(1 - c, k, 1).wait_recv()
+        alx_on(1 - c, k).wait_recv()
     remote(context, ctx_x, ctx_sem, 0, me.x_peer()).wait_recv()
 
     def output_grad(k, carry):
@@ -1612,7 +1653,8 @@
 
     for k in range(deep):
         hidx_copy(1 - c, k, 1).wait_recv()
-    qx_copy.wait_recv()
+    qx_copy(1 - c, 0).wait_recv()
+    qx_copy(c, 1).wait_recv()
 
     def query_grad(k, carry):
         value = jnp.zeros((2 * HEAD_SIZE, mine), F32)
@@ -1630,8 +1672,8 @@
         value = mm(hid_one(c, k), kvlow[...], TN) + mm(hidx[c, k], kvlow_x[...], TN)
         value = chosen_half(value)
         low, high = value[:, :HEAD_SIZE], value[:, HEAD_SIZE:]
-        dkv_out[0, k] = jnp.where(c == 0, high, low).astype(BF16)
-        dkv_out[1, k] = jnp.where(c == 0, low, high).astype(BF16)
+        dkv_out[0, k] = high.astype(BF16)
+        dkv_out[1, k] = low.astype(BF16)
         return carry
 
     lax.fori_loop(0, deep, kv_weight_grad, 0)
@@ -1795,9 +1837,10 @@
         last_copy(k).wait_send()
     for k in range(deep):
         hidx_copy(c, k, 1).wait_send()
-        alx_copy(c, k, 0).wait_send()
-        alx_copy(c, k, 1).wait_send()
-    for copy in (kvg_copy, kvx_copy, kvl_copy, dkv_copy, qx_copy, ctx_copy, cot_x, cot_on):
+        for number in range(CHUNKS):
+            alx_out(number, k).wait_send()
+        alx_on(c, k).wait_send()
+    for copy in (trade, kvg_copy, kvx_copy, kvl_copy, dkv_copy, qx_copy(1 - c, 0), qx_copy(c, 1), ctx_copy, cot_x, cot_on):
         copy.wait_send()
     for which in range(2):
         kv_copy(c, which, own_place, 0).wait_send()
@@ -1821,7 +1864,9 @@
     seg_start,
     seg_parent,
     routes,
-    small,
+    gain_one,
+    gain_two,
+    router_t,
     tokens,
     cotangent,
     w_query,
@@ -1839,7 +1884,8 @@
     length = rows * 2
     held, units = w_down.shape[0], w_down.shape[1]
     total_units = held * units
-    experts = small.shape[0] - 8
+    experts = router_t.shape[0]
+    small_rows = 8 + experts
     blocks = 2 * trees
     half = shard // 2
     count = blocks * rows
@@ -1873,9 +1919,9 @@
             out(half, mine),
             out(half // 4, KEY_VALUE_HEADS * HEAD_SIZE),
             out(half // 4, KEY_VALUE_HEADS * HEAD_SIZE),
-            out(small.shape[0], half),
+            out(small_rows, half),
         ),
-        in_specs=[smem, smem, vmem, vmem] + [hbm] * 10,
+        in_specs=[smem, smem] + [vmem] * 5 + [hbm] * 9,
         out_specs=[hbm] * 5 + [vmem] * 5,
         scratch_shapes=[
             plain(KINDS, total_units, width),
@@ -1884,7 +1930,7 @@
             plain(count, width),
             plain(deep, shard, mine + 2 * HEAD_SIZE),
             plain(deep, mine, shard),
-            plain(deep, small.shape[0], shard),
+            plain(deep, small_rows, shard),
             plain(trees, heads, rows, HEAD_SIZE),
             plain(trees, length, HEAD_SIZE),
             plain(trees, length, HEAD_SIZE),
@@ -1932,9 +1978,9 @@
             plain(1, 1, half, mine + HEAD_SIZE),
             plain(1, last, 1, half, mine + HEAD_SIZE),
             plain(1, deep, 1, half, mine + HEAD_SIZE),
-            wide(small.shape[0], width),
-            wide(4, small.shape[0], width),
-            wide(deep, small.shape[0], shard),
+            wide(small_rows, width),
+            wide(4, small_rows, width),
+            wide(deep, small_rows, shard),
             wide(half, HEAD_SIZE),
             wide(4, half // 4, HEAD_SIZE),
             pltpu.SemaphoreType.DMA((11,)),
@@ -1945,6 +1991,7 @@
             sems(deep),
             sems(deep),
             sems(2 * deep),
+            sems(1),
             sems(held * deep),
             sems(held * deep),
             sems(2 * trees),
@@ -1966,9 +2013,9 @@
             sems(CHUNKS),
             sems(CHUNKS),
             sems(4),
-            sems(1),
+            sems(2),
             sems(2 * deep),
-            sems(2 * deep),
+            sems((CHUNKS + 1) * deep),
             sems(1),
             pltpu.SemaphoreType.DMA((sets * 3 * KINDS,)),
             pltpu.SemaphoreType.DMA((sets * 5 * KINDS,)),
@@ -1994,7 +2041,9 @@
         seg_parent,
         jnp.asarray(frequency),
         routes,
-        small,
+        gain_one,
+        gain_two,
+        router_t,
         tokens,
         cotangent,
         w_query,
@@ -2027,14 +2076,13 @@
     width = tokens.shape[2]
     deep = lax.axis_size("dp")
     held, quarter = w_gate.shape[0], w_gate.shape[2]
-    small = jnp.concatenate(
-        [attn_gain[None], moe_gain[None], jnp.zeros((6, attn_gain.shape[0]), BF16), w_router.T], 0
-    )
     made = layer_call(
         seg_start,
         seg_parent,
         jnp.swapaxes(routes, 1, 2),
-        small,
+        attn_gain,
+        moe_gain,
+        w_router.T,
         tokens,
         cotangent,
         w_query,

time: 260 us -> 250 us (0.962)
  Pallas kernels: 255 us -> 248 us
    pallas_call x1, Pallas kernels: 248 us -> 241 us  [layer_call(): pl.pallas_call(layer_kernel, out_shape=(out(trees, rows, width, dtype=BF1...]
where the time goes in v6:
time: 250 us
  Pallas kernels  248 us (99%)
    pallas_call x1, Pallas kernels, layer_call(): pl.pallas_call(layer_kernel, out_shape=(out(trees, rows, width, dtype=BF1...  241 us
    pallas_call x1, Pallas kernels, place_call(): pl.pallas_call(place_kernel, out_shape=tuple((jax.ShapeDtypeStruct(a.shap...  7.06 us

profile of v6, /device:TPU:0, one launch (start us, length us, event | category | flops | bytes accessed | tf_op | source)
XLA Modules:
  0.0 250.3 jit_solution(5086713304905767700)
XLA Ops:
  0.7 241.4 %layer.1 = (bf16[2,256,1536]{2,1,0:T(8,128)(2,1)}, f32[2,256,1536]{2,1,0:T(8,128)}, f32[768,384]{1,0:T(8,128)}, f32[768,384]{1,0:T(8,128)}, f32[768,384]{1,0:T(8...) custom-call(s32[2,9]{1,0:T(2,128)} %starts.1, ...), custom_call_target="tpu_custom_call" | custom-call | tf_op jit(solution)/shard_map/layer/pallas_call | solution.py:1910
  242.0 0.0 copy-start
  242.0 7.1 %place.1 = (bf16[2,256,1536]{2,1,0:T(8,128)(2,1)}, f32[2,256,1536]{2,1,0:T(8,128)}, f32[768,384]{1,0:T(8,128)}, f32[768,384]{1,0:T(8,128)}, f32[768,384]{1,0:T(8...) custom-call(bf16[2,256,1536]{2,1,0:T(8,128)(2,1)} %get-tuple-element.31.refs_0_, ...), custom_call_target="tpu_custom_call" | custom-call | tf_op jit(solution)/shard_map/place/pallas_call | solution.py:808
  249.1 0.0 copy-done
  249.1 0.6 fusion
  249.7 0.6 slice_bitcast_fusion
Async XLA Ops:
  242.0 7.1 %copy-start = (f32[16,192]{1,0:T(8,128)S(1)}, f32[16,192]{1,0:T(8,128)}, u32[]{:S(2)}) copy-start(f32[16,192]{1,0:T(8,128)} %get-tuple-element.42) | copy-start | bytes 36868

commit v7 on v6

--- a/solution.py
+++ b/solution.py
@@ -1057,9 +1057,9 @@
         remote(
             smalls.at[source], smalls.at[source], small_sem, k - 1, me.at_z(source)
         ).wait_recv()
-    gain_one = jnp.concatenate([smalls[k, :1, :] for k in range(deep)], 1).astype(F32)
-    gain_two = jnp.concatenate([smalls[k, 1:2, :] for k in range(deep)], 1).astype(F32)
-    router = jnp.concatenate([smalls[k, 8:, :] for k in range(deep)], 1)
+    every_small = jnp.concatenate([smalls[k].astype(F32) for k in range(deep)], 1)
+    gain_one, gain_two = every_small[:1], every_small[1:2]
+    router = every_small[8:].astype(BF16)
 
     def norm_rows(source, target, at):
         value = source[at, :].astype(F32)
@@ -1419,10 +1419,10 @@
     take.finish(3)
     expert_block(last, (1 - c) * 2 + 1 - x)
     two.outward(0)
+    expert_block(last, c * 2 + 1 - x)
+    two.across()
     expert_block(last, (1 - c) * 2 + x)
     two.outward(1)
-    expert_block(last, c * 2 + 1 - x)
-    two.across()
     expert_block(last, own_block)
 
     for block in range(2 * trees):

time: 250 us -> 250 us (level)
  no operation moved by 1% of the time
where the time goes in v7:
time: 250 us
  Pallas kernels  248 us (99%)
    pallas_call x1, Pallas kernels, layer_call(): pl.pallas_call(layer_kernel, out_shape=(out(trees, rows, width, dtype=BF1...  241 us
    pallas_call x1, Pallas kernels, place_call(): pl.pallas_call(place_kernel, out_shape=tuple((jax.ShapeDtypeStruct(a.shap...  7.06 us

profile of v7, /device:TPU:0, one launch (start us, length us, event | category | flops | bytes accessed | tf_op | source)
XLA Modules:
  0.0 250.3 jit_solution(2058711636759079716)
XLA Ops:
  0.7 241.4 %layer.1 = (bf16[2,256,1536]{2,1,0:T(8,128)(2,1)}, f32[2,256,1536]{2,1,0:T(8,128)}, f32[768,384]{1,0:T(8,128)}, f32[768,384]{1,0:T(8,128)}, f32[768,384]{1,0:T(8...) custom-call(s32[2,9]{1,0:T(2,128)} %starts.1, ...), custom_call_target="tpu_custom_call" | custom-call | tf_op jit(solution)/shard_map/layer/pallas_call | solution.py:1910
  242.0 0.0 copy-start
  242.0 7.1 %place.1 = (bf16[2,256,1536]{2,1,0:T(8,128)(2,1)}, f32[2,256,1536]{2,1,0:T(8,128)}, f32[768,384]{1,0:T(8,128)}, f32[768,384]{1,0:T(8,128)}, f32[768,384]{1,0:T(8...) custom-call(bf16[2,256,1536]{2,1,0:T(8,128)(2,1)} %get-tuple-element.31.refs_0_, ...), custom_call_target="tpu_custom_call" | custom-call | tf_op jit(solution)/shard_map/place/pallas_call | solution.py:808
  249.1 0.0 copy-done
  249.1 0.6 fusion
  249.7 0.6 slice_bitcast_fusion
Async XLA Ops:
  242.0 7.1 %copy-start = (f32[16,192]{1,0:T(8,128)S(1)}, f32[16,192]{1,0:T(8,128)}, u32[]{:S(2)}) copy-start(f32[16,192]{1,0:T(8,128)} %get-tuple-element.42) | copy-start | bytes 36868
